TPU v7x, 32 devices: a whole 2x2x4 slice. The times are simulated.
32 devices in a mesh: clip: 2 (over y), seq: 4 (over z), blk: 4 (over x, core).
Axes of the slice: x: 2, y: 2, z: 4, core: 2. Of those that a mesh axis runs over, the one named last changes fastest.
Arguments:
- queries: bfloat16 [4096, 2048], P(('clip', 'seq', 'blk')), parts along dimension 0, may hold values from -6 to 6
- keys: bfloat16 [4096, 2048], P(('clip', 'seq', 'blk')), parts along dimension 0, may hold values from -6 to 6
- values: bfloat16 [4096, 2048], P(('clip', 'seq', 'blk')), parts along dimension 0, may hold values from -4 to 4
- kept: int32 [16, 16, 16], replicated, may hold values from 0 to 15, as said below
- dense_class: int32 [16], replicated, may hold values 0 or 1
Outputs:
- attended: bfloat16 [4096, 2048], P(('clip', 'seq', 'blk')), parts along dimension 0
There are 2 independent parts, one for each index of `clip`. A program takes and returns all parts, laid end to end along the dimension named above; an argument that names none is the same for every part. Nothing has to cross between parts.
Inputs may be any that keep to these rules, and one draw needn't show every extreme that they name: For each head h, query block b and span c, kept[h, b, c * 4 + s] for s < 4 are 4 different blocks k with k % 4 == c; in the span of b itself the first of them is b.
All inputs are finite; a program needn't handle non-finite values.
Results may differ from a plain program's by a relative error of at most 0.0046.
Values may be sent and summed in bfloat16 or wider, within the bound.
No kernel may reach another device: no remote copies, remote signals or barrier semaphores. Data moves between devices by JAX's collectives and lax.ppermute only.
A program may use at most 128 MiB of HBM per device.

v0:
```python
import math

import jax
import jax.numpy as jnp
from jax import lax
from jax.sharding import PartitionSpec as P

HEADS = 16
HD = 128
BLOCK = 128
KEEP = 4
LIGHT = 2


def combine_spans(partial_out, maxima, totals, along):
    largest = jnp.max(maxima, axis=along, keepdims=True)
    factor = jnp.exp(maxima - largest)
    numerator = jnp.sum(factor[..., None] * partial_out, axis=along)
    denominator = jnp.sum(factor * totals, axis=along)
    return (numerator / denominator[..., None]).astype(jnp.bfloat16)


def attend_blocks(query_rows, key_blocks, blocked_value_rows, local_ids, slot_count):
    query_blocks, part_rows, head_depth = query_rows.shape
    group_size = query_blocks
    while group_size * part_rows > 512 and group_size % 2 == 0:
        group_size = group_size // 2
    logit_scale_factor = 1.0 / math.sqrt(head_depth)
    block_rows = key_blocks.shape[1]

    def one_group(operands):
        queries_group, ids_group = operands
        collected_key_blocks = key_blocks[ids_group].reshape(
            group_size, slot_count * block_rows, head_depth
        )
        gathered_v = blocked_value_rows[ids_group].reshape(
            group_size, slot_count * block_rows, head_depth
        )
        attention_logits = (
            jnp.einsum(
                "gpd,gkd->gpk",
                queries_group,
                collected_key_blocks,
                preferred_element_type=jnp.float32,
            )
            * logit_scale_factor
        )
        maxima = jnp.max(attention_logits, axis=-1)
        weights = jnp.exp(attention_logits - maxima[..., None])
        totals = jnp.sum(weights, axis=-1)
        partial_out = jnp.einsum(
            "gpk,gkd->gpd",
            weights.astype(jnp.bfloat16),
            gathered_v,
            preferred_element_type=jnp.float32,
        )
        return (partial_out, maxima, totals)

    grouped_q = query_rows.reshape(query_blocks // group_size, group_size, part_rows, head_depth)
    grouped_ids = local_ids[:, :slot_count].reshape(
        query_blocks // group_size, group_size, slot_count
    )
    partial_out, maxima, totals = lax.map(one_group, (grouped_q, grouped_ids))
    return (
        partial_out.reshape(query_blocks, part_rows, head_depth),
        maxima.reshape(query_blocks, part_rows),
        totals.reshape(query_blocks, part_rows),
    )


def arrange_heads(stacked):
    swapped = jnp.swapaxes(stacked, 0, 1)
    return swapped.reshape((-1,) + stacked.shape[2:])


def shards(queries, keys, values, kept, dense_class):
    seq_devices = lax.axis_size("seq")
    span_count = lax.axis_size("blk")
    local_rows = queries.shape[0]
    head_count = HEADS
    head_depth = HD
    local_blocks = local_rows // BLOCK
    row_parts = max(1, 2 * seq_devices // head_count)
    part_rows = BLOCK // row_parts
    item_count = head_count * row_parts
    per_device = item_count // seq_devices
    seq_place = lax.axis_index("seq")
    blk_place = lax.axis_index("blk")
    every_item = jnp.arange(item_count, dtype=jnp.int32)
    all_item_heads = every_item // row_parts
    item_heads = lax.dynamic_slice_in_dim(all_item_heads, seq_place * per_device, per_device)
    grid_q = queries.reshape(local_blocks, row_parts, part_rows, head_count, head_depth).transpose(
        1, 3, 0, 2, 4
    )
    grid_q = grid_q.reshape(row_parts, head_count, local_blocks * part_rows, head_depth)
    head_keys = keys.reshape(local_rows, head_count, head_depth).transpose(1, 0, 2)
    head_values = values.reshape(local_rows, head_count, head_depth).transpose(1, 0, 2)
    send_q = arrange_heads(grid_q)
    q_items = lax.all_to_all(send_q, "seq", split_axis=0, concat_axis=1, tiled=True)
    stride = 1
    grid_k = jnp.broadcast_to(head_keys[None], (row_parts, head_count, local_rows, head_depth))
    grid_v = jnp.broadcast_to(head_values[None], (row_parts, head_count, local_rows, head_depth))
    send_k = arrange_heads(grid_k)
    send_v = arrange_heads(grid_v)
    k_held, v_held = (
        lax.all_to_all(send_k, "seq", split_axis=0, concat_axis=1, tiled=True),
        lax.all_to_all(send_v, "seq", split_axis=0, concat_axis=1, tiled=True),
    )
    key_blocks = k_held.reshape(per_device, seq_devices * local_blocks, BLOCK, head_depth)
    blocked_value_rows = v_held.reshape(per_device, seq_devices * local_blocks, BLOCK, head_depth)
    item_slot = jnp.arange(per_device, dtype=jnp.int32) // stride
    item_class = jnp.take(dense_class, item_heads)
    item_kept = jnp.take(kept, item_heads, axis=0)
    source_index = jnp.arange(seq_devices, dtype=jnp.int32)
    block_index = jnp.arange(local_blocks, dtype=jnp.int32)
    span_index = jnp.arange(span_count, dtype=jnp.int32)
    all_ids = (
        (source_index[None, :, None] * span_count + span_index[:, None, None]) * local_blocks
        + block_index[None, None, :]
    ).reshape(-1)
    all_kept = jnp.take(item_kept, all_ids, axis=1)
    span_ids = lax.dynamic_slice_in_dim(all_kept, blk_place * KEEP, KEEP, axis=2)
    q_all = lax.all_gather(q_items, "blk", axis=1, tiled=True)
    query_rows = q_all.reshape(
        per_device, span_count * seq_devices * local_blocks, part_rows, head_depth
    )

    def one_item(operands):
        rows_item, ids_item, class_item, slot_item = operands
        keys_item = lax.dynamic_index_in_dim(key_blocks, slot_item, 0, keepdims=False)
        values_item = lax.dynamic_index_in_dim(blocked_value_rows, slot_item, 0, keepdims=False)
        return lax.cond(
            class_item == 1,
            lambda: attend_blocks(rows_item, keys_item, values_item, ids_item, KEEP),
            lambda: attend_blocks(rows_item, keys_item, values_item, ids_item, LIGHT),
        )

    partial_out, maxima, totals = lax.map(
        one_item,
        (
            query_rows,
            span_ids // (local_blocks * span_count) * local_blocks + span_ids % local_blocks,
            item_class,
            item_slot,
        ),
    )
    own_blocks = seq_devices * local_blocks
    shaped_out = partial_out.reshape(per_device, span_count, own_blocks, part_rows, head_depth)
    shaped_max = maxima.reshape(per_device, span_count, own_blocks, part_rows)
    shaped_total = totals.reshape(per_device, span_count, own_blocks, part_rows)
    got_out, got_max, got_total = (
        lax.all_to_all(shaped_out, "blk", split_axis=1, concat_axis=1, tiled=True),
        lax.all_to_all(shaped_max, "blk", split_axis=1, concat_axis=1, tiled=True),
        lax.all_to_all(shaped_total, "blk", split_axis=1, concat_axis=1, tiled=True),
    )
    attended_items = combine_spans(got_out, got_max, got_total, 1)
    attended_items = attended_items.reshape(
        per_device, seq_devices * local_blocks * part_rows, head_depth
    )
    returned = lax.all_to_all(attended_items, "seq", split_axis=1, concat_axis=0, tiled=True)
    grid_out = returned.reshape(head_count, row_parts, local_blocks, part_rows, head_depth)
    grid_out = jnp.swapaxes(grid_out, 0, 1)
    return grid_out.transpose(2, 0, 3, 1, 4).reshape(local_rows, head_count * head_depth)


def solution(mesh):
    return jax.shard_map(
        shards,
        mesh=mesh,
        in_specs=(
            P(("clip", "seq", "blk"), None),
            P(("clip", "seq", "blk"), None),
            P(("clip", "seq", "blk"), None),
            P(),
            P(),
        ),
        out_specs=P(("clip", "seq", "blk"), None),
        check_vma=False,
    )
```

profile of v0, /device:TPU:0, one launch (start us, length us, event | category | flops | bytes accessed | tf_op | source)
XLA Modules:
  0.0 257.1 jit_solution(15702333167692978711)
XLA Ops:
  6.5 1.4 copy.104
  8.3 20.6 %all_to_all.78 = bf16[16,128,128]{2,1,0:T(8,128)(2,1)S(1)} all-to-all(bf16[16,128,128]{2,1,0:T(8,128)(2,1)S(1)} %copy.105), channel_id=1, replica_groups=mesh['clip'=2,'seq'=4,'blk'=4] {'seq'}, dimensions={0} | all-to-all | bytes 1048576 | tf_op jit(solution)/shard_map/all_to_all | solution.py:99
  30.8 3.5 %all-to-all-start.1 = ((bf16[16,128,128]{1,2,0:T(8,128)(2,1)}), bf16[16,128,128]{1,2,0:T(8,128)(2,1)S(1)}, u32[]{:S(2)}, u32[]{:S(2)}) async-start(bf16[16,128,128]{1,2,0:T(8,128)(2,1)} %bitcast.36), calls=%async_computation.1 | async-start | bytes 1048576 | tf_op jit(solution)/shard_map/all_to_all | solution.py:106
  36.2 11.6 %all-to-all-done.1 = bf16[16,128,128]{1,2,0:T(8,128)(2,1)S(1)} async-done(((bf16[16,128,128]{1,2,0:T(8,128)(2,1)}), bf16[16,128,128]{1,2,0:T(8,128)(2,1)S(1)}, u32[]{:S(2)}, u32[]{:S(2)}) %all-to-all-start.1) | async-done | bytes 524320 | tf_op jit(solution)/shard_map/all_to_all | solution.py:106
  47.9 3.5 %all-to-all-start.2 = ((bf16[16,128,128]{1,2,0:T(8,128)(2,1)}), bf16[16,128,128]{1,2,0:T(8,128)(2,1)S(1)}, u32[]{:S(2)}, u32[]{:S(2)}) async-start(bf16[16,128,128]{1,2,0:T(8,128)(2,1)} %bitcast.41), calls=%async_computation.2 | async-start | bytes 1048576 | tf_op jit(solution)/shard_map/all_to_all | solution.py:107
  53.0 12.2 %all-to-all-done.2 = bf16[16,128,128]{1,2,0:T(8,128)(2,1)S(1)} async-done(((bf16[16,128,128]{1,2,0:T(8,128)(2,1)}), bf16[16,128,128]{1,2,0:T(8,128)(2,1)S(1)}, u32[]{:S(2)}, u32[]{:S(2)}) %all-to-all-start.2) | async-done | bytes 524320 | tf_op jit(solution)/shard_map/all_to_all | solution.py:107
  65.3 92.6 %while.42 = (s32[]{:T(128)}, f32[4,16,128,128]{3,2,1,0:T(8,128)}, f32[4,16,128]{2,1,0:T(8,128)S(1)}, f32[4,16,128]{2,1,0:T(8,128)S(1)}, s32[4]{0:T(128)S(1)}, /*...) while((s32[]{:T(128)}, f32[4,16,128,128]{3,2,1,0:T(8,128)}, ...), condition=%wide.region_11.12_spmd, body=%wide.region_0.11_spmd.sunk | while | flops 135790640 | bytes 10934218 | solution.py:138
  70.5 14.5 %conditional.2 = (f32[4,4,128,128]{3,2,1,0:T(8,128)}, f32[4,4,128]{2,1,0:T(4,128)}, f32[4,4,128]{2,1,0:T(4,128)}) conditional(s32[]{:T(128)} %bitcast.134, (bf16[16,128,128]{2,1,0:T(8,128)(2,1)S(1)}, s32[16,4]{0,1:T(4,128)S(1)}, bf16[4,128,128]{2,1,0:T(8,128)(2,1)S(1)}, bf16[4,128,128]{2,1,0:T(8,128)(2,1)S(1)}) %tuple.110, ...), branch_computations={%region_1.5_spmd, %region_6.10_spmd} | conditional | flops 135790640 | bytes 6706333 | solution.py:132
  70.6 14.4 %while.40 = (s32[]{:T(128)}, f32[4,4,128,128]{3,2,1,0:T(8,128)}, f32[4,4,128]{2,1,0:T(4,128)}, f32[4,4,128]{2,1,0:T(4,128)}, bf16[4,4,128,128]{3,2,1,0:T(8,128)(...) while((s32[]{:T(128)}, f32[4,4,128,128]{3,2,1,0:T(8,128)}, ...), condition=%wide.region_5.4_spmd, body=%wide.region_2.3_spmd.sunk | while | flops 67895320 | bytes 3559893 | solution.py:63
  85.7 2.3 bitcast_dynamic-update-slice_fusion.11
  93.2 15.4 %conditional.2 = (f32[4,4,128,128]{3,2,1,0:T(8,128)}, f32[4,4,128]{2,1,0:T(4,128)}, f32[4,4,128]{2,1,0:T(4,128)}) conditional(s32[]{:T(128)} %bitcast.134, (bf16[16,128,128]{2,1,0:T(8,128)(2,1)S(1)}, s32[16,4]{0,1:T(4,128)S(1)}, bf16[4,128,128]{2,1,0:T(8,128)(2,1)S(1)}, bf16[4,128,128]{2,1,0:T(8,128)(2,1)S(1)}) %tuple.110, ...), branch_computations={%region_1.5_spmd, %region_6.10_spmd} | conditional | flops 135790640 | bytes 6706333 | solution.py:132
  93.3 15.2 %while.41 = (s32[]{:T(128)}, f32[4,4,128,128]{3,2,1,0:T(8,128)}, f32[4,4,128]{2,1,0:T(4,128)}, f32[4,4,128]{2,1,0:T(4,128)}, bf16[4,4,128,128]{3,2,1,0:T(8,128)(...) while((s32[]{:T(128)}, f32[4,4,128,128]{3,2,1,0:T(8,128)}, ...), condition=%wide.region_10.9_spmd, body=%wide.region_7.8_spmd.sunk | while | flops 135790640 | bytes 6705717 | solution.py:63
  99.2 1.1 fusion.43
  106.8 1.1 fusion.43
  109.2 2.3 bitcast_dynamic-update-slice_fusion.11
  116.8 15.4 %conditional.2 = (f32[4,4,128,128]{3,2,1,0:T(8,128)}, f32[4,4,128]{2,1,0:T(4,128)}, f32[4,4,128]{2,1,0:T(4,128)}) conditional(s32[]{:T(128)} %bitcast.134, (bf16[16,128,128]{2,1,0:T(8,128)(2,1)S(1)}, s32[16,4]{0,1:T(4,128)S(1)}, bf16[4,128,128]{2,1,0:T(8,128)(2,1)S(1)}, bf16[4,128,128]{2,1,0:T(8,128)(2,1)S(1)}) %tuple.110, ...), branch_computations={%region_1.5_spmd, %region_6.10_spmd} | conditional | flops 135790640 | bytes 6706333 | solution.py:132
  116.9 15.2 %while.41 = (s32[]{:T(128)}, f32[4,4,128,128]{3,2,1,0:T(8,128)}, f32[4,4,128]{2,1,0:T(4,128)}, f32[4,4,128]{2,1,0:T(4,128)}, bf16[4,4,128,128]{3,2,1,0:T(8,128)(...) while((s32[]{:T(128)}, f32[4,4,128,128]{3,2,1,0:T(8,128)}, ...), condition=%wide.region_10.9_spmd, body=%wide.region_7.8_spmd.sunk | while | flops 135790640 | bytes 6705717 | solution.py:63
  122.8 1.1 fusion.43
  130.5 1.1 fusion.43
  132.9 2.3 bitcast_dynamic-update-slice_fusion.11
  140.4 14.5 %conditional.2 = (f32[4,4,128,128]{3,2,1,0:T(8,128)}, f32[4,4,128]{2,1,0:T(4,128)}, f32[4,4,128]{2,1,0:T(4,128)}) conditional(s32[]{:T(128)} %bitcast.134, (bf16[16,128,128]{2,1,0:T(8,128)(2,1)S(1)}, s32[16,4]{0,1:T(4,128)S(1)}, bf16[4,128,128]{2,1,0:T(8,128)(2,1)S(1)}, bf16[4,128,128]{2,1,0:T(8,128)(2,1)S(1)}) %tuple.110, ...), branch_computations={%region_1.5_spmd, %region_6.10_spmd} | conditional | flops 135790640 | bytes 6706333 | solution.py:132
  140.5 14.3 %while.40 = (s32[]{:T(128)}, f32[4,4,128,128]{3,2,1,0:T(8,128)}, f32[4,4,128]{2,1,0:T(4,128)}, f32[4,4,128]{2,1,0:T(4,128)}, bf16[4,4,128,128]{3,2,1,0:T(8,128)(...) while((s32[]{:T(128)}, f32[4,4,128,128]{3,2,1,0:T(8,128)}, ...), condition=%wide.region_5.4_spmd, body=%wide.region_2.3_spmd.sunk | while | flops 67895320 | bytes 3559893 | solution.py:63
  155.5 2.3 bitcast_dynamic-update-slice_fusion.11
  158.5 3.3 %all-to-all-start.5 = ((f32[4,4,4,128]{3,2,0,1:T(4,128)}), f32[4,4,4,128]{3,2,0,1:T(4,128)S(1)}, u32[]{:S(2)}, u32[]{:S(2)}) async-start(f32[4,4,4,128]{3,2,0,1:T(4,128)} %copy.117), calls=%async_computation.5 | async-start | bytes 65536 | tf_op jit(solution)/shard_map/all_to_all | solution.py:154
  162.4 3.3 %all-to-all-done.5 = f32[4,4,4,128]{3,2,0,1:T(4,128)S(1)} async-done(((f32[4,4,4,128]{3,2,0,1:T(4,128)}), f32[4,4,4,128]{3,2,0,1:T(4,128)S(1)}, u32[]{:S(2)}, u32[]{:S(2)}) %all-to-all-start.5) | async-done | bytes 32800 | tf_op jit(solution)/shard_map/all_to_all | solution.py:154
  165.7 3.3 %all-to-all-start.3 = ((f32[4,4,4,128]{3,2,0,1:T(4,128)}), f32[4,4,4,128]{3,2,0,1:T(4,128)S(1)}, u32[]{:S(2)}, u32[]{:S(2)}) async-start(f32[4,4,4,128]{3,2,0,1:T(4,128)} %copy.115), calls=%async_computation.3 | async-start | bytes 65536 | tf_op jit(solution)/shard_map/all_to_all | solution.py:153
  168.9 4.7 %copy.116 = f32[4,4,4,128,128]{4,3,2,0,1:T(8,128)} copy(f32[4,4,4,128,128]{4,3,2,1,0:T(8,128)} %bitcast.167) | data formatting | bytes 8388608 | tf_op jit(solution)/shard_map/reshape | solution.py:148
  173.6 4.8 %all-to-all-start.4 = ((f32[4,4,4,128,128]{4,3,2,0,1:T(8,128)}), f32[4,4,4,128,128]{4,3,2,0,1:T(8,128)}, u32[]{:S(2)}, u32[]{:S(2)}) async-start(f32[4,4,4,128,128]{4,3,2,0,1:T(8,128)} %copy.116), calls=%async_computation.4 | async-start | bytes 8388608 | tf_op jit(solution)/shard_map/all_to_all | solution.py:152
  178.7 48.0 %all-to-all-done.4 = f32[4,4,4,128,128]{4,3,2,0,1:T(8,128)} async-done(((f32[4,4,4,128,128]{4,3,2,0,1:T(8,128)}), f32[4,4,4,128,128]{4,3,2,0,1:T(8,128)}, u32[]{:S(2)}, u32[]{:S(2)}) %all-to-all-start.4) | async-done | bytes 4194336 | tf_op jit(solution)/shard_map/all_to_all | solution.py:152
  226.7 2.9 %multiply_reduce_fusion = f32[4,4,128,128]{3,2,1,0:T(8,128)S(1)} fusion(f32[4,4,4,128,128]{4,3,2,0,1:T(8,128)} %all-to-all-done.4, f32[4,4,4,128]{3,2,0,1:T(4,128)S(1)} %get-tuple-element.431), kind=kLoop, calls=%fused_computation.43 | loop fusion | flops 1835008 | bytes 5275648 | tf_op jit(solution)/shard_map/reduce_sum | solution.py:18
  229.6 2.3 fusion.16
  231.9 17.0 %all_to_all.79 = bf16[4,512,128]{2,0,1:T(4,128)(2,1)S(1)} all-to-all(bf16[4,512,128]{2,0,1:T(4,128)(2,1)S(1)} %fusion.16), channel_id=1, replica_groups=mesh['clip'=2,'seq'=4,'blk'=4] {'seq'}, dimensions={1} | all-to-all | bytes 1048576 | tf_op jit(solution)/shard_map/all_to_all | solution.py:160
  (261 shorter events, 76.5 us)
Async XLA Ops:
  6.5 29.0 %copy-start = (s32[16,16,16]{2,1,0:T(8,128)S(1)}, s32[16,16,16]{2,1,0:T(8,128)}, u32[]{:S(2)}) copy-start(s32[16,16,16]{2,1,0:T(8,128)} %param.16) | copy-start | bytes 49156
  6.5 23.2 %copy-start.2 = (bf16[128,2048]{1,0:T(8,128)(2,1)S(1)}, bf16[128,2048]{1,0:T(8,128)(2,1)}, u32[]{:S(2)}) copy-start(bf16[128,2048]{1,0:T(8,128)(2,1)} %param.14) | copy-start | bytes 1572868
  6.5 27.9 %copy-start.3 = (bf16[128,2048]{1,0:T(8,128)(2,1)S(1)}, bf16[128,2048]{1,0:T(8,128)(2,1)}, u32[]{:S(2)}) copy-start(bf16[128,2048]{1,0:T(8,128)(2,1)} %param.15) | copy-start | bytes 1572868
  6.5 58.7 %all-gather.2.cloned.1.call-start = ((), (), s32[]{:S(2)}) async-start(), calls=%async_computation.7 | async-start | bytes 2621440 | tf_op jit(solution)/shard_map/all_gather | solution.py:123
  8.0 43.6 %copy-start.1 = (s32[16]{0:T(128)S(1)}, s32[16]{0:T(128)}, u32[]{:S(2)}) copy-start(s32[16]{0:T(128)} %param.17) | copy-start | bytes 196
  30.8 17.1 %all-to-all-start.1 = ((bf16[16,128,128]{1,2,0:T(8,128)(2,1)}), bf16[16,128,128]{1,2,0:T(8,128)(2,1)S(1)}, u32[]{:S(2)}, u32[]{:S(2)}) async-start(bf16[16,128,128]{1,2,0:T(8,128)(2,1)} %bitcast.36), calls=%async_computation.1 | async-start | bytes 1048576 | tf_op jit(solution)/shard_map/all_to_all | solution.py:106
  47.9 17.4 %all-to-all-start.2 = ((bf16[16,128,128]{1,2,0:T(8,128)(2,1)}), bf16[16,128,128]{1,2,0:T(8,128)(2,1)S(1)}, u32[]{:S(2)}, u32[]{:S(2)}) async-start(bf16[16,128,128]{1,2,0:T(8,128)(2,1)} %bitcast.41), calls=%async_computation.2 | async-start | bytes 1048576 | tf_op jit(solution)/shard_map/all_to_all | solution.py:107
  158.5 7.2 %all-to-all-start.5 = ((f32[4,4,4,128]{3,2,0,1:T(4,128)}), f32[4,4,4,128]{3,2,0,1:T(4,128)S(1)}, u32[]{:S(2)}, u32[]{:S(2)}) async-start(f32[4,4,4,128]{3,2,0,1:T(4,128)} %copy.117), calls=%async_computation.5 | async-start | bytes 65536 | tf_op jit(solution)/shard_map/all_to_all | solution.py:154
  165.7 7.9 %all-to-all-start.3 = ((f32[4,4,4,128]{3,2,0,1:T(4,128)}), f32[4,4,4,128]{3,2,0,1:T(4,128)S(1)}, u32[]{:S(2)}, u32[]{:S(2)}) async-start(f32[4,4,4,128]{3,2,0,1:T(4,128)} %copy.115), calls=%async_computation.3 | async-start | bytes 65536 | tf_op jit(solution)/shard_map/all_to_all | solution.py:153
  173.6 53.1 %all-to-all-start.4 = ((f32[4,4,4,128,128]{4,3,2,0,1:T(8,128)}), f32[4,4,4,128,128]{4,3,2,0,1:T(8,128)}, u32[]{:S(2)}, u32[]{:S(2)}) async-start(f32[4,4,4,128,128]{4,3,2,0,1:T(8,128)} %copy.116), calls=%async_computation.4 | async-start | bytes 8388608 | tf_op jit(solution)/shard_map/all_to_all | solution.py:152
Sparse Core Ops, SparseCore 0:
  29.9 21.7 all-gather.1
where the time goes:
time: 259 us; the launch traced here: 257 us
  waiting for transfers between devices  75.2 us (29%)
  local copies, waits for them, and re-layouts  68.6 us (26%)
  blocking collectives  37.6 us (15%)
  matrix products  22.2 us (9%)
  starting transfers between devices  18.3 us (7%)
  between operations  13.6 us (5%)
  loops' own time  11 us (4%)
  other arithmetic  10.6 us (4%)
    all_to_all x1, waiting for transfers between devices, shards(): lax.all_to_all(shaped_out, 'blk', split_axis=1, concat_axis=1, tiled=True)  48 us
    all_to_all x1, blocking collectives, shards(): lax.all_to_all(send_q, 'seq', split_axis=0, concat_axis=1, tiled=True)  20.6 us
    all_to_all x1, blocking collectives, shards(): lax.all_to_all(attended_items, 'seq', split_axis=1, concat_axis=0, tiled=...  17 us
    dot_general x16, matrix products, one_group(): jnp.einsum('gpk,gkd->gpd', weights.astype(jnp.bfloat16), gathered_v, pref...  16.6 us
    all_to_all x1, waiting for transfers between devices, shards(): lax.all_to_all(send_v, 'seq', split_axis=0, concat_axis=1, tiled=True)  12.2 us
    dynamic_update_slice x8, local copies, waits for them, and re-layouts, shards(): lax.map(one_item, (query_rows, span_ids // (local_blocks * span_count) *...  12.2 us
    all_to_all x1, waiting for transfers between devices, shards(): lax.all_to_all(send_k, 'seq', split_axis=0, concat_axis=1, tiled=True)  11.6 us
    another operation x1, loops' own time, shards(): lax.map(one_item, (query_rows, span_ids // (local_blocks * span_count) *...  10.6 us
  transfers between devices with their start and end apart: 6, of which 4 were waited for; matrix products, arithmetic and copies ran while one was open for 4% of the time, Pallas kernels for 0%

commit v1 on v0

--- a/solution.py
+++ b/solution.py
@@ -3,6 +3,8 @@
 import jax
 import jax.numpy as jnp
 from jax import lax
+from jax.experimental import pallas as pl
+from jax.experimental.pallas import tpu as pltpu
 from jax.sharding import PartitionSpec as P
 
 HEADS = 16
@@ -73,7 +75,7 @@
     return swapped.reshape((-1,) + stacked.shape[2:])
 
 
-def shards(queries, keys, values, kept, dense_class):
+def spans_by_device(queries, keys, values, kept, dense_class):
     seq_devices = lax.axis_size("seq")
     span_count = lax.axis_size("blk")
     local_rows = queries.shape[0]
@@ -163,6 +165,101 @@
     return grid_out.transpose(2, 0, 3, 1, 4).reshape(local_rows, head_count * head_depth)
 
 
+def head_kernel(axes, kept_hbm, class_ref, qkv_ref, out_ref, kept_ref, v_all, k_few, v_few, kept_sem):
+    block_count = qkv_ref.shape[0]
+    head_count = class_ref.shape[0]
+    head = 0
+    for axis in axes:
+        head = head * lax.axis_size(axis) + lax.axis_index(axis)
+    kept_copy = pltpu.make_async_copy(kept_hbm.at[head], kept_ref, kept_sem)
+    kept_copy.start()
+    kept_copy.wait()
+    exponent_scale = math.log2(math.e) / math.sqrt(HD)
+
+    def attend(query_rows, key_rows, value_rows):
+        logits = lax.dot_general(
+            query_rows, key_rows, (((1,), (1,)), ((), ())), preferred_element_type=jnp.float32
+        )
+        largest = jnp.max(logits, axis=-1, keepdims=True)
+        weights = jnp.exp2((logits - largest) * exponent_scale).astype(jnp.bfloat16)
+        summed = jnp.dot(weights, value_rows, preferred_element_type=jnp.float32)
+        return (summed[:, :HD] / summed[:, HD:]).astype(jnp.bfloat16)
+
+    @pl.when(class_ref[head] == 1)
+    def _():
+        v_all[:, :, :HD] = qkv_ref[:, 2]
+        v_all[:, :, HD:] = jnp.ones((block_count, BLOCK, HD), jnp.bfloat16)
+        key_rows = qkv_ref[:, 1].reshape(block_count * BLOCK, HD)
+        value_rows = v_all[...].reshape(block_count * BLOCK, 2 * HD)
+        group = 2
+
+        def step(i, carry):
+            query_rows = qkv_ref[pl.ds(i * group, group), 0].reshape(group * BLOCK, HD)
+            out = attend(query_rows, key_rows, value_rows)
+            out_ref[pl.ds(i * group, group)] = out.reshape(group, BLOCK, HD)
+            return carry
+
+        lax.fori_loop(0, block_count // group, step, 0)
+
+    @pl.when(class_ref[head] != 1)
+    def _():
+        v_few[:, HD:] = jnp.ones((v_few.shape[0], HD), jnp.bfloat16)
+
+        def step(b, carry):
+            place = 0
+            for span in range(kept_ref.shape[1] // KEEP):
+                for slot in range(LIGHT):
+                    block = kept_ref[b, span * KEEP + slot]
+                    k_few[place * BLOCK : (place + 1) * BLOCK, :] = qkv_ref[block, 1]
+                    v_few[place * BLOCK : (place + 1) * BLOCK, :HD] = qkv_ref[block, 2]
+                    place += 1
+            out_ref[b] = attend(qkv_ref[b, 0], k_few[...], v_few[...])
+            return carry
+
+        lax.fori_loop(0, block_count, step, 0)
+
+
+def heads_by_device(queries, keys, values, kept, dense_class):
+    axes = ("seq", "blk")
+    local_rows = queries.shape[0]
+    stacked = jnp.stack([queries, keys, values]).reshape(3, local_rows, HEADS, HD)
+    send = stacked.transpose(2, 0, 1, 3)
+    held = lax.all_to_all(send, axes, split_axis=0, concat_axis=0, tiled=True)
+    block_count = kept.shape[1]
+    few = kept.shape[2] // KEEP * LIGHT
+    attended = pl.pallas_call(
+        lambda *refs: head_kernel(axes, *refs),
+        out_shape=jax.ShapeDtypeStruct((block_count, BLOCK, HD), jnp.bfloat16),
+        in_specs=[
+            pl.BlockSpec(memory_space=pl.ANY),
+            pl.BlockSpec(memory_space=pltpu.SMEM),
+            pl.BlockSpec(memory_space=pltpu.VMEM),
+        ],
+        out_specs=pl.BlockSpec(memory_space=pltpu.VMEM),
+        scratch_shapes=[
+            pltpu.SMEM(kept.shape[1:], jnp.int32),
+            pltpu.VMEM((block_count, BLOCK, 2 * HD), jnp.bfloat16),
+            pltpu.VMEM((few * BLOCK, HD), jnp.bfloat16),
+            pltpu.VMEM((few * BLOCK, 2 * HD), jnp.bfloat16),
+            pltpu.SemaphoreType.DMA,
+        ],
+        compiler_params=pltpu.CompilerParams(vmem_limit_bytes=48 * 1024 * 1024),
+        name="attend_head",
+    )(kept, dense_class, held)
+    returned = lax.all_to_all(attended, axes, split_axis=0, concat_axis=0, tiled=True)
+    return returned.transpose(1, 0, 2).reshape(local_rows, HEADS * HD)
+
+
+def shards(queries, keys, values, kept, dense_class):
+    devices = lax.axis_size("seq") * lax.axis_size("blk")
+    one_head_each = devices == HEADS
+    one_block_each = queries.shape[0] == BLOCK
+    every_block_kept = kept.shape[1] == kept.shape[2]
+    if one_head_each and one_block_each and every_block_kept:
+        return heads_by_device(queries, keys, values, kept, dense_class)
+    return spans_by_device(queries, keys, values, kept, dense_class)
+
+
 def solution(mesh):
     return jax.shard_map(
         shards,

time: 259 us -> 79.8 us (0.31)
  waiting for transfers between devices: 75.2 us -> 0 us
  local copies, waits for them, and re-layouts: 68.6 us -> 4.24 us
  blocking collectives: 37.6 us -> 64.1 us
  matrix products: 22.2 us -> 0 us
  starting transfers between devices: 18.3 us -> 0 us
  between operations: 13.6 us -> 0.09 us
  Pallas kernels: 0 us -> 11.2 us
  loops' own time: 11 us -> 0 us
  other arithmetic: 10.6 us -> 0.16 us
    all_to_all x5 -> x0, waiting for transfers between devices: 75.2 us -> none  [the longest x1 48 us: shards(): lax.all_to_all(shaped_out, 'blk', split_axis=1, concat_axis=1, tiled=True)]
    all_to_all x2, blocking collectives: 37.6 us -> 64.1 us  [the longest x1 43.4 us: heads_by_device(): held = lax.all_to_all(send, axes, split_axis=0, concat_axis=0, tiled=True)]
    dot_general x32 -> x0, matrix products: 22.2 us -> none  [the longest x16 16.6 us: one_group(): jnp.einsum('gpk,gkd->gpd', weights.astype(jnp.bfloat16), gathered_v, pref...]
    gather x35 -> x0, local copies, waits for them, and re-layouts: 21.7 us -> none  [the longest x16 9.96 us: one_group(): blocked_value_rows[ids_group]]
    dynamic_update_slice x24 -> x0, local copies, waits for them, and re-layouts: 21.6 us -> none  [the longest x8 12.2 us: shards(): lax.map(one_item, (query_rows, span_ids // (local_blocks * span_count) *...]
    all_to_all x5 -> x0, starting transfers between devices: 18.3 us -> none  [the longest x1 4.83 us: shards(): lax.all_to_all(shaped_out, 'blk', split_axis=1, concat_axis=1, tiled=True)]
    pallas_call x0 -> x1, Pallas kernels: none -> 11.2 us  [heads_by_device(): pl.pallas_call(lambda *refs: head_kernel(axes, *refs), out_shape=jax.Shap...]
    another operation x9 -> x0, loops' own time: 11 us -> none  [the longest x1 10.6 us: shards(): lax.map(one_item, (query_rows, span_ids // (local_blocks * span_count) *...]
  transfers between devices with their start and end apart: 6 -> 0, of which waited for: 4 -> 0; matrix products, arithmetic and copies ran while one was open for 4% -> 0% of each run, Pallas kernels for 0% -> 0%
where the time goes in v1:
time: 79.8 us
  blocking collectives  64.1 us (80%)
  Pallas kernels  11.2 us (14%)
  local copies, waits for them, and re-layouts  4.24 us (5%)
    all_to_all x1, blocking collectives, heads_by_device(): held = lax.all_to_all(send, axes, split_axis=0, concat_axis=0, tiled=True)  43.4 us
    all_to_all x1, blocking collectives, heads_by_device(): lax.all_to_all(attended, axes, split_axis=0, concat_axis=0, tiled=True)  20.8 us
    pallas_call x1, Pallas kernels, heads_by_device(): pl.pallas_call(lambda *refs: head_kernel(axes, *refs), out_shape=jax.Shap...  11.2 us
    unnamed x11, local copies, waits for them, and re-layouts  2.1 us

profile of v1, /device:TPU:0, one launch (start us, length us, event | category | flops | bytes accessed | tf_op | source)
XLA Modules:
  0.0 79.8 jit_solution(13143510360641217276)
XLA Ops:
  0.0 0.0 copy-start.2
  0.0 1.4 %copy.6 = bf16[128,2048]{0,1:T(8,128)(2,1)S(1)} copy(bf16[128,2048]{1,0:T(8,128)(2,1)} %param.5) | data formatting | bytes 1048576 | tf_op args[0]
  1.4 0.0 copy-start.3
  1.4 0.3 copy.9
  1.7 0.0 copy-done.2
  1.7 0.3 copy.7
  2.0 0.3 copy.10
  2.2 0.2 copy-done.3
  2.4 0.3 copy.8
  2.7 0.3 copy.11
  3.0 0.2 maximum_bitcast_fusion
  3.2 0.0 copy-start
  3.2 0.0 copy-start.1
  3.2 43.4 %all_to_all.10.refs_2_ = bf16[16,3,128,128]{3,2,1,0:T(8,128)(2,1)S(1)} all-to-all(bf16[16,3,128,128]{3,2,1,0:T(8,128)(2,1)S(1)} %maximum_bitcast_fusion), channel_id=1, replica_groups=mesh['clip'=2,'seq'=4,'blk'=4] {'seq','blk'}, dimensions={0} | all-to-all | bytes 3145728 | tf_op jit(solution)/shard_map/all_to_all | solution.py:227
  46.6 0.0 copy-done
  46.6 0.0 copy-done.1
  46.6 11.2 %attend_head.1 = bf16[16,128,128]{2,1,0:T(8,128)(2,1)S(1)} custom-call(s32[16,16,16]{2,1,0:T(8,128)S(1)} %copy-done, s32[16]{0:T(128)S(1)} %copy-done.1, bf16[16,3,128,128]{3,2,1,0:T(8,128)(2,1)S(1)} %all_to_all.10.refs_2_), custom_call_target="tpu_custom_call" | custom-call | tf_op jit(solution)/shard_map/attend_head/pallas_call | solution.py:230
  57.8 20.8 %all_to_all.11 = bf16[16,128,128]{2,1,0:T(8,128)(2,1)S(1)} all-to-all(bf16[16,128,128]{2,1,0:T(8,128)(2,1)S(1)} %attend_head.1), channel_id=1, replica_groups=mesh['clip'=2,'seq'=4,'blk'=4] {'seq','blk'}, dimensions={0} | all-to-all | bytes 1048576 | tf_op jit(solution)/shard_map/all_to_all | solution.py:249
  78.5 0.3 copy.12
  78.8 1.0 %copy.13 = bf16[128,2048]{1,0:T(8,128)(2,1)} copy(bf16[128,2048]{0,1:T(8,128)(2,1)S(1)} %bitcast.8) | data formatting | bytes 1048576 | tf_op jit(solution)/shard_map/reshape | solution.py:250
Async XLA Ops:
  0.0 1.7 %copy-start.2 = (bf16[128,2048]{1,0:T(8,128)(2,1)S(1)}, bf16[128,2048]{1,0:T(8,128)(2,1)}, u32[]{:S(2)}) copy-start(bf16[128,2048]{1,0:T(8,128)(2,1)} %param.6) | copy-start | bytes 1572868
  1.4 1.0 %copy-start.3 = (bf16[128,2048]{1,0:T(8,128)(2,1)S(1)}, bf16[128,2048]{1,0:T(8,128)(2,1)}, u32[]{:S(2)}) copy-start(bf16[128,2048]{1,0:T(8,128)(2,1)} %param.7) | copy-start | bytes 1572868
  3.2 43.4 %copy-start = (s32[16,16,16]{2,1,0:T(8,128)S(1)}, s32[16,16,16]{2,1,0:T(8,128)}, u32[]{:S(2)}) copy-start(s32[16,16,16]{2,1,0:T(8,128)} %refs_0_.1) | copy-start | bytes 49156
  3.2 43.4 %copy-start.1 = (s32[16]{0:T(128)S(1)}, s32[16]{0:T(128)}, u32[]{:S(2)}) copy-start(s32[16]{0:T(128)} %refs_1_.1) | copy-start | bytes 196

commit v2 on v1

--- a/solution.py
+++ b/solution.py
@@ -165,37 +165,145 @@
     return grid_out.transpose(2, 0, 3, 1, 4).reshape(local_rows, head_count * head_depth)
 
 
-def head_kernel(axes, kept_hbm, class_ref, qkv_ref, out_ref, kept_ref, v_all, k_few, v_few, kept_sem):
-    block_count = qkv_ref.shape[0]
-    head_count = class_ref.shape[0]
+def own_head(axes):
     head = 0
     for axis in axes:
         head = head * lax.axis_size(axis) + lax.axis_index(axis)
-    kept_copy = pltpu.make_async_copy(kept_hbm.at[head], kept_ref, kept_sem)
+    return head
+
+
+def read_kept(head, kept_hbm, kept_ref, sem):
+    kept_copy = pltpu.make_async_copy(kept_hbm.at[head], kept_ref, sem)
     kept_copy.start()
     kept_copy.wait()
+
+
+def each_light_block(kept_ref, block):
+    return [
+        kept_ref[block, span * KEEP + slot]
+        for span in range(kept_ref.shape[1] // KEEP)
+        for slot in range(LIGHT)
+    ]
+
+
+def pack_kernel(*refs):
+    sources, out_ref, sems = refs[:-2], refs[-2], refs[-1]
+    copies = []
+    for head in range(out_ref.shape[0]):
+        for place, source in enumerate(sources):
+            copies.append(
+                pltpu.make_async_copy(
+                    source.at[:, head * HD : (head + 1) * HD],
+                    out_ref.at[head, place],
+                    sems.at[head, place],
+                )
+            )
+    for copy in copies:
+        copy.start()
+    for copy in copies:
+        copy.wait()
+
+
+def pack_heads(*sources):
+    count = len(sources)
+    rows = sources[0].shape[0]
+    return pl.pallas_call(
+        pack_kernel,
+        out_shape=jax.ShapeDtypeStruct((HEADS, count, rows, HD), jnp.bfloat16),
+        in_specs=[pl.BlockSpec(memory_space=pl.ANY)] * count,
+        out_specs=pl.BlockSpec(memory_space=pltpu.VMEM),
+        scratch_shapes=[pltpu.SemaphoreType.DMA((HEADS, count))],
+        compiler_params=pltpu.CompilerParams(vmem_limit_bytes=4 * 1024 * 1024),
+        name="pack_heads",
+    )(*sources)
+
+
+def unpack_kernel(held_ref, out_ref, sems):
+    copies = [
+        pltpu.make_async_copy(
+            held_ref.at[head], out_ref.at[:, head * HD : (head + 1) * HD], sems.at[head]
+        )
+        for head in range(held_ref.shape[0])
+    ]
+    for copy in copies:
+        copy.start()
+    for copy in copies:
+        copy.wait()
+
+
+def unpack_heads(held):
+    heads, rows, depth = held.shape
+    return pl.pallas_call(
+        unpack_kernel,
+        out_shape=jax.ShapeDtypeStruct((rows, heads * depth), jnp.bfloat16),
+        in_specs=[pl.BlockSpec(memory_space=pltpu.VMEM)],
+        out_specs=pl.BlockSpec(memory_space=pl.ANY),
+        scratch_shapes=[pltpu.SemaphoreType.DMA((heads,))],
+        compiler_params=pltpu.CompilerParams(vmem_limit_bytes=4 * 1024 * 1024),
+        name="unpack_heads",
+    )(held)
+
+
+def weights_kernel(axes, kept_hbm, class_ref, qk_ref, weights_ref, kept_ref, k_few, sem):
+    block_count = qk_ref.shape[0]
+    head = own_head(axes)
+    read_kept(head, kept_hbm, kept_ref, sem)
     exponent_scale = math.log2(math.e) / math.sqrt(HD)
 
-    def attend(query_rows, key_rows, value_rows):
+    def weigh(query_rows, key_rows):
         logits = lax.dot_general(
             query_rows, key_rows, (((1,), (1,)), ((), ())), preferred_element_type=jnp.float32
         )
         largest = jnp.max(logits, axis=-1, keepdims=True)
-        weights = jnp.exp2((logits - largest) * exponent_scale).astype(jnp.bfloat16)
+        return jnp.exp2((logits - largest) * exponent_scale).astype(jnp.bfloat16)
+
+    @pl.when(class_ref[head] == 1)
+    def _():
+        key_rows = qk_ref[:, 1].reshape(block_count * BLOCK, HD)
+        group = 2
+
+        def step(i, carry):
+            query_rows = qk_ref[pl.ds(i * group, group), 0].reshape(group * BLOCK, HD)
+            weights = weigh(query_rows, key_rows)
+            weights_ref[pl.ds(i * group, group)] = weights.reshape(group, BLOCK, -1)
+            return carry
+
+        lax.fori_loop(0, block_count // group, step, 0)
+
+    @pl.when(class_ref[head] != 1)
+    def _():
+        few_rows = k_few.shape[1]
+
+        def step(i, carry):
+            for lane in range(2):
+                b = i * 2 + lane
+                for place, block in enumerate(each_light_block(kept_ref, b)):
+                    k_few[lane, place * BLOCK : (place + 1) * BLOCK, :] = qk_ref[block, 1]
+                weights_ref[b, :, :few_rows] = weigh(qk_ref[b, 0], k_few[lane])
+            return carry
+
+        lax.fori_loop(0, block_count // 2, step, 0)
+
+
+def values_kernel(axes, kept_hbm, class_ref, weights_ref, v_ref, out_ref, kept_ref, v_all, v_few, sem):
+    block_count = v_ref.shape[0]
+    head = own_head(axes)
+    read_kept(head, kept_hbm, kept_ref, sem)
+
+    def blend(weights, value_rows):
         summed = jnp.dot(weights, value_rows, preferred_element_type=jnp.float32)
         return (summed[:, :HD] / summed[:, HD:]).astype(jnp.bfloat16)
 
     @pl.when(class_ref[head] == 1)
     def _():
-        v_all[:, :, :HD] = qkv_ref[:, 2]
+        v_all[:, :, :HD] = v_ref[...]
         v_all[:, :, HD:] = jnp.ones((block_count, BLOCK, HD), jnp.bfloat16)
-        key_rows = qkv_ref[:, 1].reshape(block_count * BLOCK, HD)
         value_rows = v_all[...].reshape(block_count * BLOCK, 2 * HD)
-        group = 2
+        group = 4
 
         def step(i, carry):
-            query_rows = qkv_ref[pl.ds(i * group, group), 0].reshape(group * BLOCK, HD)
-            out = attend(query_rows, key_rows, value_rows)
+            weights = weights_ref[pl.ds(i * group, group)].reshape(group * BLOCK, -1)
+            out = blend(weights, value_rows)
             out_ref[pl.ds(i * group, group)] = out.reshape(group, BLOCK, HD)
             return carry
 
@@ -203,51 +311,67 @@
 
     @pl.when(class_ref[head] != 1)
     def _():
-        v_few[:, HD:] = jnp.ones((v_few.shape[0], HD), jnp.bfloat16)
-
-        def step(b, carry):
-            place = 0
-            for span in range(kept_ref.shape[1] // KEEP):
-                for slot in range(LIGHT):
-                    block = kept_ref[b, span * KEEP + slot]
-                    k_few[place * BLOCK : (place + 1) * BLOCK, :] = qkv_ref[block, 1]
-                    v_few[place * BLOCK : (place + 1) * BLOCK, :HD] = qkv_ref[block, 2]
-                    place += 1
-            out_ref[b] = attend(qkv_ref[b, 0], k_few[...], v_few[...])
+        few_rows = v_few.shape[1]
+        v_few[:, :, HD:] = jnp.ones((2, few_rows, HD), jnp.bfloat16)
+
+        def step(i, carry):
+            for lane in range(2):
+                b = i * 2 + lane
+                for place, block in enumerate(each_light_block(kept_ref, b)):
+                    v_few[lane, place * BLOCK : (place + 1) * BLOCK, :HD] = v_ref[block]
+                out_ref[b] = blend(weights_ref[b, :, :few_rows], v_few[lane])
             return carry
 
-        lax.fori_loop(0, block_count, step, 0)
+        lax.fori_loop(0, block_count // 2, step, 0)
 
 
 def heads_by_device(queries, keys, values, kept, dense_class):
     axes = ("seq", "blk")
-    local_rows = queries.shape[0]
-    stacked = jnp.stack([queries, keys, values]).reshape(3, local_rows, HEADS, HD)
-    send = stacked.transpose(2, 0, 1, 3)
-    held = lax.all_to_all(send, axes, split_axis=0, concat_axis=0, tiled=True)
     block_count = kept.shape[1]
     few = kept.shape[2] // KEEP * LIGHT
+    any_space = pl.BlockSpec(memory_space=pl.ANY)
+    in_smem = pl.BlockSpec(memory_space=pltpu.SMEM)
+    in_vmem = pl.BlockSpec(memory_space=pltpu.VMEM)
+    limit = pltpu.CompilerParams(vmem_limit_bytes=24 * 1024 * 1024)
+
+    def exchange(send):
+        return lax.all_to_all(send, axes, split_axis=0, concat_axis=0, tiled=True)
+
+    qk_held = exchange(pack_heads(queries, keys))
+    v_held = exchange(pack_heads(values))
+    weights = pl.pallas_call(
+        lambda *refs: weights_kernel(axes, *refs),
+        out_shape=jax.ShapeDtypeStruct((block_count, BLOCK, block_count * BLOCK), jnp.bfloat16),
+        in_specs=[any_space, in_smem, in_vmem],
+        out_specs=in_vmem,
+        scratch_shapes=[
+            pltpu.SMEM(kept.shape[1:], jnp.int32),
+            pltpu.VMEM((2, few * BLOCK, HD), jnp.bfloat16),
+            pltpu.SemaphoreType.DMA,
+        ],
+        compiler_params=limit,
+        cost_estimate=pl.CostEstimate(
+            flops=2 * HD * (block_count * BLOCK) ** 2,
+            bytes_accessed=2 * (block_count * BLOCK) ** 2,
+            transcendentals=(block_count * BLOCK) ** 2,
+        ),
+        name="weigh_keys",
+    )(kept, dense_class, qk_held)
     attended = pl.pallas_call(
-        lambda *refs: head_kernel(axes, *refs),
+        lambda *refs: values_kernel(axes, *refs),
         out_shape=jax.ShapeDtypeStruct((block_count, BLOCK, HD), jnp.bfloat16),
-        in_specs=[
-            pl.BlockSpec(memory_space=pl.ANY),
-            pl.BlockSpec(memory_space=pltpu.SMEM),
-            pl.BlockSpec(memory_space=pltpu.VMEM),
-        ],
-        out_specs=pl.BlockSpec(memory_space=pltpu.VMEM),
+        in_specs=[any_space, in_smem, in_vmem, in_vmem],
+        out_specs=in_vmem,
         scratch_shapes=[
             pltpu.SMEM(kept.shape[1:], jnp.int32),
             pltpu.VMEM((block_count, BLOCK, 2 * HD), jnp.bfloat16),
-            pltpu.VMEM((few * BLOCK, HD), jnp.bfloat16),
-            pltpu.VMEM((few * BLOCK, 2 * HD), jnp.bfloat16),
+            pltpu.VMEM((2, few * BLOCK, 2 * HD), jnp.bfloat16),
             pltpu.SemaphoreType.DMA,
         ],
-        compiler_params=pltpu.CompilerParams(vmem_limit_bytes=48 * 1024 * 1024),
-        name="attend_head",
-    )(kept, dense_class, held)
-    returned = lax.all_to_all(attended, axes, split_axis=0, concat_axis=0, tiled=True)
-    return returned.transpose(1, 0, 2).reshape(local_rows, HEADS * HD)
+        compiler_params=limit,
+        name="blend_values",
+    )(kept, dense_class, weights, v_held.reshape(block_count, BLOCK, HD))
+    return unpack_heads(exchange(attended))
 
 
 def shards(queries, keys, values, kept, dense_class):

time: 79.8 us -> 82.8 us (1.038)
  blocking collectives: 64.1 us -> 18.4 us
  waiting for transfers between devices: 0 us -> 25.7 us
  starting transfers between devices: 0 us -> 14.2 us
  local copies, waits for them, and re-layouts: 4.24 us -> 11.3 us
  Pallas kernels: 11.2 us -> 12.7 us
    all_to_all x2 -> x1, blocking collectives: 64.1 us -> 18.4 us  [exchange(): return lax.all_to_all(send, axes, split_axis=0, concat_axis=0, tiled=True)]
    all_to_all x0 -> x2, waiting for transfers between devices: none -> 25.7 us  [exchange(): return lax.all_to_all(send, axes, split_axis=0, concat_axis=0, tiled=True)]
    all_to_all x0 -> x2, starting transfers between devices: none -> 14.2 us  [exchange(): return lax.all_to_all(send, axes, split_axis=0, concat_axis=0, tiled=True)]
    unnamed x11 -> x18, local copies, waits for them, and re-layouts: 2.1 us -> 11.3 us
    pallas_call x1 -> x5, Pallas kernels: 11.2 us -> 12.7 us  [the longest x1 4.81 us: heads_by_device(): pl.pallas_call(lambda *refs: weights_kernel(axes, *refs), out_shape=jax.S...]
    reshape x1 -> x0, local copies, waits for them, and re-layouts: 1.01 us -> none  [heads_by_device(): return returned.transpose(1, 0, 2).reshape(local_rows, HEADS * HD)]
    another operation x3 -> x0, local copies, waits for them, and re-layouts: 0.85 us -> none  [heads_by_device(): jnp.stack([queries, keys, values]).reshape(3, local_rows, HEADS, HD)]
  transfers between devices with their start and end apart: 0 -> 2, of which waited for: 0 -> 2; matrix products, arithmetic and copies ran while one was open for 0% -> 0% of each run, Pallas kernels for 0% -> 7%
where the time goes in v2:
time: 82.8 us; the launch traced here: 82.3 us
  waiting for transfers between devices  25.7 us (31%)
  blocking collectives  18.4 us (22%)
  starting transfers between devices  14.2 us (17%)
  Pallas kernels  12.7 us (15%)
  local copies, waits for them, and re-layouts  11.3 us (14%)
    all_to_all x2, waiting for transfers between devices, exchange(): return lax.all_to_all(send, axes, split_axis=0, concat_axis=0, tiled=True)  25.7 us
    all_to_all x1, blocking collectives, exchange(): return lax.all_to_all(send, axes, split_axis=0, concat_axis=0, tiled=True)  18.4 us
    all_to_all x2, starting transfers between devices, exchange(): return lax.all_to_all(send, axes, split_axis=0, concat_axis=0, tiled=True)  14.2 us
    unnamed x18, local copies, waits for them, and re-layouts  11.3 us
    pallas_call x1, Pallas kernels, heads_by_device(): pl.pallas_call(lambda *refs: weights_kernel(axes, *refs), out_shape=jax.S...  4.81 us
    pallas_call x1, Pallas kernels, heads_by_device(): pl.pallas_call(lambda *refs: values_kernel(axes, *refs), out_shape=jax.Sh...  4.23 us
    pallas_call x2, Pallas kernels, pack_heads(): pl.pallas_call(pack_kernel, out_shape=jax.ShapeDtypeStruct((HEADS, count,...  2.7 us
  transfers between devices with their start and end apart: 2, of which 2 were waited for; matrix products, arithmetic and copies ran while one was open for 0% of the time, Pallas kernels for 7%

profile of v2, /device:TPU:0, one launch (start us, length us, event | category | flops | bytes accessed | tf_op | source)
XLA Modules:
  0.0 82.3 jit_solution(16306187550088763978)
XLA Ops:
  0.0 0.0 copy-start.3
  0.0 0.0 copy-start.5
  0.0 1.1 %copy-done.5 = bf16[128,2048]{1,0:T(8,128)(2,1)S(1)} copy-done((bf16[128,2048]{1,0:T(8,128)(2,1)S(1)}, bf16[128,2048]{1,0:T(8,128)(2,1)}, u32[]{:S(2)}) %copy-start.5) | copy-done | bytes 524312
  1.1 0.0 copy-start.6
  1.1 1.0 %copy-done.6 = bf16[128,2048]{1,0:T(8,128)(2,1)S(1)} copy-done((bf16[128,2048]{1,0:T(8,128)(2,1)S(1)}, bf16[128,2048]{1,0:T(8,128)(2,1)}, u32[]{:S(2)}) %copy-start.6) | copy-done | bytes 524312
  2.1 0.0 copy-start.8
  2.1 1.6 %pack_heads.2 = bf16[16,2,128,128]{3,2,1,0:T(8,128)(2,1)} custom-call(bf16[128,2048]{1,0:T(8,128)(2,1)S(1)} %copy-done.5, bf16[128,2048]{1,0:T(8,128)(2,1)S(1)} %copy-done.6), custom_call_target="tpu_custom_call" | custom-call | tf_op jit(solution)/shard_map/pack_heads/pallas_call | solution.py:210
  3.7 7.4 %all-to-all-start = ((bf16[16,2,128,128]{3,2,1,0:T(8,128)(2,1)}), bf16[16,2,128,128]{3,2,1,0:T(8,128)(2,1)S(1)}, u32[]{:S(2)}, u32[]{:S(2)}) async-start(bf16[16,2,128,128]{3,2,1,0:T(8,128)(2,1)} %pack_heads.2), calls=%async_computation | async-start | bytes 2097152 | tf_op jit(solution)/shard_map/all_to_all | solution.py:338
  11.1 0.0 copy-start.4
  11.1 1.0 %copy-done.4 = bf16[128,2048]{1,0:T(8,128)(2,1)S(1)} copy-done((bf16[128,2048]{1,0:T(8,128)(2,1)S(1)}, bf16[128,2048]{1,0:T(8,128)(2,1)}, u32[]{:S(2)}) %copy-start.4) | copy-done | bytes 524312
  12.2 1.1 %pack_heads.3 = bf16[16,1,128,128]{3,2,1,0:T(8,128)(2,1)} custom-call(bf16[128,2048]{1,0:T(8,128)(2,1)S(1)} %copy-done.4), custom_call_target="tpu_custom_call" | custom-call | tf_op jit(solution)/shard_map/pack_heads/pallas_call | solution.py:210
  13.3 20.8 %all-to-all-done.refs_2_ = bf16[16,2,128,128]{3,2,1,0:T(8,128)(2,1)S(1)} async-done(((bf16[16,2,128,128]{3,2,1,0:T(8,128)(2,1)}), bf16[16,2,128,128]{3,2,1,0:T(8,128)(2,1)S(1)}, u32[]{:S(2)}, u32[]{:S(2)}) %all-to-all-start) | async-done | bytes 1048608 | tf_op jit(solution)/shard_map/all_to_all | solution.py:338
  34.0 6.9 %all-to-all-start.1 = ((bf16[16,1,128,128]{3,2,1,0:T(8,128)(2,1)}), bf16[16,1,128,128]{3,2,1,0:T(8,128)(2,1)S(1)}, u32[]{:S(2)}, u32[]{:S(2)}) async-start(bf16[16,1,128,128]{3,2,1,0:T(8,128)(2,1)} %pack_heads.3), calls=%async_computation.1 | async-start | bytes 1048576 | tf_op jit(solution)/shard_map/all_to_all | solution.py:338
  40.9 0.0 copy-start.2
  40.9 0.9 %copy-done.2 = s32[16,16,16]{2,1,0:T(8,128)S(1)} copy-done((s32[16,16,16]{2,1,0:T(8,128)S(1)}, s32[16,16,16]{2,1,0:T(8,128)}, u32[]{:S(2)}) %copy-start.2) | copy-done | bytes 16408
  41.8 0.0 copy-start.7
  41.8 0.7 copy-done.7
  42.5 4.8 %weigh_keys.1.refs_2_ = bf16[16,128,2048]{2,1,0:T(8,128)(2,1)S(1)} custom-call(s32[16,16,16]{2,1,0:T(8,128)S(1)} %copy-done.2, s32[16]{0:T(128)S(1)} %copy-done.7, bf16[16,2,128,128]{3,2,1,0:T(8,128)(2,1)S(1)} %all-to-all-done.refs_2_), custom_call_target="tpu_custom_call" | custom-call | flops 1073741824 | bytes 8388608 | tf_op jit(solution)/shard_map/weigh_keys/pallas_call | solution.py:342
  47.3 0.0 copy-start
  47.3 3.2 %copy-done = bf16[16,128,2048]{2,1,0:T(8,128)(2,1)} copy-done((bf16[16,128,2048]{2,1,0:T(8,128)(2,1)}, bf16[16,128,2048]{2,1,0:T(8,128)(2,1)S(1)}, u32[]{:S(2)}) %copy-start) | copy-done | bytes 8388632
  50.5 4.9 %all-to-all-done.1 = bf16[16,1,128,128]{3,2,1,0:T(8,128)(2,1)S(1)} async-done(((bf16[16,1,128,128]{3,2,1,0:T(8,128)(2,1)}), bf16[16,1,128,128]{3,2,1,0:T(8,128)(2,1)S(1)}, u32[]{:S(2)}, u32[]{:S(2)}) %all-to-all-start.1) | async-done | bytes 524320 | tf_op jit(solution)/shard_map/all_to_all | solution.py:338
  55.4 0.0 copy-done.3
  55.4 0.0 copy-done.8
  55.4 0.0 copy-start.1
  55.4 3.4 %copy-done.1 = bf16[16,128,2048]{2,1,0:T(8,128)(2,1)S(1)} copy-done((bf16[16,128,2048]{2,1,0:T(8,128)(2,1)S(1)}, bf16[16,128,2048]{2,1,0:T(8,128)(2,1)}, u32[]{:S(2)}) %copy-start.1) | copy-done | bytes 8388632
  58.8 4.2 %blend_values.1 = bf16[16,128,128]{2,1,0:T(8,128)(2,1)S(1)} custom-call(s32[16,16,16]{2,1,0:T(8,128)S(1)} %copy-done.3, s32[16]{0:T(128)S(1)} %copy-done.8, bf16[16,128,2048]{2,1,0:T(8,128)(2,1)S(1)} %copy-done.1, bf16[16,128,128]{2,1,0:T(8,128)(2,1)S(1)} %bitcast.1), custom_call_target="tpu_custom_call" | custom-call | tf_op jit(solution)/shard_map/blend_values/pallas_call | solution.py:360
  63.0 18.4 %all_to_all.15.held_ref = bf16[16,128,128]{2,1,0:T(8,128)(2,1)S(1)} all-to-all(bf16[16,128,128]{2,1,0:T(8,128)(2,1)S(1)} %blend_values.1), channel_id=1, replica_groups=mesh['clip'=2,'seq'=4,'blk'=4] {'seq','blk'}, dimensions={0} | all-to-all | bytes 1048576 | tf_op jit(solution)/shard_map/all_to_all | solution.py:338
  81.4 0.9 %unpack_heads.1 = bf16[128,2048]{1,0:T(8,128)(2,1)} custom-call(bf16[16,128,128]{2,1,0:T(8,128)(2,1)S(1)} %all_to_all.15.held_ref), custom_call_target="tpu_custom_call" | custom-call | tf_op jit(solution)/shard_map/unpack_heads/pallas_call | solution.py:236
Async XLA Ops:
  0.0 55.4 %copy-start.3 = (s32[16,16,16]{2,1,0:T(8,128)S(1)}, s32[16,16,16]{2,1,0:T(8,128)}, u32[]{:S(2)}) copy-start(s32[16,16,16]{2,1,0:T(8,128)} %refs_0_.7) | copy-start | bytes 49156
  0.0 1.1 %copy-start.5 = (bf16[128,2048]{1,0:T(8,128)(2,1)S(1)}, bf16[128,2048]{1,0:T(8,128)(2,1)}, u32[]{:S(2)}) copy-start(bf16[128,2048]{1,0:T(8,128)(2,1)} %refs_0_.4) | copy-start | bytes 1572868
  1.1 1.0 %copy-start.6 = (bf16[128,2048]{1,0:T(8,128)(2,1)S(1)}, bf16[128,2048]{1,0:T(8,128)(2,1)}, u32[]{:S(2)}) copy-start(bf16[128,2048]{1,0:T(8,128)(2,1)} %refs_1_.3) | copy-start | bytes 1572868
  2.1 53.3 %copy-start.8 = (s32[16]{0:T(128)S(1)}, s32[16]{0:T(128)}, u32[]{:S(2)}) copy-start(s32[16]{0:T(128)} %refs_1_.5) | copy-start | bytes 196
  3.7 30.3 %all-to-all-start = ((bf16[16,2,128,128]{3,2,1,0:T(8,128)(2,1)}), bf16[16,2,128,128]{3,2,1,0:T(8,128)(2,1)S(1)}, u32[]{:S(2)}, u32[]{:S(2)}) async-start(bf16[16,2,128,128]{3,2,1,0:T(8,128)(2,1)} %pack_heads.2), calls=%async_computation | async-start | bytes 2097152 | tf_op jit(solution)/shard_map/all_to_all | solution.py:338
  11.1 1.0 %copy-start.4 = (bf16[128,2048]{1,0:T(8,128)(2,1)S(1)}, bf16[128,2048]{1,0:T(8,128)(2,1)}, u32[]{:S(2)}) copy-start(bf16[128,2048]{1,0:T(8,128)(2,1)} %refs_0_.6) | copy-start | bytes 1572868
  34.0 21.3 %all-to-all-start.1 = ((bf16[16,1,128,128]{3,2,1,0:T(8,128)(2,1)}), bf16[16,1,128,128]{3,2,1,0:T(8,128)(2,1)S(1)}, u32[]{:S(2)}, u32[]{:S(2)}) async-start(bf16[16,1,128,128]{3,2,1,0:T(8,128)(2,1)} %pack_heads.3), calls=%async_computation.1 | async-start | bytes 1048576 | tf_op jit(solution)/shard_map/all_to_all | solution.py:338
  40.9 0.9 %copy-start.2 = (s32[16,16,16]{2,1,0:T(8,128)S(1)}, s32[16,16,16]{2,1,0:T(8,128)}, u32[]{:S(2)}) copy-start(s32[16,16,16]{2,1,0:T(8,128)} %refs_0_.7) | copy-start | bytes 49156
  41.8 0.7 copy-start.7
  47.3 3.2 %copy-start = (bf16[16,128,2048]{2,1,0:T(8,128)(2,1)}, bf16[16,128,2048]{2,1,0:T(8,128)(2,1)S(1)}, u32[]{:S(2)}) copy-start(bf16[16,128,2048]{2,1,0:T(8,128)(2,1)S(1)} %weigh_keys.1.refs_2_) | copy-start | bytes 25165828
  55.4 3.4 %copy-start.1 = (bf16[16,128,2048]{2,1,0:T(8,128)(2,1)S(1)}, bf16[16,128,2048]{2,1,0:T(8,128)(2,1)}, u32[]{:S(2)}) copy-start(bf16[16,128,2048]{2,1,0:T(8,128)(2,1)} %copy-done) | copy-start | bytes 25165828

commit v3 on v0

--- a/solution.py
+++ b/solution.py
@@ -3,6 +3,8 @@
 import jax
 import jax.numpy as jnp
 from jax import lax
+from jax.experimental import pallas as pl
+from jax.experimental.pallas import tpu as pltpu
 from jax.sharding import PartitionSpec as P
 
 HEADS = 16
@@ -73,7 +75,7 @@
     return swapped.reshape((-1,) + stacked.shape[2:])
 
 
-def shards(queries, keys, values, kept, dense_class):
+def spans_by_device(queries, keys, values, kept, dense_class):
     seq_devices = lax.axis_size("seq")
     span_count = lax.axis_size("blk")
     local_rows = queries.shape[0]
@@ -163,6 +165,224 @@
     return grid_out.transpose(2, 0, 3, 1, 4).reshape(local_rows, head_count * head_depth)
 
 
+def own_place(axes):
+    place = 0
+    for axis in axes:
+        place = place * lax.axis_size(axis) + lax.axis_index(axis)
+    return place
+
+
+def each_light_block(kept_ref, block):
+    return [
+        kept_ref[block, span * KEEP + slot]
+        for span in range(kept_ref.shape[1] // KEEP)
+        for slot in range(LIGHT)
+    ]
+
+
+def pack_kernel(*refs):
+    sources, out_ref, sems = refs[:-2], refs[-2], refs[-1]
+    copies = []
+    for head in range(out_ref.shape[0]):
+        for place, source in enumerate(sources):
+            copies.append(
+                pltpu.make_async_copy(
+                    source.at[:, head * HD : (head + 1) * HD],
+                    out_ref.at[head, place],
+                    sems.at[head, place],
+                )
+            )
+    for copy in copies:
+        copy.start()
+    for copy in copies:
+        copy.wait()
+
+
+def pack_heads(*sources):
+    count = len(sources)
+    rows = sources[0].shape[0]
+    return pl.pallas_call(
+        pack_kernel,
+        out_shape=jax.ShapeDtypeStruct((HEADS, count, rows, HD), jnp.bfloat16),
+        in_specs=[pl.BlockSpec(memory_space=pltpu.HBM)] * count,
+        out_specs=pl.BlockSpec(memory_space=pltpu.VMEM),
+        scratch_shapes=[pltpu.SemaphoreType.DMA((HEADS, count))],
+        compiler_params=pltpu.CompilerParams(vmem_limit_bytes=4 * 1024 * 1024),
+        name="pack_heads",
+    )(*sources)
+
+
+def unpack_kernel(axes, *refs):
+    held, out_ref, sems = refs[:-2], refs[-2], refs[-1]
+    me = own_place(axes)
+    copies = []
+    for distance, block in enumerate(held):
+        column = pl.multiple_of((me ^ distance) * HD, HD)
+        copies.append(
+            pltpu.make_async_copy(block, out_ref.at[:, pl.ds(column, HD)], sems.at[distance])
+        )
+    for copy in copies:
+        copy.start()
+    for copy in copies:
+        copy.wait()
+
+
+def unpack_heads(axes, held):
+    rows, depth = held[0].shape
+    heads = len(held)
+    return pl.pallas_call(
+        lambda *refs: unpack_kernel(axes, *refs),
+        out_shape=jax.ShapeDtypeStruct((rows, heads * depth), jnp.bfloat16),
+        in_specs=[pl.BlockSpec(memory_space=pl.ANY)] * heads,
+        out_specs=pl.BlockSpec(memory_space=pltpu.HBM),
+        scratch_shapes=[pltpu.SemaphoreType.DMA((heads,))],
+        compiler_params=pltpu.CompilerParams(vmem_limit_bytes=4 * 1024 * 1024),
+        name="unpack_heads",
+    )(*held)
+
+
+def pipelined(count, score, finish):
+    score(0, 0)
+
+    def step(j, carry):
+        score(2 * j + 1, 1)
+        finish(2 * j, 0)
+        score(2 * j + 2, 0)
+        finish(2 * j + 1, 1)
+        return carry
+
+    lax.fori_loop(0, count // 2 - 1, step, 0)
+    score(count - 1, 1)
+    finish(count - 2, 0)
+    finish(count - 1, 1)
+
+
+def attend_kernel(axes, first, kept_hbm, class_ref, qkv_ref, *refs):
+    (kept_ref, v_all, logits_a, logits_b, k_few, v_few, staged, sem) = refs[-8:]
+    out_refs = refs[:-8]
+    logits_slots = (logits_a, logits_b)
+    count = len(out_refs)
+    block_count = qkv_ref.shape[0]
+    few_rows = v_few.shape[1]
+    me = own_place(axes)
+    exponent_scale = math.log2(math.e) / math.sqrt(HD)
+    kept_copy = pltpu.make_async_copy(kept_hbm.at[me], kept_ref, sem)
+    kept_copy.start()
+
+    def scores(query_rows, key_rows):
+        return lax.dot_general(
+            query_rows, key_rows, (((1,), (1,)), ((), ())), preferred_element_type=jnp.float32
+        )
+
+    def blend(logits, value_rows):
+        largest = jnp.max(logits, axis=-1, keepdims=True)
+        weights = jnp.exp2((logits - largest) * exponent_scale).astype(jnp.bfloat16)
+        summed = jnp.dot(weights, value_rows, preferred_element_type=jnp.float32)
+        return (summed[:, :HD] / summed[:, HD:]).astype(jnp.bfloat16)
+
+    @pl.when(class_ref[me] == 1)
+    def _():
+        v_all[:, :, :HD] = qkv_ref[:, 2]
+        v_all[:, :, HD:] = jnp.ones((block_count, BLOCK, HD), jnp.bfloat16)
+        kept_copy.wait()
+
+        def score(i, slot):
+            query_rows = jnp.concatenate(
+                [qkv_ref[me ^ (first + 2 * i + half), 0] for half in range(2)], axis=0
+            )
+            key_rows = qkv_ref[:, 1].reshape(block_count * BLOCK, HD)
+            logits_slots[slot][...] = scores(query_rows, key_rows)
+
+        def finish(i, slot):
+            value_rows = v_all[...].reshape(block_count * BLOCK, 2 * HD)
+            out = blend(logits_slots[slot][...], value_rows)
+            staged[pl.ds(2 * i, 2)] = out.reshape(2, BLOCK, HD)
+
+        pipelined(count // 2, score, finish)
+
+    @pl.when(class_ref[me] != 1)
+    def _():
+        v_few[:, :, HD:] = jnp.ones((2, few_rows, HD), jnp.bfloat16)
+        kept_copy.wait()
+
+        def score(i, slot):
+            block = me ^ (first + i)
+            for place, kept_block in enumerate(each_light_block(kept_ref, block)):
+                k_few[slot, place * BLOCK : (place + 1) * BLOCK, :] = qkv_ref[kept_block, 1]
+            logits_slots[slot][:BLOCK, :few_rows] = scores(qkv_ref[block, 0], k_few[slot])
+
+        def finish(i, slot):
+            block = me ^ (first + i)
+            for place, kept_block in enumerate(each_light_block(kept_ref, block)):
+                v_few[slot, place * BLOCK : (place + 1) * BLOCK, :HD] = qkv_ref[kept_block, 2]
+            staged[i] = blend(logits_slots[slot][:BLOCK, :few_rows], v_few[slot])
+
+        pipelined(count, score, finish)
+
+    for place, out_ref in enumerate(out_refs):
+        out_ref[...] = staged[place]
+
+
+def heads_by_device(queries, keys, values, kept, dense_class):
+    axes = ("seq", "blk")
+    block_count = kept.shape[1]
+    few = kept.shape[2] // KEEP * LIGHT
+    in_vmem = pl.BlockSpec(memory_space=pltpu.VMEM)
+    held = lax.all_to_all(
+        pack_heads(queries, keys, values), axes, split_axis=0, concat_axis=0, tiled=True
+    )
+
+    def attend(first, count):
+        return pl.pallas_call(
+            lambda *refs: attend_kernel(axes, first, *refs),
+            out_shape=[jax.ShapeDtypeStruct((BLOCK, HD), jnp.bfloat16)] * count,
+            in_specs=[
+                pl.BlockSpec(memory_space=pl.ANY),
+                pl.BlockSpec(memory_space=pltpu.SMEM),
+                in_vmem,
+            ],
+            out_specs=[in_vmem] * count,
+            scratch_shapes=[
+                pltpu.SMEM(kept.shape[1:], jnp.int32),
+                pltpu.VMEM((block_count, BLOCK, 2 * HD), jnp.bfloat16),
+                pltpu.VMEM((2 * BLOCK, block_count * BLOCK), jnp.float32),
+                pltpu.VMEM((2 * BLOCK, block_count * BLOCK), jnp.float32),
+                pltpu.VMEM((2, few * BLOCK, HD), jnp.bfloat16),
+                pltpu.VMEM((2, few * BLOCK, 2 * HD), jnp.bfloat16),
+                pltpu.VMEM((count, BLOCK, HD), jnp.bfloat16),
+                pltpu.SemaphoreType.DMA,
+            ],
+            compiler_params=pltpu.CompilerParams(vmem_limit_bytes=32 * 1024 * 1024),
+            cost_estimate=pl.CostEstimate(
+                flops=4 * HD * BLOCK * count * BLOCK * block_count,
+                bytes_accessed=2 * HD * BLOCK * (3 * block_count + count),
+                transcendentals=BLOCK * count * BLOCK * block_count,
+            ),
+            name="attend_far" if first else "attend_near",
+        )(kept, dense_class, held)
+
+    half = block_count // 2
+    far = attend(half, half)
+    near = attend(0, half)
+    returned = []
+    for distance, block in enumerate(list(near) + list(far)):
+        if distance > 0:
+            pairs = [(i, i ^ distance) for i in range(block_count)]
+            block = lax.ppermute(block, axes, pairs)
+        returned.append(block)
+    return unpack_heads(axes, returned)
+
+
+def shards(queries, keys, values, kept, dense_class):
+    devices = lax.axis_size("seq") * lax.axis_size("blk")
+    one_head_each = devices == HEADS
+    one_block_each = queries.shape[0] == BLOCK
+    every_block_kept = kept.shape[1] == kept.shape[2]
+    if one_head_each and one_block_each and every_block_kept:
+        return heads_by_device(queries, keys, values, kept, dense_class)
+    return spans_by_device(queries, keys, values, kept, dense_class)
+
+
 def solution(mesh):
     return jax.shard_map(
         shards,

time: 259 us -> 82.5 us (0.32)
  waiting for transfers between devices: 75.2 us -> 6.53 us
  local copies, waits for them, and re-layouts: 68.6 us -> 3.14 us
  matrix products: 22.2 us -> 0 us
  between operations: 13.6 us -> 0.07 us
  loops' own time: 11 us -> 0 us
  other arithmetic: 10.6 us -> 0 us
  Pallas kernels: 0 us -> 10.2 us
  blocking collectives: 37.6 us -> 43.4 us
    all_to_all x5 -> x0, waiting for transfers between devices: 75.2 us -> none  [the longest x1 48 us: shards(): lax.all_to_all(shaped_out, 'blk', split_axis=1, concat_axis=1, tiled=True)]
    dot_general x32 -> x0, matrix products: 22.2 us -> none  [the longest x16 16.6 us: one_group(): jnp.einsum('gpk,gkd->gpd', weights.astype(jnp.bfloat16), gathered_v, pref...]
    gather x35 -> x0, local copies, waits for them, and re-layouts: 21.7 us -> none  [the longest x16 9.96 us: one_group(): blocked_value_rows[ids_group]]
    dynamic_update_slice x24 -> x0, local copies, waits for them, and re-layouts: 21.6 us -> none  [the longest x8 12.2 us: shards(): lax.map(one_item, (query_rows, span_ids // (local_blocks * span_count) *...]
    ppermute x0 -> x15, starting transfers between devices: none -> 18.9 us  [heads_by_device(): block = lax.ppermute(block, axes, pairs)]
    all_to_all x5 -> x0, starting transfers between devices: 18.3 us -> none  [the longest x1 4.83 us: shards(): lax.all_to_all(shaped_out, 'blk', split_axis=1, concat_axis=1, tiled=True)]
    another operation x9 -> x0, loops' own time: 11 us -> none  [the longest x1 10.6 us: shards(): lax.map(one_item, (query_rows, span_ids // (local_blocks * span_count) *...]
    pallas_call x0 -> x4, Pallas kernels: none -> 10.2 us  [the longest x2 8.36 us: attend(): pl.pallas_call(lambda *refs: attend_kernel(axes, first, *refs), out_shape...]
  transfers between devices with their start and end apart: 6 -> 15, of which waited for: 4 -> 5; matrix products, arithmetic and copies ran while one was open for 4% -> 0% of each run, Pallas kernels for 0% -> 5%
where the time goes in v3:
time: 82.5 us; the launch traced here: 82.2 us
  blocking collectives  43.4 us (53%)
  starting transfers between devices  18.9 us (23%)
  Pallas kernels  10.2 us (12%)
  waiting for transfers between devices  6.53 us (8%)
  local copies, waits for them, and re-layouts  3.14 us (4%)
    all_to_all x1, blocking collectives, heads_by_device(): lax.all_to_all(pack_heads(queries, keys, values), axes, split_axis=0, con...  43.4 us
    ppermute x15, starting transfers between devices, heads_by_device(): block = lax.ppermute(block, axes, pairs)  18.9 us
    pallas_call x2, Pallas kernels, attend(): pl.pallas_call(lambda *refs: attend_kernel(axes, first, *refs), out_shape...  8.36 us
    ppermute x15, waiting for transfers between devices, heads_by_device(): block = lax.ppermute(block, axes, pairs)  6.53 us
    unnamed x10, local copies, waits for them, and re-layouts  3.14 us
  transfers between devices with their start and end apart: 15, of which 5 were waited for; matrix products, arithmetic and copies ran while one was open for 0% of the time, Pallas kernels for 5%

profile of v3, /device:TPU:0, one launch (start us, length us, event | category | flops | bytes accessed | tf_op | source)
XLA Modules:
  0.0 82.2 jit_solution(1324260329258552078)
XLA Ops:
  0.0 1.0 %copy-done = bf16[128,2048]{1,0:T(8,128)(2,1)S(1)} copy-done((bf16[128,2048]{1,0:T(8,128)(2,1)S(1)}, bf16[128,2048]{1,0:T(8,128)(2,1)}, u32[]{:S(2)}) %copy-start) | copy-done | bytes 524312
  1.0 1.0 %copy-done.1 = bf16[128,2048]{1,0:T(8,128)(2,1)S(1)} copy-done((bf16[128,2048]{1,0:T(8,128)(2,1)S(1)}, bf16[128,2048]{1,0:T(8,128)(2,1)}, u32[]{:S(2)}) %copy-start.1) | copy-done | bytes 524312
  2.1 1.0 %copy-done.2 = bf16[128,2048]{1,0:T(8,128)(2,1)S(1)} copy-done((bf16[128,2048]{1,0:T(8,128)(2,1)S(1)}, bf16[128,2048]{1,0:T(8,128)(2,1)}, u32[]{:S(2)}) %copy-start.2) | copy-done | bytes 524312
  3.1 0.9 %pack_heads.1 = bf16[16,3,128,128]{3,2,1,0:T(8,128)(2,1)S(1)} custom-call(bf16[128,2048]{1,0:T(8,128)(2,1)S(1)} %copy-done, bf16[128,2048]{1,0:T(8,128)(2,1)S(1)} %copy-done.1, bf16[128,2048]{1,0:T(8,128)(2,1)S(1)} %copy-done.2), custom_call_target="tpu_custom_call" | custom-call | tf_op jit(solution)/shard_map/pack_heads/pallas_call | solution.py:204
  4.1 0.0 copy-start.3
  4.1 0.0 copy-start.4
  4.1 43.4 %all_to_all.5.refs_2_ = bf16[16,3,128,128]{3,2,1,0:T(8,128)(2,1)S(1)} all-to-all(bf16[16,3,128,128]{3,2,1,0:T(8,128)(2,1)S(1)} %pack_heads.1), channel_id=1, replica_groups=mesh['clip'=2,'seq'=4,'blk'=4] {'seq','blk'}, dimensions={0} | all-to-all | bytes 3145728 | tf_op jit(solution)/shard_map/all_to_all | solution.py:331
  47.5 4.2 %attend_far.1 = (bf16[128,128]{1,0:T(8,128)(2,1)S(1)}, bf16[128,128]{1,0:T(8,128)(2,1)S(1)}, bf16[128,128]{1,0:T(8,128)(2,1)S(1)}, bf16[128,128]{1,0:T(8,128)(2,...) custom-call(s32[16,16,16]{2,1,0:T(8,128)S(1)} %copy-done.3, ...), custom_call_target="tpu_custom_call" | custom-call | flops 1073741824 | bytes 1835008 | tf_op jit(solution)/shard_map/attend_far/pallas_call | solution.py:336
  51.7 3.2 %collective-permute-start.7 = (bf16[128,128]{1,0:T(8,128)(2,1)S(1)}, bf16[128,128]{1,0:T(8,128)(2,1)S(1)}, u32[]{:S(2)}, u32[]{:S(2)}) collective-permute-start(bf16[128,128]{1,0:T(8,128)(2,1)S(1)} %get-tuple-element.29), channel_id=1, source_target_pairs={{0,8},{1,9},{2,10},{3,11},{4,12},{5,13},{6,14},{7,15},{8,0},{9,1},... | collective-permute-start | bytes 98312 | tf_op jit(solution)/shard_map/ppermute | solution.py:371
  54.8 1.2 %collective-permute-start.9 = (bf16[128,128]{1,0:T(8,128)(2,1)S(1)}, bf16[128,128]{1,0:T(8,128)(2,1)S(1)}, u32[]{:S(2)}, u32[]{:S(2)}) collective-permute-start(bf16[128,128]{1,0:T(8,128)(2,1)S(1)} %get-tuple-element.31), channel_id=1, source_target_pairs={{0,10},{1,11},{2,8},{3,9},{4,14},{5,15},{6,12},{7,13},{8,2},{9,3},... | collective-permute-start | bytes 98312 | tf_op jit(solution)/shard_map/ppermute | solution.py:371
  56.1 2.1 %collective-permute-start.10 = (bf16[128,128]{1,0:T(8,128)(2,1)S(1)}, bf16[128,128]{1,0:T(8,128)(2,1)S(1)}, u32[]{:S(2)}, u32[]{:S(2)}) collective-permute-start(bf16[128,128]{1,0:T(8,128)(2,1)S(1)} %get-tuple-element.32), channel_id=1, source_target_pairs={{0,11},{1,10},{2,9},{3,8},{4,15},{5,14},{6,13},{7,12},{8,3},{9,2},... | collective-permute-start | bytes 98312 | tf_op jit(solution)/shard_map/ppermute | solution.py:371
  58.2 2.0 %collective-permute-start.11 = (bf16[128,128]{1,0:T(8,128)(2,1)S(1)}, bf16[128,128]{1,0:T(8,128)(2,1)S(1)}, u32[]{:S(2)}, u32[]{:S(2)}) collective-permute-start(bf16[128,128]{1,0:T(8,128)(2,1)S(1)} %get-tuple-element.33), channel_id=1, source_target_pairs={{0,12},{1,13},{2,14},{3,15},{4,8},{5,9},{6,10},{7,11},{8,4},{9,5},... | collective-permute-start | bytes 98312 | tf_op jit(solution)/shard_map/ppermute | solution.py:371
  60.1 4.2 %attend_near.1 = (bf16[128,128]{1,0:T(8,128)(2,1)S(1)}, bf16[128,128]{1,0:T(8,128)(2,1)S(1)}, bf16[128,128]{1,0:T(8,128)(2,1)S(1)}, bf16[128,128]{1,0:T(8,128)(2...) custom-call(s32[16,16,16]{2,1,0:T(8,128)S(1)} %copy-done.3, ...), custom_call_target="tpu_custom_call" | custom-call | flops 1073741824 | bytes 1835008 | tf_op jit(solution)/shard_map/attend_near/pallas_call | solution.py:336
  64.3 0.0 collective-permute-done.7.refs_8_
  64.3 1.9 %collective-permute-start.12 = (bf16[128,128]{1,0:T(8,128)(2,1)S(1)}, bf16[128,128]{1,0:T(8,128)(2,1)S(1)}, u32[]{:S(2)}, u32[]{:S(2)}) collective-permute-start(bf16[128,128]{1,0:T(8,128)(2,1)S(1)} %get-tuple-element.34), channel_id=1, source_target_pairs={{0,13},{1,12},{2,15},{3,14},{4,9},{5,8},{6,11},{7,10},{8,5},{9,4},... | collective-permute-start | bytes 98312 | tf_op jit(solution)/shard_map/ppermute | solution.py:371
  66.2 3.1 %collective-permute-start.13 = (bf16[128,128]{1,0:T(8,128)(2,1)S(1)}, bf16[128,128]{1,0:T(8,128)(2,1)S(1)}, u32[]{:S(2)}, u32[]{:S(2)}) collective-permute-start(bf16[128,128]{1,0:T(8,128)(2,1)S(1)} %get-tuple-element.35), channel_id=1, source_target_pairs={{0,14},{1,15},{2,12},{3,13},{4,10},{5,11},{6,8},{7,9},{8,6},{9,7},... | collective-permute-start | bytes 98312 | tf_op jit(solution)/shard_map/ppermute | solution.py:371
  69.3 1.1 %collective-permute-start.14 = (bf16[128,128]{1,0:T(8,128)(2,1)S(1)}, bf16[128,128]{1,0:T(8,128)(2,1)S(1)}, u32[]{:S(2)}, u32[]{:S(2)}) collective-permute-start(bf16[128,128]{1,0:T(8,128)(2,1)S(1)} %get-tuple-element.36), channel_id=1, source_target_pairs={{0,15},{1,14},{2,13},{3,12},{4,11},{5,10},{6,9},{7,8},{8,7},{9,6},... | collective-permute-start | bytes 98312 | tf_op jit(solution)/shard_map/ppermute | solution.py:371
  70.4 0.6 collective-permute-start
  71.0 1.2 %collective-permute-start.1 = (bf16[128,128]{1,0:T(8,128)(2,1)S(1)}, bf16[128,128]{1,0:T(8,128)(2,1)S(1)}, u32[]{:S(2)}, u32[]{:S(2)}) collective-permute-start(bf16[128,128]{1,0:T(8,128)(2,1)S(1)} %get-tuple-element.23), channel_id=1, source_target_pairs={{0,2},{1,3},{2,0},{3,1},{4,6},{5,7},{6,4},{7,5},{8,10},{9,11},{10,... | collective-permute-start | bytes 98312 | tf_op jit(solution)/shard_map/ppermute | solution.py:371
  72.2 0.3 collective-permute-start.2
  72.5 0.3 collective-permute-done.13.refs_14_
  72.8 0.0 collective-permute-start.3
  72.8 2.8 %collective-permute-done.14.refs_15_ = bf16[128,128]{1,0:T(8,128)(2,1)S(1)} collective-permute-done((bf16[128,128]{1,0:T(8,128)(2,1)S(1)}, bf16[128,128]{1,0:T(8,128)(2,1)S(1)}, u32[]{:S(2)}, u32[]{:S(2)}) %collective-permute-start.14) | collective-permute-done | bytes 32800 | tf_op jit(solution)/shard_map/ppermute | solution.py:371
  75.6 0.0 collective-permute-start.4
  75.6 0.0 collective-permute-done.refs_1_
  75.6 1.5 %collective-permute-start.5 = (bf16[128,128]{1,0:T(8,128)(2,1)S(1)}, bf16[128,128]{1,0:T(8,128)(2,1)S(1)}, u32[]{:S(2)}, u32[]{:S(2)}) collective-permute-start(bf16[128,128]{1,0:T(8,128)(2,1)S(1)} %get-tuple-element.27), channel_id=1, source_target_pairs={{0,6},{1,7},{2,4},{3,5},{4,2},{5,3},{6,0},{7,1},{8,14},{9,15},{10,... | collective-permute-start | bytes 98312 | tf_op jit(solution)/shard_map/ppermute | solution.py:371
  77.1 0.0 collective-permute-done.1.refs_2_
  77.1 0.9 %collective-permute-start.6 = (bf16[128,128]{1,0:T(8,128)(2,1)S(1)}, bf16[128,128]{1,0:T(8,128)(2,1)S(1)}, u32[]{:S(2)}, u32[]{:S(2)}) collective-permute-start(bf16[128,128]{1,0:T(8,128)(2,1)S(1)} %get-tuple-element.28), channel_id=1, source_target_pairs={{0,7},{1,6},{2,5},{3,4},{4,3},{5,2},{6,1},{7,0},{8,15},{9,14},{10,... | collective-permute-start | bytes 98312 | tf_op jit(solution)/shard_map/ppermute | solution.py:371
  77.9 1.1 %collective-permute-done.4.refs_5_ = bf16[128,128]{1,0:T(8,128)(2,1)S(1)} collective-permute-done((bf16[128,128]{1,0:T(8,128)(2,1)S(1)}, bf16[128,128]{1,0:T(8,128)(2,1)S(1)}, u32[]{:S(2)}, u32[]{:S(2)}) %collective-permute-start.4) | collective-permute-done | bytes 32800 | tf_op jit(solution)/shard_map/ppermute | solution.py:371
  79.0 1.4 %collective-permute-done.5.refs_6_ = bf16[128,128]{1,0:T(8,128)(2,1)S(1)} collective-permute-done((bf16[128,128]{1,0:T(8,128)(2,1)S(1)}, bf16[128,128]{1,0:T(8,128)(2,1)S(1)}, u32[]{:S(2)}, u32[]{:S(2)}) %collective-permute-start.5) | collective-permute-done | bytes 32800 | tf_op jit(solution)/shard_map/ppermute | solution.py:371
  80.4 0.9 %collective-permute-done.6.refs_7_ = bf16[128,128]{1,0:T(8,128)(2,1)S(1)} collective-permute-done((bf16[128,128]{1,0:T(8,128)(2,1)S(1)}, bf16[128,128]{1,0:T(8,128)(2,1)S(1)}, u32[]{:S(2)}, u32[]{:S(2)}) %collective-permute-start.6) | collective-permute-done | bytes 32800 | tf_op jit(solution)/shard_map/ppermute | solution.py:371
  81.3 0.9 %unpack_heads.1 = bf16[128,2048]{1,0:T(8,128)(2,1)} custom-call(bf16[128,128]{1,0:T(8,128)(2,1)S(1)} %get-tuple-element.21.refs_0_, bf16[128,128]{1,0:T(8,128)(2,1)S(1)} %collective-permute-done.refs_1_, bf16[128,128]{1,0:T(8,128)(2,1)S(1)} %collective-permute-done.1.refs_2_, bf16[128,128]{1,0:T(8,128)(2,1)S(1)} %collective-permute-done.2.refs_3_, ...), custom_call_target="tpu_custom_call" | custom-call | tf_op jit(solution)/shard_map/unpack_heads/pallas_call | solution.py:233
  (13 shorter events, 0.0 us)
Async XLA Ops:
  0.0 1.0 %copy-start = (bf16[128,2048]{1,0:T(8,128)(2,1)S(1)}, bf16[128,2048]{1,0:T(8,128)(2,1)}, u32[]{:S(2)}) copy-start(bf16[128,2048]{1,0:T(8,128)(2,1)} %refs_0_.3) | copy-start | bytes 1572868
  1.0 1.0 %copy-start.1 = (bf16[128,2048]{1,0:T(8,128)(2,1)S(1)}, bf16[128,2048]{1,0:T(8,128)(2,1)}, u32[]{:S(2)}) copy-start(bf16[128,2048]{1,0:T(8,128)(2,1)} %refs_1_.3) | copy-start | bytes 1572868
  2.1 1.0 %copy-start.2 = (bf16[128,2048]{1,0:T(8,128)(2,1)S(1)}, bf16[128,2048]{1,0:T(8,128)(2,1)}, u32[]{:S(2)}) copy-start(bf16[128,2048]{1,0:T(8,128)(2,1)} %refs_2_.1) | copy-start | bytes 1572868
  4.1 43.4 %copy-start.3 = (s32[16,16,16]{2,1,0:T(8,128)S(1)}, s32[16,16,16]{2,1,0:T(8,128)}, u32[]{:S(2)}) copy-start(s32[16,16,16]{2,1,0:T(8,128)} %refs_0_.5) | copy-start | bytes 49156
  4.1 43.4 %copy-start.4 = (s32[16]{0:T(128)S(1)}, s32[16]{0:T(128)}, u32[]{:S(2)}) copy-start(s32[16]{0:T(128)} %refs_1_.5) | copy-start | bytes 196
  51.7 12.7 %collective-permute-start.7 = (bf16[128,128]{1,0:T(8,128)(2,1)S(1)}, bf16[128,128]{1,0:T(8,128)(2,1)S(1)}, u32[]{:S(2)}, u32[]{:S(2)}) collective-permute-start(bf16[128,128]{1,0:T(8,128)(2,1)S(1)} %get-tuple-element.29), channel_id=1, source_target_pairs={{0,8},{1,9},{2,10},{3,11},{4,12},{5,13},{6,14},{7,15},{8,0},{9,1},... | collective-permute-start | bytes 98312 | tf_op jit(solution)/shard_map/ppermute | solution.py:371
  54.8 11.4 %collective-permute-start.8 = (bf16[128,128]{1,0:T(8,128)(2,1)S(1)}, bf16[128,128]{1,0:T(8,128)(2,1)S(1)}, u32[]{:S(2)}, u32[]{:S(2)}) collective-permute-start(bf16[128,128]{1,0:T(8,128)(2,1)S(1)} %get-tuple-element.30), channel_id=1, source_target_pairs={{0,9},{1,8},{2,11},{3,10},{4,13},{5,12},{6,15},{7,14},{8,1},{9,0},... | collective-permute-start | bytes 98312 | tf_op jit(solution)/shard_map/ppermute | solution.py:371
  54.8 14.4 %collective-permute-start.9 = (bf16[128,128]{1,0:T(8,128)(2,1)S(1)}, bf16[128,128]{1,0:T(8,128)(2,1)S(1)}, u32[]{:S(2)}, u32[]{:S(2)}) collective-permute-start(bf16[128,128]{1,0:T(8,128)(2,1)S(1)} %get-tuple-element.31), channel_id=1, source_target_pairs={{0,10},{1,11},{2,8},{3,9},{4,14},{5,15},{6,12},{7,13},{8,2},{9,3},... | collective-permute-start | bytes 98312 | tf_op jit(solution)/shard_map/ppermute | solution.py:371
  56.1 14.3 %collective-permute-start.10 = (bf16[128,128]{1,0:T(8,128)(2,1)S(1)}, bf16[128,128]{1,0:T(8,128)(2,1)S(1)}, u32[]{:S(2)}, u32[]{:S(2)}) collective-permute-start(bf16[128,128]{1,0:T(8,128)(2,1)S(1)} %get-tuple-element.32), channel_id=1, source_target_pairs={{0,11},{1,10},{2,9},{3,8},{4,15},{5,14},{6,13},{7,12},{8,3},{9,2},... | collective-permute-start | bytes 98312 | tf_op jit(solution)/shard_map/ppermute | solution.py:371
  58.2 12.9 %collective-permute-start.11 = (bf16[128,128]{1,0:T(8,128)(2,1)S(1)}, bf16[128,128]{1,0:T(8,128)(2,1)S(1)}, u32[]{:S(2)}, u32[]{:S(2)}) collective-permute-start(bf16[128,128]{1,0:T(8,128)(2,1)S(1)} %get-tuple-element.33), channel_id=1, source_target_pairs={{0,12},{1,13},{2,14},{3,15},{4,8},{5,9},{6,10},{7,11},{8,4},{9,5},... | collective-permute-start | bytes 98312 | tf_op jit(solution)/shard_map/ppermute | solution.py:371
  64.3 7.9 %collective-permute-start.12 = (bf16[128,128]{1,0:T(8,128)(2,1)S(1)}, bf16[128,128]{1,0:T(8,128)(2,1)S(1)}, u32[]{:S(2)}, u32[]{:S(2)}) collective-permute-start(bf16[128,128]{1,0:T(8,128)(2,1)S(1)} %get-tuple-element.34), channel_id=1, source_target_pairs={{0,13},{1,12},{2,15},{3,14},{4,9},{5,8},{6,11},{7,10},{8,5},{9,4},... | collective-permute-start | bytes 98312 | tf_op jit(solution)/shard_map/ppermute | solution.py:371
  66.2 6.6 %collective-permute-start.13 = (bf16[128,128]{1,0:T(8,128)(2,1)S(1)}, bf16[128,128]{1,0:T(8,128)(2,1)S(1)}, u32[]{:S(2)}, u32[]{:S(2)}) collective-permute-start(bf16[128,128]{1,0:T(8,128)(2,1)S(1)} %get-tuple-element.35), channel_id=1, source_target_pairs={{0,14},{1,15},{2,12},{3,13},{4,10},{5,11},{6,8},{7,9},{8,6},{9,7},... | collective-permute-start | bytes 98312 | tf_op jit(solution)/shard_map/ppermute | solution.py:371
  69.3 6.3 %collective-permute-start.14 = (bf16[128,128]{1,0:T(8,128)(2,1)S(1)}, bf16[128,128]{1,0:T(8,128)(2,1)S(1)}, u32[]{:S(2)}, u32[]{:S(2)}) collective-permute-start(bf16[128,128]{1,0:T(8,128)(2,1)S(1)} %get-tuple-element.36), channel_id=1, source_target_pairs={{0,15},{1,14},{2,13},{3,12},{4,11},{5,10},{6,9},{7,8},{8,7},{9,6},... | collective-permute-start | bytes 98312 | tf_op jit(solution)/shard_map/ppermute | solution.py:371
  70.4 5.2 %collective-permute-start = (bf16[128,128]{1,0:T(8,128)(2,1)S(1)}, bf16[128,128]{1,0:T(8,128)(2,1)S(1)}, u32[]{:S(2)}, u32[]{:S(2)}) collective-permute-start(bf16[128,128]{1,0:T(8,128)(2,1)S(1)} %get-tuple-element.22), channel_id=1, source_target_pairs={{0,1},{1,0},{2,3},{3,2},{4,5},{5,4},{6,7},{7,6},{8,9},{9,8},{10,11... | collective-permute-start | bytes 98312 | tf_op jit(solution)/shard_map/ppermute | solution.py:371
  71.0 6.0 %collective-permute-start.1 = (bf16[128,128]{1,0:T(8,128)(2,1)S(1)}, bf16[128,128]{1,0:T(8,128)(2,1)S(1)}, u32[]{:S(2)}, u32[]{:S(2)}) collective-permute-start(bf16[128,128]{1,0:T(8,128)(2,1)S(1)} %get-tuple-element.23), channel_id=1, source_target_pairs={{0,2},{1,3},{2,0},{3,1},{4,6},{5,7},{6,4},{7,5},{8,10},{9,11},{10,... | collective-permute-start | bytes 98312 | tf_op jit(solution)/shard_map/ppermute | solution.py:371
  72.2 5.7 %collective-permute-start.2 = (bf16[128,128]{1,0:T(8,128)(2,1)S(1)}, bf16[128,128]{1,0:T(8,128)(2,1)S(1)}, u32[]{:S(2)}, u32[]{:S(2)}) collective-permute-start(bf16[128,128]{1,0:T(8,128)(2,1)S(1)} %get-tuple-element.24), channel_id=1, source_target_pairs={{0,3},{1,2},{2,1},{3,0},{4,7},{5,6},{6,5},{7,4},{8,11},{9,10},{10,... | collective-permute-start | bytes 98312 | tf_op jit(solution)/shard_map/ppermute | solution.py:371
  72.8 5.1 %collective-permute-start.3 = (bf16[128,128]{1,0:T(8,128)(2,1)S(1)}, bf16[128,128]{1,0:T(8,128)(2,1)S(1)}, u32[]{:S(2)}, u32[]{:S(2)}) collective-permute-start(bf16[128,128]{1,0:T(8,128)(2,1)S(1)} %get-tuple-element.25), channel_id=1, source_target_pairs={{0,4},{1,5},{2,6},{3,7},{4,0},{5,1},{6,2},{7,3},{8,12},{9,13},{10,... | collective-permute-start | bytes 98312 | tf_op jit(solution)/shard_map/ppermute | solution.py:371
  75.6 3.4 %collective-permute-start.4 = (bf16[128,128]{1,0:T(8,128)(2,1)S(1)}, bf16[128,128]{1,0:T(8,128)(2,1)S(1)}, u32[]{:S(2)}, u32[]{:S(2)}) collective-permute-start(bf16[128,128]{1,0:T(8,128)(2,1)S(1)} %get-tuple-element.26), channel_id=1, source_target_pairs={{0,5},{1,4},{2,7},{3,6},{4,1},{5,0},{6,3},{7,2},{8,13},{9,12},{10,... | collective-permute-start | bytes 98312 | tf_op jit(solution)/shard_map/ppermute | solution.py:371
  75.6 4.8 %collective-permute-start.5 = (bf16[128,128]{1,0:T(8,128)(2,1)S(1)}, bf16[128,128]{1,0:T(8,128)(2,1)S(1)}, u32[]{:S(2)}, u32[]{:S(2)}) collective-permute-start(bf16[128,128]{1,0:T(8,128)(2,1)S(1)} %get-tuple-element.27), channel_id=1, source_target_pairs={{0,6},{1,7},{2,4},{3,5},{4,2},{5,3},{6,0},{7,1},{8,14},{9,15},{10,... | collective-permute-start | bytes 98312 | tf_op jit(solution)/shard_map/ppermute | solution.py:371
  77.1 4.3 %collective-permute-start.6 = (bf16[128,128]{1,0:T(8,128)(2,1)S(1)}, bf16[128,128]{1,0:T(8,128)(2,1)S(1)}, u32[]{:S(2)}, u32[]{:S(2)}) collective-permute-start(bf16[128,128]{1,0:T(8,128)(2,1)S(1)} %get-tuple-element.28), channel_id=1, source_target_pairs={{0,7},{1,6},{2,5},{3,4},{4,3},{5,2},{6,1},{7,0},{8,15},{9,14},{10,... | collective-permute-start | bytes 98312 | tf_op jit(solution)/shard_map/ppermute | solution.py:371

commit v4 on v3

--- a/solution.py
+++ b/solution.py
@@ -205,40 +205,37 @@
         pack_kernel,
         out_shape=jax.ShapeDtypeStruct((HEADS, count, rows, HD), jnp.bfloat16),
         in_specs=[pl.BlockSpec(memory_space=pltpu.HBM)] * count,
-        out_specs=pl.BlockSpec(memory_space=pltpu.VMEM),
+        out_specs=pl.BlockSpec(memory_space=pl.ANY),
         scratch_shapes=[pltpu.SemaphoreType.DMA((HEADS, count))],
-        compiler_params=pltpu.CompilerParams(vmem_limit_bytes=4 * 1024 * 1024),
+        compiler_params=pltpu.CompilerParams(vmem_limit_bytes=59 * 1024 * 1024),
         name="pack_heads",
     )(*sources)
 
 
-def unpack_kernel(axes, *refs):
-    held, out_ref, sems = refs[:-2], refs[-2], refs[-1]
-    me = own_place(axes)
-    copies = []
-    for distance, block in enumerate(held):
-        column = pl.multiple_of((me ^ distance) * HD, HD)
-        copies.append(
-            pltpu.make_async_copy(block, out_ref.at[:, pl.ds(column, HD)], sems.at[distance])
-        )
+def unpack_kernel(held_ref, out_ref, sems):
+    copies = [
+        pltpu.make_async_copy(
+            held_ref.at[head], out_ref.at[:, head * HD : (head + 1) * HD], sems.at[head]
+        )
+        for head in range(held_ref.shape[0])
+    ]
     for copy in copies:
         copy.start()
     for copy in copies:
         copy.wait()
 
 
-def unpack_heads(axes, held):
-    rows, depth = held[0].shape
-    heads = len(held)
+def unpack_heads(held):
+    heads, rows, depth = held.shape
     return pl.pallas_call(
-        lambda *refs: unpack_kernel(axes, *refs),
+        unpack_kernel,
         out_shape=jax.ShapeDtypeStruct((rows, heads * depth), jnp.bfloat16),
-        in_specs=[pl.BlockSpec(memory_space=pl.ANY)] * heads,
+        in_specs=[pl.BlockSpec(memory_space=pl.ANY)],
         out_specs=pl.BlockSpec(memory_space=pltpu.HBM),
         scratch_shapes=[pltpu.SemaphoreType.DMA((heads,))],
         compiler_params=pltpu.CompilerParams(vmem_limit_bytes=4 * 1024 * 1024),
         name="unpack_heads",
-    )(*held)
+    )(held)
 
 
 def pipelined(count, score, finish):
@@ -257,120 +254,110 @@
     finish(count - 1, 1)
 
 
-def attend_kernel(axes, first, kept_hbm, class_ref, qkv_ref, *refs):
-    (kept_ref, v_all, logits_a, logits_b, k_few, v_few, staged, sem) = refs[-8:]
-    out_refs = refs[:-8]
+def attend_kernel(axes, kept_hbm, class_ref, qkv_ref, out_ref, kept_ref, v_all, logits_a, logits_b, sem):
     logits_slots = (logits_a, logits_b)
-    count = len(out_refs)
     block_count = qkv_ref.shape[0]
-    few_rows = v_few.shape[1]
     me = own_place(axes)
     exponent_scale = math.log2(math.e) / math.sqrt(HD)
     kept_copy = pltpu.make_async_copy(kept_hbm.at[me], kept_ref, sem)
     kept_copy.start()
+    v_all[:, :, :HD] = qkv_ref[:, 2]
+    v_all[:, :, HD:] = jnp.ones((block_count, BLOCK, HD), jnp.bfloat16)
+    kept_copy.wait()
 
     def scores(query_rows, key_rows):
         return lax.dot_general(
             query_rows, key_rows, (((1,), (1,)), ((), ())), preferred_element_type=jnp.float32
         )
 
-    def blend(logits, value_rows):
+    def weigh(logits):
         largest = jnp.max(logits, axis=-1, keepdims=True)
-        weights = jnp.exp2((logits - largest) * exponent_scale).astype(jnp.bfloat16)
-        summed = jnp.dot(weights, value_rows, preferred_element_type=jnp.float32)
+        return jnp.exp2((logits - largest) * exponent_scale).astype(jnp.bfloat16)
+
+    def normalized(summed):
         return (summed[:, :HD] / summed[:, HD:]).astype(jnp.bfloat16)
 
     @pl.when(class_ref[me] == 1)
     def _():
-        v_all[:, :, :HD] = qkv_ref[:, 2]
-        v_all[:, :, HD:] = jnp.ones((block_count, BLOCK, HD), jnp.bfloat16)
-        kept_copy.wait()
+        group = 2
 
         def score(i, slot):
-            query_rows = jnp.concatenate(
-                [qkv_ref[me ^ (first + 2 * i + half), 0] for half in range(2)], axis=0
-            )
+            query_rows = qkv_ref[pl.ds(group * i, group), 0].reshape(group * BLOCK, HD)
             key_rows = qkv_ref[:, 1].reshape(block_count * BLOCK, HD)
             logits_slots[slot][...] = scores(query_rows, key_rows)
 
         def finish(i, slot):
             value_rows = v_all[...].reshape(block_count * BLOCK, 2 * HD)
-            out = blend(logits_slots[slot][...], value_rows)
-            staged[pl.ds(2 * i, 2)] = out.reshape(2, BLOCK, HD)
-
-        pipelined(count // 2, score, finish)
+            weights = weigh(logits_slots[slot][...])
+            out = normalized(jnp.dot(weights, value_rows, preferred_element_type=jnp.float32))
+            out_ref[pl.ds(group * i, group)] = out.reshape(group, BLOCK, HD)
+
+        pipelined(block_count // group, score, finish)
 
     @pl.when(class_ref[me] != 1)
     def _():
-        v_few[:, :, HD:] = jnp.ones((2, few_rows, HD), jnp.bfloat16)
-        kept_copy.wait()
+        group = 2
+
+        def block_pairs(block):
+            kept_blocks = each_light_block(kept_ref, block)
+            return list(zip(kept_blocks[::2], kept_blocks[1::2]))
 
         def score(i, slot):
-            block = me ^ (first + i)
-            for place, kept_block in enumerate(each_light_block(kept_ref, block)):
-                k_few[slot, place * BLOCK : (place + 1) * BLOCK, :] = qkv_ref[kept_block, 1]
-            logits_slots[slot][:BLOCK, :few_rows] = scores(qkv_ref[block, 0], k_few[slot])
+            for member in range(group):
+                block = group * i + member
+                rows = slice(member * BLOCK, (member + 1) * BLOCK)
+                for place, (one, other) in enumerate(block_pairs(block)):
+                    key_rows = jnp.concatenate([qkv_ref[one, 1], qkv_ref[other, 1]], axis=0)
+                    columns = slice(place * 2 * BLOCK, (place + 1) * 2 * BLOCK)
+                    logits_slots[slot][rows, columns] = scores(qkv_ref[block, 0], key_rows)
 
         def finish(i, slot):
-            block = me ^ (first + i)
-            for place, kept_block in enumerate(each_light_block(kept_ref, block)):
-                v_few[slot, place * BLOCK : (place + 1) * BLOCK, :HD] = qkv_ref[kept_block, 2]
-            staged[i] = blend(logits_slots[slot][:BLOCK, :few_rows], v_few[slot])
-
-        pipelined(count, score, finish)
-
-    for place, out_ref in enumerate(out_refs):
-        out_ref[...] = staged[place]
+            for member in range(group):
+                block = group * i + member
+                rows = slice(member * BLOCK, (member + 1) * BLOCK)
+                pairs = block_pairs(block)
+                weights = weigh(logits_slots[slot][rows, : 2 * BLOCK * len(pairs)])
+                summed = jnp.zeros((BLOCK, 2 * HD), jnp.float32)
+                for place, (one, other) in enumerate(pairs):
+                    value_rows = jnp.concatenate([v_all[one], v_all[other]], axis=0)
+                    columns = slice(place * 2 * BLOCK, (place + 1) * 2 * BLOCK)
+                    summed += jnp.dot(
+                        weights[:, columns], value_rows, preferred_element_type=jnp.float32
+                    )
+                out_ref[block] = normalized(summed)
+
+        pipelined(block_count // group, score, finish)
 
 
 def heads_by_device(queries, keys, values, kept, dense_class):
     axes = ("seq", "blk")
     block_count = kept.shape[1]
-    few = kept.shape[2] // KEEP * LIGHT
     in_vmem = pl.BlockSpec(memory_space=pltpu.VMEM)
-    held = lax.all_to_all(
-        pack_heads(queries, keys, values), axes, split_axis=0, concat_axis=0, tiled=True
-    )
-
-    def attend(first, count):
-        return pl.pallas_call(
-            lambda *refs: attend_kernel(axes, first, *refs),
-            out_shape=[jax.ShapeDtypeStruct((BLOCK, HD), jnp.bfloat16)] * count,
-            in_specs=[
-                pl.BlockSpec(memory_space=pl.ANY),
-                pl.BlockSpec(memory_space=pltpu.SMEM),
-                in_vmem,
-            ],
-            out_specs=[in_vmem] * count,
-            scratch_shapes=[
-                pltpu.SMEM(kept.shape[1:], jnp.int32),
-                pltpu.VMEM((block_count, BLOCK, 2 * HD), jnp.bfloat16),
-                pltpu.VMEM((2 * BLOCK, block_count * BLOCK), jnp.float32),
-                pltpu.VMEM((2 * BLOCK, block_count * BLOCK), jnp.float32),
-                pltpu.VMEM((2, few * BLOCK, HD), jnp.bfloat16),
-                pltpu.VMEM((2, few * BLOCK, 2 * HD), jnp.bfloat16),
-                pltpu.VMEM((count, BLOCK, HD), jnp.bfloat16),
-                pltpu.SemaphoreType.DMA,
-            ],
-            compiler_params=pltpu.CompilerParams(vmem_limit_bytes=32 * 1024 * 1024),
-            cost_estimate=pl.CostEstimate(
-                flops=4 * HD * BLOCK * count * BLOCK * block_count,
-                bytes_accessed=2 * HD * BLOCK * (3 * block_count + count),
-                transcendentals=BLOCK * count * BLOCK * block_count,
-            ),
-            name="attend_far" if first else "attend_near",
-        )(kept, dense_class, held)
-
-    half = block_count // 2
-    far = attend(half, half)
-    near = attend(0, half)
-    returned = []
-    for distance, block in enumerate(list(near) + list(far)):
-        if distance > 0:
-            pairs = [(i, i ^ distance) for i in range(block_count)]
-            block = lax.ppermute(block, axes, pairs)
-        returned.append(block)
-    return unpack_heads(axes, returned)
+
+    def exchange(send):
+        return lax.all_to_all(send, axes, split_axis=0, concat_axis=0, tiled=True)
+
+    held = exchange(pack_heads(queries, keys, values))
+    attended = pl.pallas_call(
+        lambda *refs: attend_kernel(axes, *refs),
+        out_shape=jax.ShapeDtypeStruct((block_count, BLOCK, HD), jnp.bfloat16),
+        in_specs=[
+            pl.BlockSpec(memory_space=pl.ANY),
+            pl.BlockSpec(memory_space=pltpu.SMEM),
+            in_vmem,
+        ],
+        out_specs=in_vmem,
+        scratch_shapes=[
+            pltpu.SMEM(kept.shape[1:], jnp.int32),
+            pltpu.VMEM((block_count, BLOCK, 2 * HD), jnp.bfloat16),
+            pltpu.VMEM((2 * BLOCK, block_count * BLOCK), jnp.float32),
+            pltpu.VMEM((2 * BLOCK, block_count * BLOCK), jnp.float32),
+            pltpu.SemaphoreType.DMA,
+        ],
+        compiler_params=pltpu.CompilerParams(vmem_limit_bytes=32 * 1024 * 1024),
+        name="attend_head",
+    )(kept, dense_class, held)
+    return unpack_heads(exchange(attended))
 
 
 def shards(queries, keys, values, kept, dense_class):

time: 82.5 us -> 120 us (1.45)
  Pallas kernels: 10.2 us -> 57.3 us
  blocking collectives: 43.4 us -> 62.3 us
  starting transfers between devices: 18.9 us -> 0 us
  waiting for transfers between devices: 6.53 us -> 0 us
  local copies, waits for them, and re-layouts: 3.14 us -> 0.01 us
    pallas_call x1, Pallas kernels: 0.94 us -> 49.2 us  [pack_heads(): pl.pallas_call(pack_kernel, out_shape=jax.ShapeDtypeStruct((HEADS, count,...]
    all_to_all x1 -> x2, blocking collectives: 43.4 us -> 62.3 us  [exchange(): return lax.all_to_all(send, axes, split_axis=0, concat_axis=0, tiled=True)]
    ppermute x15 -> x0, starting transfers between devices: 18.9 us -> none  [heads_by_device(): block = lax.ppermute(block, axes, pairs)]
    ppermute x15 -> x0, waiting for transfers between devices: 6.53 us -> none  [heads_by_device(): block = lax.ppermute(block, axes, pairs)]
    unnamed x10 -> x4, local copies, waits for them, and re-layouts: 3.14 us -> 0.01 us
    pallas_call x3 -> x2, Pallas kernels: 9.27 us -> 8.09 us  [the longest x1 7.18 us: heads_by_device(): pl.pallas_call(lambda *refs: attend_kernel(axes, *refs), out_shape=jax.Sh...]
  transfers between devices with their start and end apart: 15 -> 0, of which waited for: 5 -> 0; matrix products, arithmetic and copies ran while one was open for 0% -> 0% of each run, Pallas kernels for 5% -> 0%
where the time goes in v4:
time: 120 us
  blocking collectives  62.3 us (52%)
  Pallas kernels  57.3 us (48%)
    all_to_all x2, blocking collectives, exchange(): return lax.all_to_all(send, axes, split_axis=0, concat_axis=0, tiled=True)  62.3 us
    pallas_call x1, Pallas kernels, pack_heads(): pl.pallas_call(pack_kernel, out_shape=jax.ShapeDtypeStruct((HEADS, count,...  49.2 us
    pallas_call x1, Pallas kernels, heads_by_device(): pl.pallas_call(lambda *refs: attend_kernel(axes, *refs), out_shape=jax.Sh...  7.18 us

profile of v4, /device:TPU:0, one launch (start us, length us, event | category | flops | bytes accessed | tf_op | source)
XLA Modules:
  0.0 119.7 jit_solution(5086105854614350326)
XLA Ops:
  0.0 49.2 %pack_heads.1 = bf16[16,3,128,128]{3,2,1,0:T(8,128)(2,1)} custom-call(bf16[128,2048]{1,0:T(8,128)(2,1)} %refs_0_.2, bf16[128,2048]{1,0:T(8,128)(2,1)} %refs_1_.2, bf16[128,2048]{1,0:T(8,128)(2,1)} %refs_2_.1), custom_call_target="tpu_custom_call" | custom-call | tf_op jit(solution)/shard_map/pack_heads/pallas_call | solution.py:204
  49.2 0.0 copy-start
  49.2 0.0 copy-start.1
  49.2 43.6 %all_to_all.10.refs_2_ = bf16[16,3,128,128]{3,2,1,0:T(8,128)(2,1)S(1)} all-to-all(bf16[16,3,128,128]{3,2,1,0:T(8,128)(2,1)} %pack_heads.1), channel_id=1, replica_groups=mesh['clip'=2,'seq'=4,'blk'=4] {'seq','blk'}, dimensions={0} | all-to-all | bytes 3145728 | tf_op jit(solution)/shard_map/all_to_all | solution.py:338
  92.8 0.0 copy-done
  92.8 0.0 copy-done.1
  92.8 7.2 %attend_head.1 = bf16[16,128,128]{2,1,0:T(8,128)(2,1)S(1)} custom-call(s32[16,16,16]{2,1,0:T(8,128)S(1)} %copy-done, s32[16]{0:T(128)S(1)} %copy-done.1, bf16[16,3,128,128]{3,2,1,0:T(8,128)(2,1)S(1)} %all_to_all.10.refs_2_), custom_call_target="tpu_custom_call" | custom-call | tf_op jit(solution)/shard_map/attend_head/pallas_call | solution.py:341
  100.0 18.8 %all_to_all.11.held_ref = bf16[16,128,128]{2,1,0:T(8,128)(2,1)S(1)} all-to-all(bf16[16,128,128]{2,1,0:T(8,128)(2,1)S(1)} %attend_head.1), channel_id=1, replica_groups=mesh['clip'=2,'seq'=4,'blk'=4] {'seq','blk'}, dimensions={0} | all-to-all | bytes 1048576 | tf_op jit(solution)/shard_map/all_to_all | solution.py:338
  118.7 0.9 unpack_heads.1
Async XLA Ops:
  49.2 43.6 %copy-start = (s32[16,16,16]{2,1,0:T(8,128)S(1)}, s32[16,16,16]{2,1,0:T(8,128)}, u32[]{:S(2)}) copy-start(s32[16,16,16]{2,1,0:T(8,128)} %refs_0_.3) | copy-start | bytes 49156
  49.2 43.6 %copy-start.1 = (s32[16]{0:T(128)S(1)}, s32[16]{0:T(128)}, u32[]{:S(2)}) copy-start(s32[16]{0:T(128)} %refs_1_.3) | copy-start | bytes 196

commit v5 on v4

--- a/solution.py
+++ b/solution.py
@@ -172,29 +172,38 @@
     return place
 
 
-def each_light_block(kept_ref, block):
-    return [
-        kept_ref[block, span * KEEP + slot]
-        for span in range(kept_ref.shape[1] // KEEP)
-        for slot in range(LIGHT)
+def each_light_place(kept_ref, place, seq_devices, span_count):
+    block = place % seq_devices * span_count + place // seq_devices
+    kept_blocks = [
+        kept_ref[block, span * KEEP + slot] for span in range(span_count) for slot in range(LIGHT)
     ]
+    return [kept % span_count * seq_devices + kept // span_count for kept in kept_blocks]
 
 
 def pack_kernel(*refs):
-    sources, out_ref, sems = refs[:-2], refs[-2], refs[-1]
-    copies = []
-    for head in range(out_ref.shape[0]):
-        for place, source in enumerate(sources):
-            copies.append(
+    sources, (out_ref, staged, in_sems, out_sems) = refs[:-4], refs[-4:]
+    heads, count = staged.shape[:2]
+    arrivals, departures = [], []
+    for head in range(heads):
+        for place in range(count):
+            arrivals.append(
                 pltpu.make_async_copy(
-                    source.at[:, head * HD : (head + 1) * HD],
-                    out_ref.at[head, place],
-                    sems.at[head, place],
+                    sources[place].at[:, head * HD : (head + 1) * HD],
+                    staged.at[head, place],
+                    in_sems.at[head, place],
                 )
             )
-    for copy in copies:
+            departures.append(
+                pltpu.make_async_copy(
+                    staged.at[head, place], out_ref.at[head, place], out_sems.at[head, place]
+                )
+            )
+    for copy in arrivals:
         copy.start()
-    for copy in copies:
+    for arrival, departure in zip(arrivals, departures):
+        arrival.wait()
+        departure.start()
+    for copy in departures:
         copy.wait()
 
 
@@ -206,7 +215,11 @@
         out_shape=jax.ShapeDtypeStruct((HEADS, count, rows, HD), jnp.bfloat16),
         in_specs=[pl.BlockSpec(memory_space=pltpu.HBM)] * count,
         out_specs=pl.BlockSpec(memory_space=pl.ANY),
-        scratch_shapes=[pltpu.SemaphoreType.DMA((HEADS, count))],
+        scratch_shapes=[
+            pltpu.VMEM((HEADS, count, rows, HD), jnp.bfloat16),
+            pltpu.SemaphoreType.DMA((HEADS, count)),
+            pltpu.SemaphoreType.DMA((HEADS, count)),
+        ],
         compiler_params=pltpu.CompilerParams(vmem_limit_bytes=59 * 1024 * 1024),
         name="pack_heads",
     )(*sources)
@@ -257,6 +270,7 @@
 def attend_kernel(axes, kept_hbm, class_ref, qkv_ref, out_ref, kept_ref, v_all, logits_a, logits_b, sem):
     logits_slots = (logits_a, logits_b)
     block_count = qkv_ref.shape[0]
+    seq_devices, span_count = lax.axis_size("seq"), lax.axis_size("blk")
     me = own_place(axes)
     exponent_scale = math.log2(math.e) / math.sqrt(HD)
     kept_copy = pltpu.make_async_copy(kept_hbm.at[me], kept_ref, sem)
@@ -279,7 +293,7 @@
 
     @pl.when(class_ref[me] == 1)
     def _():
-        group = 2
+        group = 4
 
         def score(i, slot):
             query_rows = qkv_ref[pl.ds(group * i, group), 0].reshape(group * BLOCK, HD)
@@ -298,9 +312,9 @@
     def _():
         group = 2
 
-        def block_pairs(block):
-            kept_blocks = each_light_block(kept_ref, block)
-            return list(zip(kept_blocks[::2], kept_blocks[1::2]))
+        def block_pairs(place):
+            kept_places = each_light_place(kept_ref, place, seq_devices, span_count)
+            return list(zip(kept_places[::2], kept_places[1::2]))
 
         def score(i, slot):
             for member in range(group):
@@ -330,7 +344,7 @@
 
 
 def heads_by_device(queries, keys, values, kept, dense_class):
-    axes = ("seq", "blk")
+    axes = ("blk", "seq")
     block_count = kept.shape[1]
     in_vmem = pl.BlockSpec(memory_space=pltpu.VMEM)
 
@@ -350,8 +364,8 @@
         scratch_shapes=[
             pltpu.SMEM(kept.shape[1:], jnp.int32),
             pltpu.VMEM((block_count, BLOCK, 2 * HD), jnp.bfloat16),
-            pltpu.VMEM((2 * BLOCK, block_count * BLOCK), jnp.float32),
-            pltpu.VMEM((2 * BLOCK, block_count * BLOCK), jnp.float32),
+            pltpu.VMEM((4 * BLOCK, block_count * BLOCK), jnp.float32),
+            pltpu.VMEM((4 * BLOCK, block_count * BLOCK), jnp.float32),
             pltpu.SemaphoreType.DMA,
         ],
         compiler_params=pltpu.CompilerParams(vmem_limit_bytes=32 * 1024 * 1024),

time: 120 us -> 74.8 us (0.62)
  Pallas kernels: 57.3 us -> 10.2 us
  blocking collectives: 62.3 us -> 64.2 us
    pallas_call x1, Pallas kernels: 49.2 us -> 2.86 us  [pack_heads(): pl.pallas_call(pack_kernel, out_shape=jax.ShapeDtypeStruct((HEADS, count,...]
    all_to_all x2, blocking collectives: 62.3 us -> 64.2 us  [exchange(): return lax.all_to_all(send, axes, split_axis=0, concat_axis=0, tiled=True)]
where the time goes in v5:
time: 74.8 us; the launch traced here: 74.5 us
  blocking collectives  64.2 us (86%)
  Pallas kernels  10.2 us (14%)
    all_to_all x2, blocking collectives, exchange(): return lax.all_to_all(send, axes, split_axis=0, concat_axis=0, tiled=True)  64.2 us
    pallas_call x1, Pallas kernels, heads_by_device(): pl.pallas_call(lambda *refs: attend_kernel(axes, *refs), out_shape=jax.Sh...  6.46 us
    pallas_call x1, Pallas kernels, pack_heads(): pl.pallas_call(pack_kernel, out_shape=jax.ShapeDtypeStruct((HEADS, count,...  2.86 us

profile of v5, /device:TPU:0, one launch (start us, length us, event | category | flops | bytes accessed | tf_op | source)
XLA Modules:
  0.0 74.5 jit_solution(10283816222735362150)
XLA Ops:
  0.0 2.9 %pack_heads.1 = bf16[16,3,128,128]{3,2,1,0:T(8,128)(2,1)} custom-call(bf16[128,2048]{1,0:T(8,128)(2,1)} %refs_0_.2, bf16[128,2048]{1,0:T(8,128)(2,1)} %refs_1_.2, bf16[128,2048]{1,0:T(8,128)(2,1)} %refs_2_.1), custom_call_target="tpu_custom_call" | custom-call | tf_op jit(solution)/shard_map/pack_heads/pallas_call | solution.py:213
  2.9 0.0 copy-start
  2.9 0.0 copy-start.1
  2.9 45.7 %all_to_all.10.refs_2_ = bf16[16,3,128,128]{3,2,1,0:T(8,128)(2,1)S(1)} all-to-all(bf16[16,3,128,128]{3,2,1,0:T(8,128)(2,1)} %pack_heads.1), channel_id=1, replica_groups=mesh['clip'=2,'seq'=4,'blk'=4] {'blk','seq'}, dimensions={0} | all-to-all | bytes 3145728 | tf_op jit(solution)/shard_map/all_to_all | solution.py:352
  48.6 0.0 copy-done
  48.6 0.0 copy-done.1
  48.6 6.5 %attend_head.1 = bf16[16,128,128]{2,1,0:T(8,128)(2,1)S(1)} custom-call(s32[16,16,16]{2,1,0:T(8,128)S(1)} %copy-done, s32[16]{0:T(128)S(1)} %copy-done.1, bf16[16,3,128,128]{3,2,1,0:T(8,128)(2,1)S(1)} %all_to_all.10.refs_2_), custom_call_target="tpu_custom_call" | custom-call | tf_op jit(solution)/shard_map/attend_head/pallas_call | solution.py:355
  55.1 18.5 %all_to_all.11.held_ref = bf16[16,128,128]{2,1,0:T(8,128)(2,1)S(1)} all-to-all(bf16[16,128,128]{2,1,0:T(8,128)(2,1)S(1)} %attend_head.1), channel_id=1, replica_groups=mesh['clip'=2,'seq'=4,'blk'=4] {'blk','seq'}, dimensions={0} | all-to-all | bytes 1048576 | tf_op jit(solution)/shard_map/all_to_all | solution.py:352
  73.5 0.9 %unpack_heads.1 = bf16[128,2048]{1,0:T(8,128)(2,1)} custom-call(bf16[16,128,128]{2,1,0:T(8,128)(2,1)S(1)} %all_to_all.11.held_ref), custom_call_target="tpu_custom_call" | custom-call | tf_op jit(solution)/shard_map/unpack_heads/pallas_call | solution.py:243
Async XLA Ops:
  2.9 45.7 %copy-start = (s32[16,16,16]{2,1,0:T(8,128)S(1)}, s32[16,16,16]{2,1,0:T(8,128)}, u32[]{:S(2)}) copy-start(s32[16,16,16]{2,1,0:T(8,128)} %refs_0_.3) | copy-start | bytes 49156
  2.9 45.7 %copy-start.1 = (s32[16]{0:T(128)S(1)}, s32[16]{0:T(128)}, u32[]{:S(2)}) copy-start(s32[16]{0:T(128)} %refs_1_.3) | copy-start | bytes 196

commit v6 on v4

--- a/solution.py
+++ b/solution.py
@@ -181,32 +181,54 @@
 
 
 def pack_kernel(*refs):
-    sources, out_ref, sems = refs[:-2], refs[-2], refs[-1]
-    copies = []
-    for head in range(out_ref.shape[0]):
-        for place, source in enumerate(sources):
-            copies.append(
-                pltpu.make_async_copy(
-                    source.at[:, head * HD : (head + 1) * HD],
-                    out_ref.at[head, place],
-                    sems.at[head, place],
-                )
+    sources, (out_ref, landed, staged, in_sems, out_sems) = refs[:-5], refs[-5:]
+    heads = out_ref.shape[0]
+    count, rows = landed.shape[:2]
+    pieces = in_sems.shape[1]
+    piece_rows = rows // pieces
+    arrivals = [
+        [
+            pltpu.make_async_copy(
+                source.at[pl.ds(piece * piece_rows, piece_rows), :],
+                landed.at[place, pl.ds(piece * piece_rows, piece_rows), :],
+                in_sems.at[place, piece],
             )
-    for copy in copies:
-        copy.start()
-    for copy in copies:
+            for piece in range(pieces)
+        ]
+        for place, source in enumerate(sources)
+    ]
+    departures = [
+        pltpu.make_async_copy(staged.at[place], out_ref.at[:, place], out_sems.at[place])
+        for place in range(count)
+    ]
+    for copies in arrivals:
+        for copy in copies:
+            copy.start()
+    for place in range(count):
+        for copy in arrivals[place]:
+            copy.wait()
+        for head in range(heads):
+            staged[place, head] = landed[place, :, head * HD : (head + 1) * HD]
+        departures[place].start()
+    for copy in departures:
         copy.wait()
 
 
 def pack_heads(*sources):
     count = len(sources)
     rows = sources[0].shape[0]
+    pieces = 4
     return pl.pallas_call(
         pack_kernel,
         out_shape=jax.ShapeDtypeStruct((HEADS, count, rows, HD), jnp.bfloat16),
         in_specs=[pl.BlockSpec(memory_space=pltpu.HBM)] * count,
         out_specs=pl.BlockSpec(memory_space=pl.ANY),
-        scratch_shapes=[pltpu.SemaphoreType.DMA((HEADS, count))],
+        scratch_shapes=[
+            pltpu.VMEM((count, rows, HEADS * HD), jnp.bfloat16),
+            pltpu.VMEM((count, HEADS, rows, HD), jnp.bfloat16),
+            pltpu.SemaphoreType.DMA((count, pieces)),
+            pltpu.SemaphoreType.DMA((count,)),
+        ],
         compiler_params=pltpu.CompilerParams(vmem_limit_bytes=59 * 1024 * 1024),
         name="pack_heads",
     )(*sources)
@@ -238,65 +260,75 @@
     )(held)
 
 
-def pipelined(count, score, finish):
+def pipelined(count, score, weigh, blend):
     score(0, 0)
+    weigh(0, 0)
+    score(1, 1)
 
     def step(j, carry):
-        score(2 * j + 1, 1)
-        finish(2 * j, 0)
+        blend(2 * j, 0)
+        weigh(2 * j + 1, 1)
         score(2 * j + 2, 0)
-        finish(2 * j + 1, 1)
+        blend(2 * j + 1, 1)
+        weigh(2 * j + 2, 0)
+        score(2 * j + 3, 1)
         return carry
 
     lax.fori_loop(0, count // 2 - 1, step, 0)
-    score(count - 1, 1)
-    finish(count - 2, 0)
-    finish(count - 1, 1)
-
-
-def attend_kernel(axes, kept_hbm, class_ref, qkv_ref, out_ref, kept_ref, v_all, logits_a, logits_b, sem):
+    blend(count - 2, 0)
+    weigh(count - 1, 1)
+    blend(count - 1, 1)
+
+
+def attend_kernel(axes, kept_hbm, class_ref, qkv_ref, out_ref, *scratch):
+    kept_ref, v_all, logits_a, logits_b, weights_a, weights_b, sem = scratch
     logits_slots = (logits_a, logits_b)
+    weights_slots = (weights_a, weights_b)
     block_count = qkv_ref.shape[0]
     me = own_place(axes)
+    group = 2
     exponent_scale = math.log2(math.e) / math.sqrt(HD)
     kept_copy = pltpu.make_async_copy(kept_hbm.at[me], kept_ref, sem)
     kept_copy.start()
     v_all[:, :, :HD] = qkv_ref[:, 2]
     v_all[:, :, HD:] = jnp.ones((block_count, BLOCK, HD), jnp.bfloat16)
-    kept_copy.wait()
 
     def scores(query_rows, key_rows):
         return lax.dot_general(
             query_rows, key_rows, (((1,), (1,)), ((), ())), preferred_element_type=jnp.float32
         )
 
-    def weigh(logits):
+    def weigh(columns, slot):
+        logits = logits_slots[slot][:, :columns]
         largest = jnp.max(logits, axis=-1, keepdims=True)
-        return jnp.exp2((logits - largest) * exponent_scale).astype(jnp.bfloat16)
+        weights = jnp.exp2((logits - largest) * exponent_scale).astype(jnp.bfloat16)
+        weights_slots[slot][:, :columns] = weights
 
     def normalized(summed):
         return (summed[:, :HD] / summed[:, HD:]).astype(jnp.bfloat16)
 
     @pl.when(class_ref[me] == 1)
     def _():
-        group = 2
-
         def score(i, slot):
             query_rows = qkv_ref[pl.ds(group * i, group), 0].reshape(group * BLOCK, HD)
             key_rows = qkv_ref[:, 1].reshape(block_count * BLOCK, HD)
             logits_slots[slot][...] = scores(query_rows, key_rows)
 
-        def finish(i, slot):
+        def blend(i, slot):
             value_rows = v_all[...].reshape(block_count * BLOCK, 2 * HD)
-            weights = weigh(logits_slots[slot][...])
-            out = normalized(jnp.dot(weights, value_rows, preferred_element_type=jnp.float32))
+            out = normalized(
+                jnp.dot(weights_slots[slot][...], value_rows, preferred_element_type=jnp.float32)
+            )
             out_ref[pl.ds(group * i, group)] = out.reshape(group, BLOCK, HD)
 
-        pipelined(block_count // group, score, finish)
+        all_columns = block_count * BLOCK
+        pipelined(block_count // group, score, lambda i, slot: weigh(all_columns, slot), blend)
+        kept_copy.wait()
 
     @pl.when(class_ref[me] != 1)
     def _():
-        group = 2
+        kept_copy.wait()
+        few_columns = block_count // KEEP * LIGHT * BLOCK
 
         def block_pairs(block):
             kept_blocks = each_light_block(kept_ref, block)
@@ -311,22 +343,19 @@
                     columns = slice(place * 2 * BLOCK, (place + 1) * 2 * BLOCK)
                     logits_slots[slot][rows, columns] = scores(qkv_ref[block, 0], key_rows)
 
-        def finish(i, slot):
+        def blend(i, slot):
             for member in range(group):
                 block = group * i + member
                 rows = slice(member * BLOCK, (member + 1) * BLOCK)
-                pairs = block_pairs(block)
-                weights = weigh(logits_slots[slot][rows, : 2 * BLOCK * len(pairs)])
                 summed = jnp.zeros((BLOCK, 2 * HD), jnp.float32)
-                for place, (one, other) in enumerate(pairs):
+                for place, (one, other) in enumerate(block_pairs(block)):
                     value_rows = jnp.concatenate([v_all[one], v_all[other]], axis=0)
                     columns = slice(place * 2 * BLOCK, (place + 1) * 2 * BLOCK)
-                    summed += jnp.dot(
-                        weights[:, columns], value_rows, preferred_element_type=jnp.float32
-                    )
+                    weights = weights_slots[slot][rows, columns]
+                    summed += jnp.dot(weights, value_rows, preferred_element_type=jnp.float32)
                 out_ref[block] = normalized(summed)
 
-        pipelined(block_count // group, score, finish)
+        pipelined(block_count // group, score, lambda i, slot: weigh(few_columns, slot), blend)
 
 
 def heads_by_device(queries, keys, values, kept, dense_class):
@@ -352,6 +381,8 @@
             pltpu.VMEM((block_count, BLOCK, 2 * HD), jnp.bfloat16),
             pltpu.VMEM((2 * BLOCK, block_count * BLOCK), jnp.float32),
             pltpu.VMEM((2 * BLOCK, block_count * BLOCK), jnp.float32),
+            pltpu.VMEM((2 * BLOCK, block_count * BLOCK), jnp.bfloat16),
+            pltpu.VMEM((2 * BLOCK, block_count * BLOCK), jnp.bfloat16),
             pltpu.SemaphoreType.DMA,
         ],
         compiler_params=pltpu.CompilerParams(vmem_limit_bytes=32 * 1024 * 1024),

time: 120 us -> 73.7 us (0.61)
  Pallas kernels: 57.3 us -> 8.1 us
  blocking collectives: 62.3 us -> 65.4 us
    pallas_call x1, Pallas kernels: 49.2 us -> 2.48 us  [pack_heads(): pl.pallas_call(pack_kernel, out_shape=jax.ShapeDtypeStruct((HEADS, count,...]
    all_to_all x2, blocking collectives: 62.3 us -> 65.4 us  [exchange(): return lax.all_to_all(send, axes, split_axis=0, concat_axis=0, tiled=True)]
    pallas_call x1, Pallas kernels: 7.18 us -> 4.7 us  [heads_by_device(): pl.pallas_call(lambda *refs: attend_kernel(axes, *refs), out_shape=jax.Sh...]
where the time goes in v6:
time: 73.7 us; the launch traced here: 73.5 us
  blocking collectives  65.4 us (89%)
  Pallas kernels  8.1 us (11%)
    all_to_all x2, blocking collectives, exchange(): return lax.all_to_all(send, axes, split_axis=0, concat_axis=0, tiled=True)  65.4 us
    pallas_call x1, Pallas kernels, heads_by_device(): pl.pallas_call(lambda *refs: attend_kernel(axes, *refs), out_shape=jax.Sh...  4.7 us
    pallas_call x1, Pallas kernels, pack_heads(): pl.pallas_call(pack_kernel, out_shape=jax.ShapeDtypeStruct((HEADS, count,...  2.48 us

profile of v6, /device:TPU:0, one launch (start us, length us, event | category | flops | bytes accessed | tf_op | source)
XLA Modules:
  0.0 73.5 jit_solution(16958724272223585136)
XLA Ops:
  0.0 2.5 %pack_heads.1 = bf16[16,3,128,128]{3,2,1,0:T(8,128)(2,1)} custom-call(bf16[128,2048]{1,0:T(8,128)(2,1)} %refs_0_.2, bf16[128,2048]{1,0:T(8,128)(2,1)} %refs_1_.2, bf16[128,2048]{1,0:T(8,128)(2,1)} %refs_2_.1), custom_call_target="tpu_custom_call" | custom-call | tf_op jit(solution)/shard_map/pack_heads/pallas_call | solution.py:221
  2.5 0.0 copy-start
  2.5 0.0 copy-start.1
  2.5 43.6 %all_to_all.10.refs_2_ = bf16[16,3,128,128]{3,2,1,0:T(8,128)(2,1)S(1)} all-to-all(bf16[16,3,128,128]{3,2,1,0:T(8,128)(2,1)} %pack_heads.1), channel_id=1, replica_groups=mesh['clip'=2,'seq'=4,'blk'=4] {'seq','blk'}, dimensions={0} | all-to-all | bytes 3145728 | tf_op jit(solution)/shard_map/all_to_all | solution.py:367
  46.1 0.0 copy-done
  46.1 0.0 copy-done.1
  46.1 4.7 %attend_head.1 = bf16[16,128,128]{2,1,0:T(8,128)(2,1)S(1)} custom-call(s32[16,16,16]{2,1,0:T(8,128)S(1)} %copy-done, s32[16]{0:T(128)S(1)} %copy-done.1, bf16[16,3,128,128]{3,2,1,0:T(8,128)(2,1)S(1)} %all_to_all.10.refs_2_), custom_call_target="tpu_custom_call" | custom-call | tf_op jit(solution)/shard_map/attend_head/pallas_call | solution.py:370
  50.8 21.8 %all_to_all.11.held_ref = bf16[16,128,128]{2,1,0:T(8,128)(2,1)S(1)} all-to-all(bf16[16,128,128]{2,1,0:T(8,128)(2,1)S(1)} %attend_head.1), channel_id=1, replica_groups=mesh['clip'=2,'seq'=4,'blk'=4] {'seq','blk'}, dimensions={0} | all-to-all | bytes 1048576 | tf_op jit(solution)/shard_map/all_to_all | solution.py:367
  72.6 0.9 %unpack_heads.1 = bf16[128,2048]{1,0:T(8,128)(2,1)} custom-call(bf16[16,128,128]{2,1,0:T(8,128)(2,1)S(1)} %all_to_all.11.held_ref), custom_call_target="tpu_custom_call" | custom-call | tf_op jit(solution)/shard_map/unpack_heads/pallas_call | solution.py:252
Async XLA Ops:
  2.5 43.6 %copy-start = (s32[16,16,16]{2,1,0:T(8,128)S(1)}, s32[16,16,16]{2,1,0:T(8,128)}, u32[]{:S(2)}) copy-start(s32[16,16,16]{2,1,0:T(8,128)} %refs_0_.3) | copy-start | bytes 49156
  2.5 43.6 %copy-start.1 = (s32[16]{0:T(128)S(1)}, s32[16]{0:T(128)}, u32[]{:S(2)}) copy-start(s32[16]{0:T(128)} %refs_1_.3) | copy-start | bytes 196

commit v7 on v6

--- a/solution.py
+++ b/solution.py
@@ -197,8 +197,16 @@
         ]
         for place, source in enumerate(sources)
     ]
+    share = heads // pieces
     departures = [
-        pltpu.make_async_copy(staged.at[place], out_ref.at[:, place], out_sems.at[place])
+        [
+            pltpu.make_async_copy(
+                staged.at[place, pl.ds(piece * share, share)],
+                out_ref.at[pl.ds(piece * share, share), place],
+                out_sems.at[place, piece],
+            )
+            for piece in range(pieces)
+        ]
         for place in range(count)
     ]
     for copies in arrivals:
@@ -207,11 +215,13 @@
     for place in range(count):
         for copy in arrivals[place]:
             copy.wait()
-        for head in range(heads):
-            staged[place, head] = landed[place, :, head * HD : (head + 1) * HD]
-        departures[place].start()
-    for copy in departures:
-        copy.wait()
+        for piece in range(pieces):
+            for head in range(piece * share, (piece + 1) * share):
+                staged[place, head] = landed[place, :, head * HD : (head + 1) * HD]
+            departures[place][piece].start()
+    for copies in departures:
+        for copy in copies:
+            copy.wait()
 
 
 def pack_heads(*sources):
@@ -227,7 +237,7 @@
             pltpu.VMEM((count, rows, HEADS * HD), jnp.bfloat16),
             pltpu.VMEM((count, HEADS, rows, HD), jnp.bfloat16),
             pltpu.SemaphoreType.DMA((count, pieces)),
-            pltpu.SemaphoreType.DMA((count,)),
+            pltpu.SemaphoreType.DMA((count, pieces)),
         ],
         compiler_params=pltpu.CompilerParams(vmem_limit_bytes=59 * 1024 * 1024),
         name="pack_heads",
@@ -281,12 +291,11 @@
 
 
 def attend_kernel(axes, kept_hbm, class_ref, qkv_ref, out_ref, *scratch):
-    kept_ref, v_all, logits_a, logits_b, weights_a, weights_b, sem = scratch
+    kept_ref, v_all, logits_a, logits_b, weights_a, weights_b, largest_rows, sem = scratch
     logits_slots = (logits_a, logits_b)
     weights_slots = (weights_a, weights_b)
     block_count = qkv_ref.shape[0]
     me = own_place(axes)
-    group = 2
     exponent_scale = math.log2(math.e) / math.sqrt(HD)
     kept_copy = pltpu.make_async_copy(kept_hbm.at[me], kept_ref, sem)
     kept_copy.start()
@@ -298,17 +307,25 @@
             query_rows, key_rows, (((1,), (1,)), ((), ())), preferred_element_type=jnp.float32
         )
 
-    def weigh(columns, slot):
-        logits = logits_slots[slot][:, :columns]
-        largest = jnp.max(logits, axis=-1, keepdims=True)
-        weights = jnp.exp2((logits - largest) * exponent_scale).astype(jnp.bfloat16)
-        weights_slots[slot][:, :columns] = weights
+    def weigh(rows, columns, slot):
+        chunk = 16
+        for row in range(0, rows, chunk):
+            largest = jnp.max(logits_slots[slot][row : row + chunk, :columns], -1, keepdims=True)
+            largest_rows[row : row + chunk, :] = jnp.broadcast_to(largest, (chunk, HD))
+        for row in range(0, rows, chunk):
+            largest = largest_rows[row : row + chunk, :]
+            for column in range(0, columns, HD):
+                logits = logits_slots[slot][row : row + chunk, column : column + HD]
+                weights = jnp.exp2((logits - largest) * exponent_scale).astype(jnp.bfloat16)
+                weights_slots[slot][row : row + chunk, column : column + HD] = weights
 
     def normalized(summed):
         return (summed[:, :HD] / summed[:, HD:]).astype(jnp.bfloat16)
 
     @pl.when(class_ref[me] == 1)
     def _():
+        group = 4
+
         def score(i, slot):
             query_rows = qkv_ref[pl.ds(group * i, group), 0].reshape(group * BLOCK, HD)
             key_rows = qkv_ref[:, 1].reshape(block_count * BLOCK, HD)
@@ -321,14 +338,16 @@
             )
             out_ref[pl.ds(group * i, group)] = out.reshape(group, BLOCK, HD)
 
-        all_columns = block_count * BLOCK
-        pipelined(block_count // group, score, lambda i, slot: weigh(all_columns, slot), blend)
+        def weigh_all(i, slot):
+            weigh(group * BLOCK, block_count * BLOCK, slot)
+
+        pipelined(block_count // group, score, weigh_all, blend)
         kept_copy.wait()
 
     @pl.when(class_ref[me] != 1)
     def _():
         kept_copy.wait()
-        few_columns = block_count // KEEP * LIGHT * BLOCK
+        group = 2
 
         def block_pairs(block):
             kept_blocks = each_light_block(kept_ref, block)
@@ -355,7 +374,10 @@
                     summed += jnp.dot(weights, value_rows, preferred_element_type=jnp.float32)
                 out_ref[block] = normalized(summed)
 
-        pipelined(block_count // group, score, lambda i, slot: weigh(few_columns, slot), blend)
+        def weigh_few(i, slot):
+            weigh(group * BLOCK, block_count // KEEP * LIGHT * BLOCK, slot)
+
+        pipelined(block_count // group, score, weigh_few, blend)
 
 
 def heads_by_device(queries, keys, values, kept, dense_class):
@@ -379,10 +401,11 @@
         scratch_shapes=[
             pltpu.SMEM(kept.shape[1:], jnp.int32),
             pltpu.VMEM((block_count, BLOCK, 2 * HD), jnp.bfloat16),
-            pltpu.VMEM((2 * BLOCK, block_count * BLOCK), jnp.float32),
-            pltpu.VMEM((2 * BLOCK, block_count * BLOCK), jnp.float32),
-            pltpu.VMEM((2 * BLOCK, block_count * BLOCK), jnp.bfloat16),
-            pltpu.VMEM((2 * BLOCK, block_count * BLOCK), jnp.bfloat16),
+            pltpu.VMEM((4 * BLOCK, block_count * BLOCK), jnp.float32),
+            pltpu.VMEM((4 * BLOCK, block_count * BLOCK), jnp.float32),
+            pltpu.VMEM((4 * BLOCK, block_count * BLOCK), jnp.bfloat16),
+            pltpu.VMEM((4 * BLOCK, block_count * BLOCK), jnp.bfloat16),
+            pltpu.VMEM((4 * BLOCK, HD), jnp.float32),
             pltpu.SemaphoreType.DMA,
         ],
         compiler_params=pltpu.CompilerParams(vmem_limit_bytes=32 * 1024 * 1024),

time: 73.7 us -> 72.1 us (0.978)
  blocking collectives: 65.4 us -> 63.3 us
    all_to_all x2, blocking collectives: 65.4 us -> 63.3 us  [exchange(): return lax.all_to_all(send, axes, split_axis=0, concat_axis=0, tiled=True)]
where the time goes in v7:
time: 72.1 us; the launch traced here: 71.8 us
  blocking collectives  63.3 us (88%)
  Pallas kernels  8.51 us (12%)
    all_to_all x2, blocking collectives, exchange(): return lax.all_to_all(send, axes, split_axis=0, concat_axis=0, tiled=True)  63.3 us
    pallas_call x1, Pallas kernels, heads_by_device(): pl.pallas_call(lambda *refs: attend_kernel(axes, *refs), out_shape=jax.Sh...  5.09 us
    pallas_call x1, Pallas kernels, pack_heads(): pl.pallas_call(pack_kernel, out_shape=jax.ShapeDtypeStruct((HEADS, count,...  2.5 us

profile of v7, /device:TPU:0, one launch (start us, length us, event | category | flops | bytes accessed | tf_op | source)
XLA Modules:
  0.0 71.8 jit_solution(4723123176622406438)
XLA Ops:
  0.0 2.5 %pack_heads.1 = bf16[16,3,128,128]{3,2,1,0:T(8,128)(2,1)} custom-call(bf16[128,2048]{1,0:T(8,128)(2,1)} %refs_0_.2, bf16[128,2048]{1,0:T(8,128)(2,1)} %refs_1_.2, bf16[128,2048]{1,0:T(8,128)(2,1)} %refs_2_.1), custom_call_target="tpu_custom_call" | custom-call | tf_op jit(solution)/shard_map/pack_heads/pallas_call | solution.py:231
  2.5 0.0 copy-start
  2.5 0.0 copy-start.1
  2.5 43.6 %all_to_all.10.refs_2_ = bf16[16,3,128,128]{3,2,1,0:T(8,128)(2,1)S(1)} all-to-all(bf16[16,3,128,128]{3,2,1,0:T(8,128)(2,1)} %pack_heads.1), channel_id=1, replica_groups=mesh['clip'=2,'seq'=4,'blk'=4] {'seq','blk'}, dimensions={0} | all-to-all | bytes 3145728 | tf_op jit(solution)/shard_map/all_to_all | solution.py:389
  46.1 0.0 copy-done
  46.1 0.0 copy-done.1
  46.1 5.1 %attend_head.1 = bf16[16,128,128]{2,1,0:T(8,128)(2,1)S(1)} custom-call(s32[16,16,16]{2,1,0:T(8,128)S(1)} %copy-done, s32[16]{0:T(128)S(1)} %copy-done.1, bf16[16,3,128,128]{3,2,1,0:T(8,128)(2,1)S(1)} %all_to_all.10.refs_2_), custom_call_target="tpu_custom_call" | custom-call | tf_op jit(solution)/shard_map/attend_head/pallas_call | solution.py:392
  51.2 19.7 %all_to_all.11.held_ref = bf16[16,128,128]{2,1,0:T(8,128)(2,1)S(1)} all-to-all(bf16[16,128,128]{2,1,0:T(8,128)(2,1)S(1)} %attend_head.1), channel_id=1, replica_groups=mesh['clip'=2,'seq'=4,'blk'=4] {'seq','blk'}, dimensions={0} | all-to-all | bytes 1048576 | tf_op jit(solution)/shard_map/all_to_all | solution.py:389
  70.9 0.9 %unpack_heads.1 = bf16[128,2048]{1,0:T(8,128)(2,1)} custom-call(bf16[16,128,128]{2,1,0:T(8,128)(2,1)S(1)} %all_to_all.11.held_ref), custom_call_target="tpu_custom_call" | custom-call | tf_op jit(solution)/shard_map/unpack_heads/pallas_call | solution.py:262
Async XLA Ops:
  2.5 43.6 %copy-start = (s32[16,16,16]{2,1,0:T(8,128)S(1)}, s32[16,16,16]{2,1,0:T(8,128)}, u32[]{:S(2)}) copy-start(s32[16,16,16]{2,1,0:T(8,128)} %refs_0_.3) | copy-start | bytes 49156
  2.5 43.6 %copy-start.1 = (s32[16]{0:T(128)S(1)}, s32[16]{0:T(128)}, u32[]{:S(2)}) copy-start(s32[16]{0:T(128)} %refs_1_.3) | copy-start | bytes 196

commit v8 on v4

--- a/solution.py
+++ b/solution.py
@@ -205,11 +205,11 @@
         pack_kernel,
         out_shape=jax.ShapeDtypeStruct((HEADS, count, rows, HD), jnp.bfloat16),
         in_specs=[pl.BlockSpec(memory_space=pltpu.HBM)] * count,
-        out_specs=pl.BlockSpec(memory_space=pl.ANY),
+        out_specs=pl.BlockSpec(memory_space=pltpu.VMEM),
         scratch_shapes=[pltpu.SemaphoreType.DMA((HEADS, count))],
-        compiler_params=pltpu.CompilerParams(vmem_limit_bytes=59 * 1024 * 1024),
+        compiler_params=pltpu.CompilerParams(vmem_limit_bytes=4 * 1024 * 1024),
         name="pack_heads",
-    )(*sources)
+    )(*[pltpu.with_memory_space_constraint(source, pltpu.HBM) for source in sources])
 
 
 def unpack_kernel(held_ref, out_ref, sems):
@@ -238,64 +238,80 @@
     )(held)
 
 
-def pipelined(count, score, finish):
+def pipelined(count, prepare, score, weigh, blend):
     score(0, 0)
+    prepare()
+    weigh(0, 0)
+    score(1, 1)
 
     def step(j, carry):
-        score(2 * j + 1, 1)
-        finish(2 * j, 0)
+        blend(2 * j, 0)
+        weigh(2 * j + 1, 1)
         score(2 * j + 2, 0)
-        finish(2 * j + 1, 1)
+        blend(2 * j + 1, 1)
+        weigh(2 * j + 2, 0)
+        score(2 * j + 3, 1)
         return carry
 
     lax.fori_loop(0, count // 2 - 1, step, 0)
-    score(count - 1, 1)
-    finish(count - 2, 0)
-    finish(count - 1, 1)
-
-
-def attend_kernel(axes, kept_hbm, class_ref, qkv_ref, out_ref, kept_ref, v_all, logits_a, logits_b, sem):
+    blend(count - 2, 0)
+    weigh(count - 1, 1)
+    blend(count - 1, 1)
+
+
+def attend_kernel(axes, kept_hbm, class_ref, qkv_ref, out_ref, *scratch):
+    kept_ref, v_all, logits_a, logits_b, weights_a, weights_b, sem = scratch
     logits_slots = (logits_a, logits_b)
+    weights_slots = (weights_a, weights_b)
     block_count = qkv_ref.shape[0]
     me = own_place(axes)
     exponent_scale = math.log2(math.e) / math.sqrt(HD)
     kept_copy = pltpu.make_async_copy(kept_hbm.at[me], kept_ref, sem)
     kept_copy.start()
-    v_all[:, :, :HD] = qkv_ref[:, 2]
-    v_all[:, :, HD:] = jnp.ones((block_count, BLOCK, HD), jnp.bfloat16)
-    kept_copy.wait()
+
+    def set_values():
+        v_all[:, :, :HD] = qkv_ref[:, 2]
+        v_all[:, :, HD:] = jnp.ones((block_count, BLOCK, HD), jnp.bfloat16)
 
     def scores(query_rows, key_rows):
         return lax.dot_general(
             query_rows, key_rows, (((1,), (1,)), ((), ())), preferred_element_type=jnp.float32
         )
 
-    def weigh(logits):
+    def weigh(rows, columns, slot):
+        logits = logits_slots[slot][:rows, :columns]
         largest = jnp.max(logits, axis=-1, keepdims=True)
-        return jnp.exp2((logits - largest) * exponent_scale).astype(jnp.bfloat16)
+        weights = jnp.exp2((logits - largest) * exponent_scale).astype(jnp.bfloat16)
+        weights_slots[slot][:rows, :columns] = weights
 
     def normalized(summed):
         return (summed[:, :HD] / summed[:, HD:]).astype(jnp.bfloat16)
 
     @pl.when(class_ref[me] == 1)
     def _():
-        group = 2
+        group = 4
 
         def score(i, slot):
             query_rows = qkv_ref[pl.ds(group * i, group), 0].reshape(group * BLOCK, HD)
             key_rows = qkv_ref[:, 1].reshape(block_count * BLOCK, HD)
             logits_slots[slot][...] = scores(query_rows, key_rows)
 
-        def finish(i, slot):
+        def blend(i, slot):
             value_rows = v_all[...].reshape(block_count * BLOCK, 2 * HD)
-            weights = weigh(logits_slots[slot][...])
-            out = normalized(jnp.dot(weights, value_rows, preferred_element_type=jnp.float32))
+            out = normalized(
+                jnp.dot(weights_slots[slot][...], value_rows, preferred_element_type=jnp.float32)
+            )
             out_ref[pl.ds(group * i, group)] = out.reshape(group, BLOCK, HD)
 
-        pipelined(block_count // group, score, finish)
+        def weigh_all(i, slot):
+            weigh(group * BLOCK, block_count * BLOCK, slot)
+
+        pipelined(block_count // group, set_values, score, weigh_all, blend)
+        kept_copy.wait()
 
     @pl.when(class_ref[me] != 1)
     def _():
+        kept_copy.wait()
         group = 2
 
         def block_pairs(block):
@@ -311,22 +327,22 @@
                     columns = slice(place * 2 * BLOCK, (place + 1) * 2 * BLOCK)
                     logits_slots[slot][rows, columns] = scores(qkv_ref[block, 0], key_rows)
 
-        def finish(i, slot):
+        def blend(i, slot):
             for member in range(group):
                 block = group * i + member
                 rows = slice(member * BLOCK, (member + 1) * BLOCK)
-                pairs = block_pairs(block)
-                weights = weigh(logits_slots[slot][rows, : 2 * BLOCK * len(pairs)])
                 summed = jnp.zeros((BLOCK, 2 * HD), jnp.float32)
-                for place, (one, other) in enumerate(pairs):
+                for place, (one, other) in enumerate(block_pairs(block)):
                     value_rows = jnp.concatenate([v_all[one], v_all[other]], axis=0)
                     columns = slice(place * 2 * BLOCK, (place + 1) * 2 * BLOCK)
-                    summed += jnp.dot(
-                        weights[:, columns], value_rows, preferred_element_type=jnp.float32
-                    )
+                    weights = weights_slots[slot][rows, columns]
+                    summed += jnp.dot(weights, value_rows, preferred_element_type=jnp.float32)
                 out_ref[block] = normalized(summed)
 
-        pipelined(block_count // group, score, finish)
+        def weigh_few(i, slot):
+            weigh(group * BLOCK, block_count // KEEP * LIGHT * BLOCK, slot)
+
+        pipelined(block_count // group, set_values, score, weigh_few, blend)
 
 
 def heads_by_device(queries, keys, values, kept, dense_class):
@@ -350,8 +366,10 @@
         scratch_shapes=[
             pltpu.SMEM(kept.shape[1:], jnp.int32),
             pltpu.VMEM((block_count, BLOCK, 2 * HD), jnp.bfloat16),
-            pltpu.VMEM((2 * BLOCK, block_count * BLOCK), jnp.float32),
-            pltpu.VMEM((2 * BLOCK, block_count * BLOCK), jnp.float32),
+            pltpu.VMEM((4 * BLOCK, block_count * BLOCK), jnp.float32),
+            pltpu.VMEM((4 * BLOCK, block_count * BLOCK), jnp.float32),
+            pltpu.VMEM((4 * BLOCK, block_count * BLOCK), jnp.bfloat16),
+            pltpu.VMEM((4 * BLOCK, block_count * BLOCK), jnp.bfloat16),
             pltpu.SemaphoreType.DMA,
         ],
         compiler_params=pltpu.CompilerParams(vmem_limit_bytes=32 * 1024 * 1024),

time: 120 us -> 71.8 us (0.60)
  Pallas kernels: 57.3 us -> 8.79 us
    pallas_call x1, Pallas kernels: 49.2 us -> 1.78 us  [pack_heads(): pl.pallas_call(pack_kernel, out_shape=jax.ShapeDtypeStruct((HEADS, count,...]
where the time goes in v8:
time: 71.8 us; the launch traced here: 71.5 us
  blocking collectives  62.7 us (87%)
  Pallas kernels  8.79 us (12%)
    all_to_all x2, blocking collectives, exchange(): return lax.all_to_all(send, axes, split_axis=0, concat_axis=0, tiled=True)  62.7 us
    pallas_call x1, Pallas kernels, heads_by_device(): pl.pallas_call(lambda *refs: attend_kernel(axes, *refs), out_shape=jax.Sh...  6.09 us
    pallas_call x1, Pallas kernels, pack_heads(): pl.pallas_call(pack_kernel, out_shape=jax.ShapeDtypeStruct((HEADS, count,...  1.78 us

profile of v8, /device:TPU:0, one launch (start us, length us, event | category | flops | bytes accessed | tf_op | source)
XLA Modules:
  0.0 71.5 jit_solution(181035266286627569)
XLA Ops:
  0.0 1.8 %pack_heads.1 = bf16[16,3,128,128]{3,2,1,0:T(8,128)(2,1)S(1)} custom-call(bf16[128,2048]{1,0:T(8,128)(2,1)} %refs_0_.2, bf16[128,2048]{1,0:T(8,128)(2,1)} %refs_1_.2, bf16[128,2048]{1,0:T(8,128)(2,1)} %refs_2_.1), custom_call_target="tpu_custom_call" | custom-call | tf_op jit(solution)/shard_map/pack_heads/pallas_call | solution.py:204
  1.8 0.0 copy-start
  1.8 0.0 copy-start.1
  1.8 43.4 %all_to_all.10.refs_2_ = bf16[16,3,128,128]{3,2,1,0:T(8,128)(2,1)S(1)} all-to-all(bf16[16,3,128,128]{3,2,1,0:T(8,128)(2,1)S(1)} %pack_heads.1), channel_id=1, replica_groups=mesh['clip'=2,'seq'=4,'blk'=4] {'seq','blk'}, dimensions={0} | all-to-all | bytes 3145728 | tf_op jit(solution)/shard_map/all_to_all | solution.py:354
  45.2 0.0 copy-done
  45.2 0.0 copy-done.1
  45.2 6.1 %attend_head.1 = bf16[16,128,128]{2,1,0:T(8,128)(2,1)S(1)} custom-call(s32[16,16,16]{2,1,0:T(8,128)S(1)} %copy-done, s32[16]{0:T(128)S(1)} %copy-done.1, bf16[16,3,128,128]{3,2,1,0:T(8,128)(2,1)S(1)} %all_to_all.10.refs_2_), custom_call_target="tpu_custom_call" | custom-call | tf_op jit(solution)/shard_map/attend_head/pallas_call | solution.py:357
  51.3 19.3 %all_to_all.11.held_ref = bf16[16,128,128]{2,1,0:T(8,128)(2,1)S(1)} all-to-all(bf16[16,128,128]{2,1,0:T(8,128)(2,1)S(1)} %attend_head.1), channel_id=1, replica_groups=mesh['clip'=2,'seq'=4,'blk'=4] {'seq','blk'}, dimensions={0} | all-to-all | bytes 1048576 | tf_op jit(solution)/shard_map/all_to_all | solution.py:354
  70.6 0.9 %unpack_heads.1 = bf16[128,2048]{1,0:T(8,128)(2,1)} custom-call(bf16[16,128,128]{2,1,0:T(8,128)(2,1)S(1)} %all_to_all.11.held_ref), custom_call_target="tpu_custom_call" | custom-call | tf_op jit(solution)/shard_map/unpack_heads/pallas_call | solution.py:230
Async XLA Ops:
  1.8 43.4 %copy-start = (s32[16,16,16]{2,1,0:T(8,128)S(1)}, s32[16,16,16]{2,1,0:T(8,128)}, u32[]{:S(2)}) copy-start(s32[16,16,16]{2,1,0:T(8,128)} %refs_0_.3) | copy-start | bytes 49156
  1.8 43.4 %copy-start.1 = (s32[16]{0:T(128)S(1)}, s32[16]{0:T(128)}, u32[]{:S(2)}) copy-start(s32[16]{0:T(128)} %refs_1_.3) | copy-start | bytes 196

commit v9 on v8

--- a/solution.py
+++ b/solution.py
@@ -181,33 +181,49 @@
 
 
 def pack_kernel(*refs):
-    sources, out_ref, sems = refs[:-2], refs[-2], refs[-1]
-    copies = []
-    for head in range(out_ref.shape[0]):
-        for place, source in enumerate(sources):
-            copies.append(
-                pltpu.make_async_copy(
-                    source.at[:, head * HD : (head + 1) * HD],
-                    out_ref.at[head, place],
-                    sems.at[head, place],
-                )
+    sources, (out_ref, landed, sems) = refs[:-3], refs[-3:]
+    heads = out_ref.shape[0]
+    rows = landed.shape[1]
+    pieces = sems.shape[1]
+    piece_rows = rows // pieces
+    arrivals = [
+        [
+            pltpu.make_async_copy(
+                source.at[pl.ds(piece * piece_rows, piece_rows), :],
+                landed.at[place, pl.ds(piece * piece_rows, piece_rows), :],
+                sems.at[place, piece],
             )
-    for copy in copies:
-        copy.start()
-    for copy in copies:
-        copy.wait()
+            for piece in range(pieces)
+        ]
+        for place, source in enumerate(sources)
+    ]
+    for copies in arrivals:
+        for copy in copies:
+            copy.start()
+    for place, copies in enumerate(arrivals):
+        for piece, copy in enumerate(copies):
+            copy.wait()
+            kept_rows = slice(piece * piece_rows, (piece + 1) * piece_rows)
+            for head in range(heads):
+                out_ref[head, place, kept_rows, :] = landed[
+                    place, kept_rows, head * HD : (head + 1) * HD
+                ]
 
 
 def pack_heads(*sources):
     count = len(sources)
     rows = sources[0].shape[0]
+    pieces = 4
     return pl.pallas_call(
         pack_kernel,
         out_shape=jax.ShapeDtypeStruct((HEADS, count, rows, HD), jnp.bfloat16),
         in_specs=[pl.BlockSpec(memory_space=pltpu.HBM)] * count,
         out_specs=pl.BlockSpec(memory_space=pltpu.VMEM),
-        scratch_shapes=[pltpu.SemaphoreType.DMA((HEADS, count))],
-        compiler_params=pltpu.CompilerParams(vmem_limit_bytes=4 * 1024 * 1024),
+        scratch_shapes=[
+            pltpu.VMEM((count, rows, HEADS * HD), jnp.bfloat16),
+            pltpu.SemaphoreType.DMA((count, pieces)),
+        ],
+        compiler_params=pltpu.CompilerParams(vmem_limit_bytes=8 * 1024 * 1024),
         name="pack_heads",
     )(*[pltpu.with_memory_space_constraint(source, pltpu.HBM) for source in sources])
 
@@ -260,7 +276,7 @@
 
 
 def attend_kernel(axes, kept_hbm, class_ref, qkv_ref, out_ref, *scratch):
-    kept_ref, v_all, logits_a, logits_b, weights_a, weights_b, sem = scratch
+    kept_ref, k_turned, v_all, logits_a, logits_b, weights_a, weights_b, sem = scratch
     logits_slots = (logits_a, logits_b)
     weights_slots = (weights_a, weights_b)
     block_count = qkv_ref.shape[0]
@@ -268,15 +284,15 @@
     exponent_scale = math.log2(math.e) / math.sqrt(HD)
     kept_copy = pltpu.make_async_copy(kept_hbm.at[me], kept_ref, sem)
     kept_copy.start()
+    for block in range(block_count):
+        k_turned[:, block * BLOCK : (block + 1) * BLOCK] = qkv_ref[block, 1].T
 
     def set_values():
         v_all[:, :, :HD] = qkv_ref[:, 2]
         v_all[:, :, HD:] = jnp.ones((block_count, BLOCK, HD), jnp.bfloat16)
 
-    def scores(query_rows, key_rows):
-        return lax.dot_general(
-            query_rows, key_rows, (((1,), (1,)), ((), ())), preferred_element_type=jnp.float32
-        )
+    def key_columns(block):
+        return k_turned[:, pl.ds(pl.multiple_of(block * BLOCK, BLOCK), BLOCK)]
 
     def weigh(rows, columns, slot):
         logits = logits_slots[slot][:rows, :columns]
@@ -293,8 +309,9 @@
 
         def score(i, slot):
             query_rows = qkv_ref[pl.ds(group * i, group), 0].reshape(group * BLOCK, HD)
-            key_rows = qkv_ref[:, 1].reshape(block_count * BLOCK, HD)
-            logits_slots[slot][...] = scores(query_rows, key_rows)
+            logits_slots[slot][...] = jnp.dot(
+                query_rows, k_turned[...], preferred_element_type=jnp.float32
+            )
 
         def blend(i, slot):
             value_rows = v_all[...].reshape(block_count * BLOCK, 2 * HD)
@@ -323,9 +340,11 @@
                 block = group * i + member
                 rows = slice(member * BLOCK, (member + 1) * BLOCK)
                 for place, (one, other) in enumerate(block_pairs(block)):
-                    key_rows = jnp.concatenate([qkv_ref[one, 1], qkv_ref[other, 1]], axis=0)
+                    pair = jnp.concatenate([key_columns(one), key_columns(other)], axis=1)
                     columns = slice(place * 2 * BLOCK, (place + 1) * 2 * BLOCK)
-                    logits_slots[slot][rows, columns] = scores(qkv_ref[block, 0], key_rows)
+                    logits_slots[slot][rows, columns] = jnp.dot(
+                        qkv_ref[block, 0], pair, preferred_element_type=jnp.float32
+                    )
 
         def blend(i, slot):
             for member in range(group):
@@ -365,6 +384,7 @@
         out_specs=in_vmem,
         scratch_shapes=[
             pltpu.SMEM(kept.shape[1:], jnp.int32),
+            pltpu.VMEM((HD, block_count * BLOCK), jnp.bfloat16),
             pltpu.VMEM((block_count, BLOCK, 2 * HD), jnp.bfloat16),
             pltpu.VMEM((4 * BLOCK, block_count * BLOCK), jnp.float32),
             pltpu.VMEM((4 * BLOCK, block_count * BLOCK), jnp.float32),

time: 71.8 us -> 71.6 us (level)
  Pallas kernels: 8.79 us -> 7.92 us
    all_to_all x2, blocking collectives: 62.7 us -> 63.4 us  [exchange(): return lax.all_to_all(send, axes, split_axis=0, concat_axis=0, tiled=True)]
where the time goes in v9:
time: 71.6 us; the launch traced here: 71.4 us
  blocking collectives  63.4 us (89%)
  Pallas kernels  7.92 us (11%)
    all_to_all x2, blocking collectives, exchange(): return lax.all_to_all(send, axes, split_axis=0, concat_axis=0, tiled=True)  63.4 us
    pallas_call x1, Pallas kernels, heads_by_device(): pl.pallas_call(lambda *refs: attend_kernel(axes, *refs), out_shape=jax.Sh...  5.44 us
    pallas_call x1, Pallas kernels, pack_heads(): pl.pallas_call(pack_kernel, out_shape=jax.ShapeDtypeStruct((HEADS, count,...  1.56 us

profile of v9, /device:TPU:0, one launch (start us, length us, event | category | flops | bytes accessed | tf_op | source)
XLA Modules:
  0.0 71.4 jit_solution(4083668846494585638)
XLA Ops:
  0.0 1.6 %pack_heads.1 = bf16[16,3,128,128]{3,2,1,0:T(8,128)(2,1)S(1)} custom-call(bf16[128,2048]{1,0:T(8,128)(2,1)} %refs_0_.2, bf16[128,2048]{1,0:T(8,128)(2,1)} %refs_1_.2, bf16[128,2048]{1,0:T(8,128)(2,1)} %refs_2_.1), custom_call_target="tpu_custom_call" | custom-call | tf_op jit(solution)/shard_map/pack_heads/pallas_call | solution.py:217
  1.6 0.0 copy-start
  1.6 0.0 copy-start.1
  1.6 43.4 %all_to_all.10.refs_2_ = bf16[16,3,128,128]{3,2,1,0:T(8,128)(2,1)S(1)} all-to-all(bf16[16,3,128,128]{3,2,1,0:T(8,128)(2,1)S(1)} %pack_heads.1), channel_id=1, replica_groups=mesh['clip'=2,'seq'=4,'blk'=4] {'seq','blk'}, dimensions={0} | all-to-all | bytes 3145728 | tf_op jit(solution)/shard_map/all_to_all | solution.py:373
  45.0 0.0 copy-done
  45.0 0.0 copy-done.1
  45.0 5.4 %attend_head.1 = bf16[16,128,128]{2,1,0:T(8,128)(2,1)S(1)} custom-call(s32[16,16,16]{2,1,0:T(8,128)S(1)} %copy-done, s32[16]{0:T(128)S(1)} %copy-done.1, bf16[16,3,128,128]{3,2,1,0:T(8,128)(2,1)S(1)} %all_to_all.10.refs_2_), custom_call_target="tpu_custom_call" | custom-call | tf_op jit(solution)/shard_map/attend_head/pallas_call | solution.py:376
  50.4 20.1 %all_to_all.11.held_ref = bf16[16,128,128]{2,1,0:T(8,128)(2,1)S(1)} all-to-all(bf16[16,128,128]{2,1,0:T(8,128)(2,1)S(1)} %attend_head.1), channel_id=1, replica_groups=mesh['clip'=2,'seq'=4,'blk'=4] {'seq','blk'}, dimensions={0} | all-to-all | bytes 1048576 | tf_op jit(solution)/shard_map/all_to_all | solution.py:373
  70.5 0.9 %unpack_heads.1 = bf16[128,2048]{1,0:T(8,128)(2,1)} custom-call(bf16[16,128,128]{2,1,0:T(8,128)(2,1)S(1)} %all_to_all.11.held_ref), custom_call_target="tpu_custom_call" | custom-call | tf_op jit(solution)/shard_map/unpack_heads/pallas_call | solution.py:246
Async XLA Ops:
  1.6 43.4 %copy-start = (s32[16,16,16]{2,1,0:T(8,128)S(1)}, s32[16,16,16]{2,1,0:T(8,128)}, u32[]{:S(2)}) copy-start(s32[16,16,16]{2,1,0:T(8,128)} %refs_0_.3) | copy-start | bytes 49156
  1.6 43.4 %copy-start.1 = (s32[16]{0:T(128)S(1)}, s32[16]{0:T(128)}, u32[]{:S(2)}) copy-start(s32[16]{0:T(128)} %refs_1_.3) | copy-start | bytes 196

commit v10 on v9

--- a/solution.py
+++ b/solution.py
@@ -276,7 +276,7 @@
 
 
 def attend_kernel(axes, kept_hbm, class_ref, qkv_ref, out_ref, *scratch):
-    kept_ref, k_turned, v_all, logits_a, logits_b, weights_a, weights_b, sem = scratch
+    kept_ref, v_all, logits_a, logits_b, weights_a, weights_b, sem = scratch
     logits_slots = (logits_a, logits_b)
     weights_slots = (weights_a, weights_b)
     block_count = qkv_ref.shape[0]
@@ -284,15 +284,15 @@
     exponent_scale = math.log2(math.e) / math.sqrt(HD)
     kept_copy = pltpu.make_async_copy(kept_hbm.at[me], kept_ref, sem)
     kept_copy.start()
-    for block in range(block_count):
-        k_turned[:, block * BLOCK : (block + 1) * BLOCK] = qkv_ref[block, 1].T
 
     def set_values():
         v_all[:, :, :HD] = qkv_ref[:, 2]
         v_all[:, :, HD:] = jnp.ones((block_count, BLOCK, HD), jnp.bfloat16)
 
-    def key_columns(block):
-        return k_turned[:, pl.ds(pl.multiple_of(block * BLOCK, BLOCK), BLOCK)]
+    def scores(query_rows, key_rows):
+        return lax.dot_general(
+            query_rows, key_rows, (((1,), (1,)), ((), ())), preferred_element_type=jnp.float32
+        )
 
     def weigh(rows, columns, slot):
         logits = logits_slots[slot][:rows, :columns]
@@ -305,25 +305,35 @@
 
     @pl.when(class_ref[me] == 1)
     def _():
-        group = 4
-
-        def score(i, slot):
-            query_rows = qkv_ref[pl.ds(group * i, group), 0].reshape(group * BLOCK, HD)
-            logits_slots[slot][...] = jnp.dot(
-                query_rows, k_turned[...], preferred_element_type=jnp.float32
-            )
-
-        def blend(i, slot):
+        sizes = [2] + [4] * (block_count // 4 - 1) + [2]
+        starts = [sum(sizes[:i]) for i in range(len(sizes))]
+
+        def score(i):
+            rows = sizes[i] * BLOCK
+            query_rows = qkv_ref[starts[i] : starts[i] + sizes[i], 0].reshape(rows, HD)
+            key_rows = qkv_ref[:, 1].reshape(block_count * BLOCK, HD)
+            logits_slots[i % 2][:rows, :] = scores(query_rows, key_rows)
+
+        def weigh_all(i):
+            weigh(sizes[i] * BLOCK, block_count * BLOCK, i % 2)
+
+        def blend(i):
+            rows = sizes[i] * BLOCK
             value_rows = v_all[...].reshape(block_count * BLOCK, 2 * HD)
-            out = normalized(
-                jnp.dot(weights_slots[slot][...], value_rows, preferred_element_type=jnp.float32)
-            )
-            out_ref[pl.ds(group * i, group)] = out.reshape(group, BLOCK, HD)
-
-        def weigh_all(i, slot):
-            weigh(group * BLOCK, block_count * BLOCK, slot)
-
-        pipelined(block_count // group, set_values, score, weigh_all, blend)
+            weights = weights_slots[i % 2][:rows, :]
+            out = normalized(jnp.dot(weights, value_rows, preferred_element_type=jnp.float32))
+            out_ref[starts[i] : starts[i] + sizes[i]] = out.reshape(sizes[i], BLOCK, HD)
+
+        score(0)
+        set_values()
+        weigh_all(0)
+        score(1)
+        for i in range(1, len(sizes)):
+            blend(i - 1)
+            weigh_all(i)
+            if i + 1 < len(sizes):
+                score(i + 1)
+        blend(len(sizes) - 1)
         kept_copy.wait()
 
     @pl.when(class_ref[me] != 1)
@@ -340,11 +350,9 @@
                 block = group * i + member
                 rows = slice(member * BLOCK, (member + 1) * BLOCK)
                 for place, (one, other) in enumerate(block_pairs(block)):
-                    pair = jnp.concatenate([key_columns(one), key_columns(other)], axis=1)
+                    key_rows = jnp.concatenate([qkv_ref[one, 1], qkv_ref[other, 1]], axis=0)
                     columns = slice(place * 2 * BLOCK, (place + 1) * 2 * BLOCK)
-                    logits_slots[slot][rows, columns] = jnp.dot(
-                        qkv_ref[block, 0], pair, preferred_element_type=jnp.float32
-                    )
+                    logits_slots[slot][rows, columns] = scores(qkv_ref[block, 0], key_rows)
 
         def blend(i, slot):
             for member in range(group):
@@ -384,7 +392,6 @@
         out_specs=in_vmem,
         scratch_shapes=[
             pltpu.SMEM(kept.shape[1:], jnp.int32),
-            pltpu.VMEM((HD, block_count * BLOCK), jnp.bfloat16),
             pltpu.VMEM((block_count, BLOCK, 2 * HD), jnp.bfloat16),
             pltpu.VMEM((4 * BLOCK, block_count * BLOCK), jnp.float32),
             pltpu.VMEM((4 * BLOCK, block_count * BLOCK), jnp.float32),

time: 71.6 us -> 70.8 us (0.989)
    all_to_all x2, blocking collectives: 63.4 us -> 62.7 us  [exchange(): return lax.all_to_all(send, axes, split_axis=0, concat_axis=0, tiled=True)]
where the time goes in v10:
time: 70.8 us; the launch traced here: 70.1 us
  blocking collectives  62.7 us (89%)
  Pallas kernels  7.38 us (10%)
    all_to_all x2, blocking collectives, exchange(): return lax.all_to_all(send, axes, split_axis=0, concat_axis=0, tiled=True)  62.7 us
    pallas_call x1, Pallas kernels, heads_by_device(): pl.pallas_call(lambda *refs: attend_kernel(axes, *refs), out_shape=jax.Sh...  4.9 us
    pallas_call x1, Pallas kernels, pack_heads(): pl.pallas_call(pack_kernel, out_shape=jax.ShapeDtypeStruct((HEADS, count,...  1.56 us

profile of v10, /device:TPU:0, one launch (start us, length us, event | category | flops | bytes accessed | tf_op | source)
XLA Modules:
  0.0 70.1 jit_solution(14872791385234181307)
XLA Ops:
  0.0 1.6 %pack_heads.1 = bf16[16,3,128,128]{3,2,1,0:T(8,128)(2,1)S(1)} custom-call(bf16[128,2048]{1,0:T(8,128)(2,1)} %refs_0_.2, bf16[128,2048]{1,0:T(8,128)(2,1)} %refs_1_.2, bf16[128,2048]{1,0:T(8,128)(2,1)} %refs_2_.1), custom_call_target="tpu_custom_call" | custom-call | tf_op jit(solution)/shard_map/pack_heads/pallas_call | solution.py:217
  1.6 0.0 copy-start
  1.6 0.0 copy-start.1
  1.6 43.4 %all_to_all.10.refs_2_ = bf16[16,3,128,128]{3,2,1,0:T(8,128)(2,1)S(1)} all-to-all(bf16[16,3,128,128]{3,2,1,0:T(8,128)(2,1)S(1)} %pack_heads.1), channel_id=1, replica_groups=mesh['clip'=2,'seq'=4,'blk'=4] {'seq','blk'}, dimensions={0} | all-to-all | bytes 3145728 | tf_op jit(solution)/shard_map/all_to_all | solution.py:381
  45.0 0.0 copy-done
  45.0 0.0 copy-done.1
  45.0 4.9 %attend_head.1 = bf16[16,128,128]{2,1,0:T(8,128)(2,1)S(1)} custom-call(s32[16,16,16]{2,1,0:T(8,128)S(1)} %copy-done, s32[16]{0:T(128)S(1)} %copy-done.1, bf16[16,3,128,128]{3,2,1,0:T(8,128)(2,1)S(1)} %all_to_all.10.refs_2_), custom_call_target="tpu_custom_call" | custom-call | tf_op jit(solution)/shard_map/attend_head/pallas_call | solution.py:384
  49.9 19.3 %all_to_all.11.held_ref = bf16[16,128,128]{2,1,0:T(8,128)(2,1)S(1)} all-to-all(bf16[16,128,128]{2,1,0:T(8,128)(2,1)S(1)} %attend_head.1), channel_id=1, replica_groups=mesh['clip'=2,'seq'=4,'blk'=4] {'seq','blk'}, dimensions={0} | all-to-all | bytes 1048576 | tf_op jit(solution)/shard_map/all_to_all | solution.py:381
  69.2 0.9 %unpack_heads.1 = bf16[128,2048]{1,0:T(8,128)(2,1)} custom-call(bf16[16,128,128]{2,1,0:T(8,128)(2,1)S(1)} %all_to_all.11.held_ref), custom_call_target="tpu_custom_call" | custom-call | tf_op jit(solution)/shard_map/unpack_heads/pallas_call | solution.py:246
Async XLA Ops:
  1.6 43.4 %copy-start = (s32[16,16,16]{2,1,0:T(8,128)S(1)}, s32[16,16,16]{2,1,0:T(8,128)}, u32[]{:S(2)}) copy-start(s32[16,16,16]{2,1,0:T(8,128)} %refs_0_.3) | copy-start | bytes 49156
  1.6 43.4 %copy-start.1 = (s32[16]{0:T(128)S(1)}, s32[16]{0:T(128)}, u32[]{:S(2)}) copy-start(s32[16]{0:T(128)} %refs_1_.3) | copy-start | bytes 196

commit v11 on v10

--- a/solution.py
+++ b/solution.py
@@ -228,17 +228,24 @@
     )(*[pltpu.with_memory_space_constraint(source, pltpu.HBM) for source in sources])
 
 
-def unpack_kernel(held_ref, out_ref, sems):
-    copies = [
-        pltpu.make_async_copy(
-            held_ref.at[head], out_ref.at[:, head * HD : (head + 1) * HD], sems.at[head]
-        )
-        for head in range(held_ref.shape[0])
-    ]
-    for copy in copies:
-        copy.start()
-    for copy in copies:
-        copy.wait()
+def unpack_kernel(held_ref, out_ref, turned, sems):
+    heads = held_ref.shape[0]
+    pieces = sems.shape[0]
+    piece_rows = turned.shape[0] // pieces
+    departures = []
+    for piece in range(pieces):
+        rows = slice(piece * piece_rows, (piece + 1) * piece_rows)
+        for head in range(heads):
+            turned[rows, head * HD : (head + 1) * HD] = held_ref[head, rows, :]
+        departure = pltpu.make_async_copy(
+            turned.at[pl.ds(piece * piece_rows, piece_rows), :],
+            out_ref.at[pl.ds(piece * piece_rows, piece_rows), :],
+            sems.at[piece],
+        )
+        departure.start()
+        departures.append(departure)
+    for departure in departures:
+        departure.wait()
 
 
 def unpack_heads(held):
@@ -246,17 +253,19 @@
     return pl.pallas_call(
         unpack_kernel,
         out_shape=jax.ShapeDtypeStruct((rows, heads * depth), jnp.bfloat16),
-        in_specs=[pl.BlockSpec(memory_space=pl.ANY)],
+        in_specs=[pl.BlockSpec(memory_space=pltpu.VMEM)],
         out_specs=pl.BlockSpec(memory_space=pltpu.HBM),
-        scratch_shapes=[pltpu.SemaphoreType.DMA((heads,))],
-        compiler_params=pltpu.CompilerParams(vmem_limit_bytes=4 * 1024 * 1024),
+        scratch_shapes=[
+            pltpu.VMEM((rows, heads * depth), jnp.bfloat16),
+            pltpu.SemaphoreType.DMA((4,)),
+        ],
+        compiler_params=pltpu.CompilerParams(vmem_limit_bytes=8 * 1024 * 1024),
         name="unpack_heads",
     )(held)
 
 
-def pipelined(count, prepare, score, weigh, blend):
+def pipelined(count, score, weigh, blend):
     score(0, 0)
-    prepare()
     weigh(0, 0)
     score(1, 1)
 
@@ -275,19 +284,20 @@
     blend(count - 1, 1)
 
 
-def attend_kernel(axes, kept_hbm, class_ref, qkv_ref, out_ref, *scratch):
-    kept_ref, v_all, logits_a, logits_b, weights_a, weights_b, sem = scratch
+def attend_kernel(axes, kept_hbm, class_hbm, qkv_ref, out_ref, *scratch):
+    kept_ref, class_ref, v_all, logits_a, logits_b, weights_a, weights_b, kept_sem, class_sem = scratch
     logits_slots = (logits_a, logits_b)
     weights_slots = (weights_a, weights_b)
     block_count = qkv_ref.shape[0]
     me = own_place(axes)
     exponent_scale = math.log2(math.e) / math.sqrt(HD)
-    kept_copy = pltpu.make_async_copy(kept_hbm.at[me], kept_ref, sem)
+    kept_copy = pltpu.make_async_copy(kept_hbm.at[me], kept_ref, kept_sem)
+    class_copy = pltpu.make_async_copy(class_hbm, class_ref, class_sem)
+    class_copy.start()
     kept_copy.start()
-
-    def set_values():
-        v_all[:, :, :HD] = qkv_ref[:, 2]
-        v_all[:, :, HD:] = jnp.ones((block_count, BLOCK, HD), jnp.bfloat16)
+    v_all[:, :, :HD] = qkv_ref[:, 2]
+    v_all[:, :, HD:] = jnp.ones((block_count, BLOCK, HD), jnp.bfloat16)
+    class_copy.wait()
 
     def scores(query_rows, key_rows):
         return lax.dot_general(
@@ -305,7 +315,7 @@
 
     @pl.when(class_ref[me] == 1)
     def _():
-        sizes = [2] + [4] * (block_count // 4 - 1) + [2]
+        sizes = [2, block_count // 2 - 2, block_count // 2 - 2, 2]
         starts = [sum(sizes[:i]) for i in range(len(sizes))]
 
         def score(i):
@@ -325,7 +335,6 @@
             out_ref[starts[i] : starts[i] + sizes[i]] = out.reshape(sizes[i], BLOCK, HD)
 
         score(0)
-        set_values()
         weigh_all(0)
         score(1)
         for i in range(1, len(sizes)):
@@ -369,7 +378,7 @@
         def weigh_few(i, slot):
             weigh(group * BLOCK, block_count // KEEP * LIGHT * BLOCK, slot)
 
-        pipelined(block_count // group, set_values, score, weigh_few, blend)
+        pipelined(block_count // group, score, weigh_few, blend)
 
 
 def heads_by_device(queries, keys, values, kept, dense_class):
@@ -381,25 +390,28 @@
         return lax.all_to_all(send, axes, split_axis=0, concat_axis=0, tiled=True)
 
     held = exchange(pack_heads(queries, keys, values))
+    stage_rows = (block_count // 2 - 2) * BLOCK
     attended = pl.pallas_call(
         lambda *refs: attend_kernel(axes, *refs),
         out_shape=jax.ShapeDtypeStruct((block_count, BLOCK, HD), jnp.bfloat16),
         in_specs=[
             pl.BlockSpec(memory_space=pl.ANY),
-            pl.BlockSpec(memory_space=pltpu.SMEM),
+            pl.BlockSpec(memory_space=pl.ANY),
             in_vmem,
         ],
         out_specs=in_vmem,
         scratch_shapes=[
             pltpu.SMEM(kept.shape[1:], jnp.int32),
+            pltpu.SMEM(dense_class.shape, jnp.int32),
             pltpu.VMEM((block_count, BLOCK, 2 * HD), jnp.bfloat16),
-            pltpu.VMEM((4 * BLOCK, block_count * BLOCK), jnp.float32),
-            pltpu.VMEM((4 * BLOCK, block_count * BLOCK), jnp.float32),
-            pltpu.VMEM((4 * BLOCK, block_count * BLOCK), jnp.bfloat16),
-            pltpu.VMEM((4 * BLOCK, block_count * BLOCK), jnp.bfloat16),
+            pltpu.VMEM((stage_rows, block_count * BLOCK), jnp.float32),
+            pltpu.VMEM((stage_rows, block_count * BLOCK), jnp.float32),
+            pltpu.VMEM((stage_rows, block_count * BLOCK), jnp.bfloat16),
+            pltpu.VMEM((stage_rows, block_count * BLOCK), jnp.bfloat16),
+            pltpu.SemaphoreType.DMA,
             pltpu.SemaphoreType.DMA,
         ],
-        compiler_params=pltpu.CompilerParams(vmem_limit_bytes=32 * 1024 * 1024),
+        compiler_params=pltpu.CompilerParams(vmem_limit_bytes=40 * 1024 * 1024),
         name="attend_head",
     )(kept, dense_class, held)
     return unpack_heads(exchange(attended))

time: 70.8 us -> 70.4 us (level); the launches traced: 70.1 us -> 70.5 us
  blocking collectives: 62.7 us -> 63.7 us
    all_to_all x2, blocking collectives: 62.7 us -> 63.7 us  [exchange(): return lax.all_to_all(send, axes, split_axis=0, concat_axis=0, tiled=True)]
where the time goes in v11:
time: 70.4 us; the launch traced here: 70.5 us
  blocking collectives  63.7 us (90%)
  Pallas kernels  6.72 us (10%)
    all_to_all x2, blocking collectives, exchange(): return lax.all_to_all(send, axes, split_axis=0, concat_axis=0, tiled=True)  63.7 us
    pallas_call x1, Pallas kernels, heads_by_device(): pl.pallas_call(lambda *refs: attend_kernel(axes, *refs), out_shape=jax.Sh...  4.32 us
    pallas_call x1, Pallas kernels, pack_heads(): pl.pallas_call(pack_kernel, out_shape=jax.ShapeDtypeStruct((HEADS, count,...  1.56 us

profile of v11, /device:TPU:0, one launch (start us, length us, event | category | flops | bytes accessed | tf_op | source)
XLA Modules:
  0.0 70.5 jit_solution(4232250585647342046)
XLA Ops:
  0.0 1.6 %pack_heads.1 = bf16[16,3,128,128]{3,2,1,0:T(8,128)(2,1)S(1)} custom-call(bf16[128,2048]{1,0:T(8,128)(2,1)} %refs_0_.2, bf16[128,2048]{1,0:T(8,128)(2,1)} %refs_1_.2, bf16[128,2048]{1,0:T(8,128)(2,1)} %refs_2_.1), custom_call_target="tpu_custom_call" | custom-call | tf_op jit(solution)/shard_map/pack_heads/pallas_call | solution.py:217
  1.6 0.0 copy-start
  1.6 0.0 copy-start.1
  1.6 43.4 %all_to_all.10.refs_2_ = bf16[16,3,128,128]{3,2,1,0:T(8,128)(2,1)S(1)} all-to-all(bf16[16,3,128,128]{3,2,1,0:T(8,128)(2,1)S(1)} %pack_heads.1), channel_id=1, replica_groups=mesh['clip'=2,'seq'=4,'blk'=4] {'seq','blk'}, dimensions={0} | all-to-all | bytes 3145728 | tf_op jit(solution)/shard_map/all_to_all | solution.py:390
  45.0 0.0 copy-done
  45.0 0.0 copy-done.1
  45.0 4.3 %attend_head.1 = bf16[16,128,128]{2,1,0:T(8,128)(2,1)S(1)} custom-call(s32[16,16,16]{2,1,0:T(8,128)S(1)} %copy-done, s32[16]{0:T(128)S(1)} %copy-done.1, bf16[16,3,128,128]{3,2,1,0:T(8,128)(2,1)S(1)} %all_to_all.10.refs_2_), custom_call_target="tpu_custom_call" | custom-call | tf_op jit(solution)/shard_map/attend_head/pallas_call | solution.py:394
  49.3 20.4 %all_to_all.11.held_ref = bf16[16,128,128]{2,1,0:T(8,128)(2,1)S(1)} all-to-all(bf16[16,128,128]{2,1,0:T(8,128)(2,1)S(1)} %attend_head.1), channel_id=1, replica_groups=mesh['clip'=2,'seq'=4,'blk'=4] {'seq','blk'}, dimensions={0} | all-to-all | bytes 1048576 | tf_op jit(solution)/shard_map/all_to_all | solution.py:390
  69.7 0.8 %unpack_heads.1 = bf16[128,2048]{1,0:T(8,128)(2,1)} custom-call(bf16[16,128,128]{2,1,0:T(8,128)(2,1)S(1)} %all_to_all.11.held_ref), custom_call_target="tpu_custom_call" | custom-call | tf_op jit(solution)/shard_map/unpack_heads/pallas_call | solution.py:253
Async XLA Ops:
  1.6 43.4 %copy-start = (s32[16,16,16]{2,1,0:T(8,128)S(1)}, s32[16,16,16]{2,1,0:T(8,128)}, u32[]{:S(2)}) copy-start(s32[16,16,16]{2,1,0:T(8,128)} %refs_0_.3) | copy-start | bytes 49156
  1.6 43.4 %copy-start.1 = (s32[16]{0:T(128)S(1)}, s32[16]{0:T(128)}, u32[]{:S(2)}) copy-start(s32[16]{0:T(128)} %refs_1_.3) | copy-start | bytes 196

commit v12 on v11

--- a/solution.py
+++ b/solution.py
@@ -291,7 +291,7 @@
     block_count = qkv_ref.shape[0]
     me = own_place(axes)
     exponent_scale = math.log2(math.e) / math.sqrt(HD)
-    kept_copy = pltpu.make_async_copy(kept_hbm.at[me], kept_ref, kept_sem)
+    kept_copy = pltpu.make_async_copy(kept_hbm, kept_ref, kept_sem)
     class_copy = pltpu.make_async_copy(class_hbm, class_ref, class_sem)
     class_copy.start()
     kept_copy.start()
@@ -315,7 +315,7 @@
 
     @pl.when(class_ref[me] == 1)
     def _():
-        sizes = [2, block_count // 2 - 2, block_count // 2 - 2, 2]
+        sizes = [2] + [4] * (block_count // 4 - 1) + [2]
         starts = [sum(sizes[:i]) for i in range(len(sizes))]
 
         def score(i):
@@ -390,7 +390,8 @@
         return lax.all_to_all(send, axes, split_axis=0, concat_axis=0, tiled=True)
 
     held = exchange(pack_heads(queries, keys, values))
-    stage_rows = (block_count // 2 - 2) * BLOCK
+    own_kept = lax.dynamic_index_in_dim(kept, own_place(axes), 0, keepdims=False)
+    stage_rows = 4 * BLOCK
     attended = pl.pallas_call(
         lambda *refs: attend_kernel(axes, *refs),
         out_shape=jax.ShapeDtypeStruct((block_count, BLOCK, HD), jnp.bfloat16),
@@ -413,7 +414,7 @@
         ],
         compiler_params=pltpu.CompilerParams(vmem_limit_bytes=40 * 1024 * 1024),
         name="attend_head",
-    )(kept, dense_class, held)
+    )(own_kept, dense_class, held)
     return unpack_heads(exchange(attended))
 
 

time: 70.4 us -> 71.8 us (1.020)
  blocking collectives: 63.7 us -> 23.4 us
  waiting for transfers between devices: 0 us -> 31.9 us
  starting transfers between devices: 0 us -> 7.37 us
  Pallas kernels: 6.72 us -> 9.2 us
    all_to_all x2 -> x1, blocking collectives: 63.7 us -> 23.4 us  [exchange(): return lax.all_to_all(send, axes, split_axis=0, concat_axis=0, tiled=True)]
    all_to_all x0 -> x1, waiting for transfers between devices: none -> 31.9 us  [exchange(): return lax.all_to_all(send, axes, split_axis=0, concat_axis=0, tiled=True)]
    all_to_all x0 -> x1, starting transfers between devices: none -> 7.37 us  [exchange(): return lax.all_to_all(send, axes, split_axis=0, concat_axis=0, tiled=True)]
    pallas_call x1, Pallas kernels: 4.32 us -> 5.61 us  [heads_by_device(): pl.pallas_call(lambda *refs: attend_kernel(axes, *refs), out_shape=jax.Sh...]
    pallas_call x1, Pallas kernels: 1.56 us -> 2.76 us  [pack_heads(): pl.pallas_call(pack_kernel, out_shape=jax.ShapeDtypeStruct((HEADS, count,...]
  transfers between devices with their start and end apart: 0 -> 1, of which waited for: 0 -> 1; matrix products, arithmetic and copies ran while one was open for 0% -> 0% of each run, Pallas kernels for 0% -> 0%
where the time goes in v12:
time: 71.8 us; the launch traced here: 72 us
  waiting for transfers between devices  31.9 us (44%)
  blocking collectives  23.4 us (33%)
  Pallas kernels  9.2 us (13%)
  starting transfers between devices  7.37 us (10%)
    all_to_all x1, waiting for transfers between devices, exchange(): return lax.all_to_all(send, axes, split_axis=0, concat_axis=0, tiled=True)  31.9 us
    all_to_all x1, blocking collectives, exchange(): return lax.all_to_all(send, axes, split_axis=0, concat_axis=0, tiled=True)  23.4 us
    all_to_all x1, starting transfers between devices, exchange(): return lax.all_to_all(send, axes, split_axis=0, concat_axis=0, tiled=True)  7.37 us
    pallas_call x1, Pallas kernels, heads_by_device(): pl.pallas_call(lambda *refs: attend_kernel(axes, *refs), out_shape=jax.Sh...  5.61 us
    pallas_call x1, Pallas kernels, pack_heads(): pl.pallas_call(pack_kernel, out_shape=jax.ShapeDtypeStruct((HEADS, count,...  2.76 us
  transfers between devices with their start and end apart: 1, of which 1 were waited for; matrix products, arithmetic and copies ran while one was open for 0% of the time, Pallas kernels for 0%

profile of v12, /device:TPU:0, one launch (start us, length us, event | category | flops | bytes accessed | tf_op | source)
XLA Modules:
  0.0 72.0 jit_solution(14614061805917298565)
XLA Ops:
  0.0 0.0 copy-start
  0.0 2.8 %pack_heads.1 = bf16[16,3,128,128]{3,2,1,0:T(8,128)(2,1)} custom-call(bf16[128,2048]{1,0:T(8,128)(2,1)} %refs_0_.1, bf16[128,2048]{1,0:T(8,128)(2,1)} %refs_1_.2, bf16[128,2048]{1,0:T(8,128)(2,1)} %refs_2_.1), custom_call_target="tpu_custom_call" | custom-call | tf_op jit(solution)/shard_map/pack_heads/pallas_call | solution.py:217
  2.8 0.0 copy-start.1
  2.8 7.4 %all-to-all-start = ((bf16[16,3,128,128]{3,2,1,0:T(8,128)(2,1)}), bf16[16,3,128,128]{3,2,1,0:T(8,128)(2,1)S(1)}, u32[]{:S(2)}, u32[]{:S(2)}) async-start(bf16[16,3,128,128]{3,2,1,0:T(8,128)(2,1)} %pack_heads.1), calls=%async_computation | async-start | bytes 3145728 | tf_op jit(solution)/shard_map/all_to_all | solution.py:390
  10.2 0.0 copy-done
  10.2 31.9 %all-to-all-done.refs_2_ = bf16[16,3,128,128]{3,2,1,0:T(8,128)(2,1)S(1)} async-done(((bf16[16,3,128,128]{3,2,1,0:T(8,128)(2,1)}), bf16[16,3,128,128]{3,2,1,0:T(8,128)(2,1)S(1)}, u32[]{:S(2)}, u32[]{:S(2)}) %all-to-all-start) | async-done | bytes 1572896 | tf_op jit(solution)/shard_map/all_to_all | solution.py:390
  42.1 0.0 copy-done.1
  42.1 5.6 %attend_head.1 = bf16[16,128,128]{2,1,0:T(8,128)(2,1)S(1)} custom-call(s32[16,16]{1,0:T(8,128)S(1)} %dynamic-slice_bitcast_fusion.refs_0_, s32[16]{0:T(128)S(1)} %copy-done.1, bf16[16,3,128,128]{3,2,1,0:T(8,128)(2,1)S(1)} %all-to-all-done.refs_2_), custom_call_target="tpu_custom_call" | custom-call | tf_op jit(solution)/shard_map/attend_head/pallas_call | solution.py:395
  47.8 23.4 %all_to_all.10.held_ref = bf16[16,128,128]{2,1,0:T(8,128)(2,1)S(1)} all-to-all(bf16[16,128,128]{2,1,0:T(8,128)(2,1)S(1)} %attend_head.1), channel_id=1, replica_groups=mesh['clip'=2,'seq'=4,'blk'=4] {'seq','blk'}, dimensions={0} | all-to-all | bytes 1048576 | tf_op jit(solution)/shard_map/all_to_all | solution.py:390
  71.1 0.8 %unpack_heads.1 = bf16[128,2048]{1,0:T(8,128)(2,1)} custom-call(bf16[16,128,128]{2,1,0:T(8,128)(2,1)S(1)} %all_to_all.10.held_ref), custom_call_target="tpu_custom_call" | custom-call | tf_op jit(solution)/shard_map/unpack_heads/pallas_call | solution.py:253
  (1 shorter events, 0.0 us)
Async XLA Ops:
  0.0 10.2 %copy-start = (s32[16,16,16]{2,1,0:T(8,128)S(1)}, s32[16,16,16]{2,1,0:T(8,128)}, u32[]{:S(2)}) copy-start(s32[16,16,16]{2,1,0:T(8,128)} %param.8) | copy-start | bytes 49156
  2.8 39.4 %copy-start.1 = (s32[16]{0:T(128)S(1)}, s32[16]{0:T(128)}, u32[]{:S(2)}) copy-start(s32[16]{0:T(128)} %refs_1_.3) | copy-start | bytes 196
  2.8 39.4 %all-to-all-start = ((bf16[16,3,128,128]{3,2,1,0:T(8,128)(2,1)}), bf16[16,3,128,128]{3,2,1,0:T(8,128)(2,1)S(1)}, u32[]{:S(2)}, u32[]{:S(2)}) async-start(bf16[16,3,128,128]{3,2,1,0:T(8,128)(2,1)} %pack_heads.1), calls=%async_computation | async-start | bytes 3145728 | tf_op jit(solution)/shard_map/all_to_all | solution.py:390

commit v13 on v11

--- a/solution.py
+++ b/solution.py
@@ -315,7 +315,7 @@
 
     @pl.when(class_ref[me] == 1)
     def _():
-        sizes = [2, block_count // 2 - 2, block_count // 2 - 2, 2]
+        sizes = [2] + [4] * (block_count // 4 - 1) + [2]
         starts = [sum(sizes[:i]) for i in range(len(sizes))]
 
         def score(i):
@@ -390,7 +390,7 @@
         return lax.all_to_all(send, axes, split_axis=0, concat_axis=0, tiled=True)
 
     held = exchange(pack_heads(queries, keys, values))
-    stage_rows = (block_count // 2 - 2) * BLOCK
+    stage_rows = 4 * BLOCK
     attended = pl.pallas_call(
         lambda *refs: attend_kernel(axes, *refs),
         out_shape=jax.ShapeDtypeStruct((block_count, BLOCK, HD), jnp.bfloat16),

time: 70.4 us -> 70.8 us (level)
  Pallas kernels: 6.72 us -> 8.17 us
  blocking collectives: 63.7 us -> 62.7 us
    pallas_call x1, Pallas kernels: 4.32 us -> 5.77 us  [heads_by_device(): pl.pallas_call(lambda *refs: attend_kernel(axes, *refs), out_shape=jax.Sh...]
    all_to_all x2, blocking collectives: 63.7 us -> 62.7 us  [exchange(): return lax.all_to_all(send, axes, split_axis=0, concat_axis=0, tiled=True)]
where the time goes in v13:
time: 70.8 us; the launch traced here: 70.9 us
  blocking collectives  62.7 us (89%)
  Pallas kernels  8.17 us (12%)
    all_to_all x2, blocking collectives, exchange(): return lax.all_to_all(send, axes, split_axis=0, concat_axis=0, tiled=True)  62.7 us
    pallas_call x1, Pallas kernels, heads_by_device(): pl.pallas_call(lambda *refs: attend_kernel(axes, *refs), out_shape=jax.Sh...  5.77 us
    pallas_call x1, Pallas kernels, pack_heads(): pl.pallas_call(pack_kernel, out_shape=jax.ShapeDtypeStruct((HEADS, count,...  1.56 us

profile of v13, /device:TPU:0, one launch (start us, length us, event | category | flops | bytes accessed | tf_op | source)
XLA Modules:
  0.0 70.9 jit_solution(5911664281309465328)
XLA Ops:
  0.0 1.6 %pack_heads.1 = bf16[16,3,128,128]{3,2,1,0:T(8,128)(2,1)S(1)} custom-call(bf16[128,2048]{1,0:T(8,128)(2,1)} %refs_0_.2, bf16[128,2048]{1,0:T(8,128)(2,1)} %refs_1_.2, bf16[128,2048]{1,0:T(8,128)(2,1)} %refs_2_.1), custom_call_target="tpu_custom_call" | custom-call | tf_op jit(solution)/shard_map/pack_heads/pallas_call | solution.py:217
  1.6 0.0 copy-start
  1.6 0.0 copy-start.1
  1.6 43.4 %all_to_all.10.refs_2_ = bf16[16,3,128,128]{3,2,1,0:T(8,128)(2,1)S(1)} all-to-all(bf16[16,3,128,128]{3,2,1,0:T(8,128)(2,1)S(1)} %pack_heads.1), channel_id=1, replica_groups=mesh['clip'=2,'seq'=4,'blk'=4] {'seq','blk'}, dimensions={0} | all-to-all | bytes 3145728 | tf_op jit(solution)/shard_map/all_to_all | solution.py:390
  45.0 0.0 copy-done
  45.0 0.0 copy-done.1
  45.0 5.8 %attend_head.1 = bf16[16,128,128]{2,1,0:T(8,128)(2,1)S(1)} custom-call(s32[16,16,16]{2,1,0:T(8,128)S(1)} %copy-done, s32[16]{0:T(128)S(1)} %copy-done.1, bf16[16,3,128,128]{3,2,1,0:T(8,128)(2,1)S(1)} %all_to_all.10.refs_2_), custom_call_target="tpu_custom_call" | custom-call | tf_op jit(solution)/shard_map/attend_head/pallas_call | solution.py:394
  50.7 19.3 %all_to_all.11.held_ref = bf16[16,128,128]{2,1,0:T(8,128)(2,1)S(1)} all-to-all(bf16[16,128,128]{2,1,0:T(8,128)(2,1)S(1)} %attend_head.1), channel_id=1, replica_groups=mesh['clip'=2,'seq'=4,'blk'=4] {'seq','blk'}, dimensions={0} | all-to-all | bytes 1048576 | tf_op jit(solution)/shard_map/all_to_all | solution.py:390
  70.0 0.8 %unpack_heads.1 = bf16[128,2048]{1,0:T(8,128)(2,1)} custom-call(bf16[16,128,128]{2,1,0:T(8,128)(2,1)S(1)} %all_to_all.11.held_ref), custom_call_target="tpu_custom_call" | custom-call | tf_op jit(solution)/shard_map/unpack_heads/pallas_call | solution.py:253
Async XLA Ops:
  1.6 43.4 %copy-start = (s32[16,16,16]{2,1,0:T(8,128)S(1)}, s32[16,16,16]{2,1,0:T(8,128)}, u32[]{:S(2)}) copy-start(s32[16,16,16]{2,1,0:T(8,128)} %refs_0_.3) | copy-start | bytes 49156
  1.6 43.4 %copy-start.1 = (s32[16]{0:T(128)S(1)}, s32[16]{0:T(128)}, u32[]{:S(2)}) copy-start(s32[16]{0:T(128)} %refs_1_.3) | copy-start | bytes 196

commit v14 on v13

--- a/solution.py
+++ b/solution.py
@@ -304,11 +304,12 @@
             query_rows, key_rows, (((1,), (1,)), ((), ())), preferred_element_type=jnp.float32
         )
 
-    def weigh(rows, columns, slot):
-        logits = logits_slots[slot][:rows, :columns]
+    def weigh(first, rows, columns, slot):
+        chosen = slice(first, first + rows)
+        logits = logits_slots[slot][chosen, :columns]
         largest = jnp.max(logits, axis=-1, keepdims=True)
         weights = jnp.exp2((logits - largest) * exponent_scale).astype(jnp.bfloat16)
-        weights_slots[slot][:rows, :columns] = weights
+        weights_slots[slot][chosen, :columns] = weights
 
     def normalized(summed):
         return (summed[:, :HD] / summed[:, HD:]).astype(jnp.bfloat16)
@@ -318,14 +319,20 @@
         sizes = [2] + [4] * (block_count // 4 - 1) + [2]
         starts = [sum(sizes[:i]) for i in range(len(sizes))]
 
-        def score(i):
+        parts = 4
+        part_blocks = block_count // parts
+
+        def score(i, part):
             rows = sizes[i] * BLOCK
             query_rows = qkv_ref[starts[i] : starts[i] + sizes[i], 0].reshape(rows, HD)
-            key_rows = qkv_ref[:, 1].reshape(block_count * BLOCK, HD)
-            logits_slots[i % 2][:rows, :] = scores(query_rows, key_rows)
-
-        def weigh_all(i):
-            weigh(sizes[i] * BLOCK, block_count * BLOCK, i % 2)
+            blocks = slice(part * part_blocks, (part + 1) * part_blocks)
+            key_rows = qkv_ref[blocks, 1].reshape(part_blocks * BLOCK, HD)
+            columns = slice(part * part_blocks * BLOCK, (part + 1) * part_blocks * BLOCK)
+            logits_slots[i % 2][:rows, columns] = scores(query_rows, key_rows)
+
+        def weigh_all(i, part):
+            rows = sizes[i] * BLOCK // parts
+            weigh(part * rows, rows, block_count * BLOCK, i % 2)
 
         def blend(i):
             rows = sizes[i] * BLOCK
@@ -334,14 +341,15 @@
             out = normalized(jnp.dot(weights, value_rows, preferred_element_type=jnp.float32))
             out_ref[starts[i] : starts[i] + sizes[i]] = out.reshape(sizes[i], BLOCK, HD)
 
-        score(0)
-        weigh_all(0)
-        score(1)
-        for i in range(1, len(sizes)):
-            blend(i - 1)
-            weigh_all(i)
-            if i + 1 < len(sizes):
-                score(i + 1)
+        for part in range(parts):
+            score(0, part)
+        for i in range(len(sizes)):
+            if i > 0:
+                blend(i - 1)
+            for part in range(parts):
+                weigh_all(i, part)
+                if i + 1 < len(sizes):
+                    score(i + 1, part)
         blend(len(sizes) - 1)
         kept_copy.wait()
 
@@ -376,7 +384,7 @@
                 out_ref[block] = normalized(summed)
 
         def weigh_few(i, slot):
-            weigh(group * BLOCK, block_count // KEEP * LIGHT * BLOCK, slot)
+            weigh(0, group * BLOCK, block_count // KEEP * LIGHT * BLOCK, slot)
 
         pipelined(block_count // group, score, weigh_few, blend)
 

time: 70.8 us -> 70.3 us (level); the launches traced: 70.9 us -> 69.5 us
  Pallas kernels: 8.17 us -> 6.72 us
    pallas_call x1, Pallas kernels: 5.77 us -> 4.32 us  [heads_by_device(): pl.pallas_call(lambda *refs: attend_kernel(axes, *refs), out_shape=jax.Sh...]
where the time goes in v14:
time: 70.3 us; the launch traced here: 69.5 us
  blocking collectives  62.7 us (89%)
  Pallas kernels  6.72 us (10%)
    all_to_all x2, blocking collectives, exchange(): return lax.all_to_all(send, axes, split_axis=0, concat_axis=0, tiled=True)  62.7 us
    pallas_call x1, Pallas kernels, heads_by_device(): pl.pallas_call(lambda *refs: attend_kernel(axes, *refs), out_shape=jax.Sh...  4.32 us
    pallas_call x1, Pallas kernels, pack_heads(): pl.pallas_call(pack_kernel, out_shape=jax.ShapeDtypeStruct((HEADS, count,...  1.56 us

profile of v14, /device:TPU:0, one launch (start us, length us, event | category | flops | bytes accessed | tf_op | source)
XLA Modules:
  0.0 69.5 jit_solution(15584459050273499491)
XLA Ops:
  0.0 1.6 %pack_heads.1 = bf16[16,3,128,128]{3,2,1,0:T(8,128)(2,1)S(1)} custom-call(bf16[128,2048]{1,0:T(8,128)(2,1)} %refs_0_.2, bf16[128,2048]{1,0:T(8,128)(2,1)} %refs_1_.2, bf16[128,2048]{1,0:T(8,128)(2,1)} %refs_2_.1), custom_call_target="tpu_custom_call" | custom-call | tf_op jit(solution)/shard_map/pack_heads/pallas_call | solution.py:217
  1.6 0.0 copy-start
  1.6 0.0 copy-start.1
  1.6 43.4 %all_to_all.10.refs_2_ = bf16[16,3,128,128]{3,2,1,0:T(8,128)(2,1)S(1)} all-to-all(bf16[16,3,128,128]{3,2,1,0:T(8,128)(2,1)S(1)} %pack_heads.1), channel_id=1, replica_groups=mesh['clip'=2,'seq'=4,'blk'=4] {'seq','blk'}, dimensions={0} | all-to-all | bytes 3145728 | tf_op jit(solution)/shard_map/all_to_all | solution.py:398
  45.0 0.0 copy-done
  45.0 0.0 copy-done.1
  45.0 4.3 %attend_head.1 = bf16[16,128,128]{2,1,0:T(8,128)(2,1)S(1)} custom-call(s32[16,16,16]{2,1,0:T(8,128)S(1)} %copy-done, s32[16]{0:T(128)S(1)} %copy-done.1, bf16[16,3,128,128]{3,2,1,0:T(8,128)(2,1)S(1)} %all_to_all.10.refs_2_), custom_call_target="tpu_custom_call" | custom-call | tf_op jit(solution)/shard_map/attend_head/pallas_call | solution.py:402
  49.3 19.3 %all_to_all.11.held_ref = bf16[16,128,128]{2,1,0:T(8,128)(2,1)S(1)} all-to-all(bf16[16,128,128]{2,1,0:T(8,128)(2,1)S(1)} %attend_head.1), channel_id=1, replica_groups=mesh['clip'=2,'seq'=4,'blk'=4] {'seq','blk'}, dimensions={0} | all-to-all | bytes 1048576 | tf_op jit(solution)/shard_map/all_to_all | solution.py:398
  68.6 0.8 %unpack_heads.1 = bf16[128,2048]{1,0:T(8,128)(2,1)} custom-call(bf16[16,128,128]{2,1,0:T(8,128)(2,1)S(1)} %all_to_all.11.held_ref), custom_call_target="tpu_custom_call" | custom-call | tf_op jit(solution)/shard_map/unpack_heads/pallas_call | solution.py:253
Async XLA Ops:
  1.6 43.4 %copy-start = (s32[16,16,16]{2,1,0:T(8,128)S(1)}, s32[16,16,16]{2,1,0:T(8,128)}, u32[]{:S(2)}) copy-start(s32[16,16,16]{2,1,0:T(8,128)} %refs_0_.3) | copy-start | bytes 49156
  1.6 43.4 %copy-start.1 = (s32[16]{0:T(128)S(1)}, s32[16]{0:T(128)}, u32[]{:S(2)}) copy-start(s32[16]{0:T(128)} %refs_1_.3) | copy-start | bytes 196

commit v15 on v13

--- a/solution.py
+++ b/solution.py
@@ -285,9 +285,10 @@
 
 
 def attend_kernel(axes, kept_hbm, class_hbm, qkv_ref, out_ref, *scratch):
-    kept_ref, class_ref, v_all, logits_a, logits_b, weights_a, weights_b, kept_sem, class_sem = scratch
+    kept_ref, class_ref, logits_a, logits_b, weights_a, weights_b, totals_a, totals_b, kept_sem, class_sem = scratch
     logits_slots = (logits_a, logits_b)
     weights_slots = (weights_a, weights_b)
+    totals_slots = (totals_a, totals_b)
     block_count = qkv_ref.shape[0]
     me = own_place(axes)
     exponent_scale = math.log2(math.e) / math.sqrt(HD)
@@ -295,8 +296,6 @@
     class_copy = pltpu.make_async_copy(class_hbm, class_ref, class_sem)
     class_copy.start()
     kept_copy.start()
-    v_all[:, :, :HD] = qkv_ref[:, 2]
-    v_all[:, :, HD:] = jnp.ones((block_count, BLOCK, HD), jnp.bfloat16)
     class_copy.wait()
 
     def scores(query_rows, key_rows):
@@ -307,11 +306,13 @@
     def weigh(rows, columns, slot):
         logits = logits_slots[slot][:rows, :columns]
         largest = jnp.max(logits, axis=-1, keepdims=True)
-        weights = jnp.exp2((logits - largest) * exponent_scale).astype(jnp.bfloat16)
-        weights_slots[slot][:rows, :columns] = weights
-
-    def normalized(summed):
-        return (summed[:, :HD] / summed[:, HD:]).astype(jnp.bfloat16)
+        weights = jnp.exp2((logits - largest) * exponent_scale)
+        totals = jnp.sum(weights, axis=-1, keepdims=True)
+        totals_slots[slot][:rows, :] = jnp.broadcast_to(totals, (rows, HD))
+        weights_slots[slot][:rows, :columns] = weights.astype(jnp.bfloat16)
+
+    def normalized(summed, totals):
+        return (summed / totals).astype(jnp.bfloat16)
 
     @pl.when(class_ref[me] == 1)
     def _():
@@ -329,9 +330,10 @@
 
         def blend(i):
             rows = sizes[i] * BLOCK
-            value_rows = v_all[...].reshape(block_count * BLOCK, 2 * HD)
+            value_rows = qkv_ref[:, 2].reshape(block_count * BLOCK, HD)
             weights = weights_slots[i % 2][:rows, :]
-            out = normalized(jnp.dot(weights, value_rows, preferred_element_type=jnp.float32))
+            summed = jnp.dot(weights, value_rows, preferred_element_type=jnp.float32)
+            out = normalized(summed, totals_slots[i % 2][:rows, :])
             out_ref[starts[i] : starts[i] + sizes[i]] = out.reshape(sizes[i], BLOCK, HD)
 
         score(0)
@@ -367,13 +369,13 @@
             for member in range(group):
                 block = group * i + member
                 rows = slice(member * BLOCK, (member + 1) * BLOCK)
-                summed = jnp.zeros((BLOCK, 2 * HD), jnp.float32)
+                summed = jnp.zeros((BLOCK, HD), jnp.float32)
                 for place, (one, other) in enumerate(block_pairs(block)):
-                    value_rows = jnp.concatenate([v_all[one], v_all[other]], axis=0)
+                    value_rows = jnp.concatenate([qkv_ref[one, 2], qkv_ref[other, 2]], axis=0)
                     columns = slice(place * 2 * BLOCK, (place + 1) * 2 * BLOCK)
                     weights = weights_slots[slot][rows, columns]
                     summed += jnp.dot(weights, value_rows, preferred_element_type=jnp.float32)
-                out_ref[block] = normalized(summed)
+                out_ref[block] = normalized(summed, totals_slots[slot][rows, :])
 
         def weigh_few(i, slot):
             weigh(group * BLOCK, block_count // KEEP * LIGHT * BLOCK, slot)
@@ -403,11 +405,12 @@
         scratch_shapes=[
             pltpu.SMEM(kept.shape[1:], jnp.int32),
             pltpu.SMEM(dense_class.shape, jnp.int32),
-            pltpu.VMEM((block_count, BLOCK, 2 * HD), jnp.bfloat16),
             pltpu.VMEM((stage_rows, block_count * BLOCK), jnp.float32),
             pltpu.VMEM((stage_rows, block_count * BLOCK), jnp.float32),
             pltpu.VMEM((stage_rows, block_count * BLOCK), jnp.bfloat16),
             pltpu.VMEM((stage_rows, block_count * BLOCK), jnp.bfloat16),
+            pltpu.VMEM((stage_rows, HD), jnp.float32),
+            pltpu.VMEM((stage_rows, HD), jnp.float32),
             pltpu.SemaphoreType.DMA,
             pltpu.SemaphoreType.DMA,
         ],

time: 70.8 us -> 71.9 us (1.016)
  Pallas kernels: 8.17 us -> 9.02 us
    pallas_call x1, Pallas kernels: 5.77 us -> 6.62 us  [heads_by_device(): pl.pallas_call(lambda *refs: attend_kernel(axes, *refs), out_shape=jax.Sh...]
where the time goes in v15:
time: 71.9 us; the launch traced here: 71.6 us
  blocking collectives  62.6 us (87%)
  Pallas kernels  9.02 us (13%)
    all_to_all x2, blocking collectives, exchange(): return lax.all_to_all(send, axes, split_axis=0, concat_axis=0, tiled=True)  62.6 us
    pallas_call x1, Pallas kernels, heads_by_device(): pl.pallas_call(lambda *refs: attend_kernel(axes, *refs), out_shape=jax.Sh...  6.62 us
    pallas_call x1, Pallas kernels, pack_heads(): pl.pallas_call(pack_kernel, out_shape=jax.ShapeDtypeStruct((HEADS, count,...  1.56 us

profile of v15, /device:TPU:0, one launch (start us, length us, event | category | flops | bytes accessed | tf_op | source)
XLA Modules:
  0.0 71.6 jit_solution(1587827460795170833)
XLA Ops:
  0.0 1.6 %pack_heads.1 = bf16[16,3,128,128]{3,2,1,0:T(8,128)(2,1)S(1)} custom-call(bf16[128,2048]{1,0:T(8,128)(2,1)} %refs_0_.2, bf16[128,2048]{1,0:T(8,128)(2,1)} %refs_1_.2, bf16[128,2048]{1,0:T(8,128)(2,1)} %refs_2_.1), custom_call_target="tpu_custom_call" | custom-call | tf_op jit(solution)/shard_map/pack_heads/pallas_call | solution.py:217
  1.6 0.0 copy-start
  1.6 0.0 copy-start.1
  1.6 43.4 %all_to_all.10.refs_2_ = bf16[16,3,128,128]{3,2,1,0:T(8,128)(2,1)S(1)} all-to-all(bf16[16,3,128,128]{3,2,1,0:T(8,128)(2,1)S(1)} %pack_heads.1), channel_id=1, replica_groups=mesh['clip'=2,'seq'=4,'blk'=4] {'seq','blk'}, dimensions={0} | all-to-all | bytes 3145728 | tf_op jit(solution)/shard_map/all_to_all | solution.py:392
  45.0 0.0 copy-done
  45.0 0.0 copy-done.1
  45.0 6.6 %attend_head.1 = bf16[16,128,128]{2,1,0:T(8,128)(2,1)S(1)} custom-call(s32[16,16,16]{2,1,0:T(8,128)S(1)} %copy-done, s32[16]{0:T(128)S(1)} %copy-done.1, bf16[16,3,128,128]{3,2,1,0:T(8,128)(2,1)S(1)} %all_to_all.10.refs_2_), custom_call_target="tpu_custom_call" | custom-call | tf_op jit(solution)/shard_map/attend_head/pallas_call | solution.py:396
  51.6 19.2 %all_to_all.11.held_ref = bf16[16,128,128]{2,1,0:T(8,128)(2,1)S(1)} all-to-all(bf16[16,128,128]{2,1,0:T(8,128)(2,1)S(1)} %attend_head.1), channel_id=1, replica_groups=mesh['clip'=2,'seq'=4,'blk'=4] {'seq','blk'}, dimensions={0} | all-to-all | bytes 1048576 | tf_op jit(solution)/shard_map/all_to_all | solution.py:392
  70.8 0.8 %unpack_heads.1 = bf16[128,2048]{1,0:T(8,128)(2,1)} custom-call(bf16[16,128,128]{2,1,0:T(8,128)(2,1)S(1)} %all_to_all.11.held_ref), custom_call_target="tpu_custom_call" | custom-call | tf_op jit(solution)/shard_map/unpack_heads/pallas_call | solution.py:253
Async XLA Ops:
  1.6 43.4 %copy-start = (s32[16,16,16]{2,1,0:T(8,128)S(1)}, s32[16,16,16]{2,1,0:T(8,128)}, u32[]{:S(2)}) copy-start(s32[16,16,16]{2,1,0:T(8,128)} %refs_0_.3) | copy-start | bytes 49156
  1.6 43.4 %copy-start.1 = (s32[16]{0:T(128)S(1)}, s32[16]{0:T(128)}, u32[]{:S(2)}) copy-start(s32[16]{0:T(128)} %refs_1_.3) | copy-start | bytes 196

commit v16 on v13

--- a/solution.py
+++ b/solution.py
@@ -285,7 +285,7 @@
 
 
 def attend_kernel(axes, kept_hbm, class_hbm, qkv_ref, out_ref, *scratch):
-    kept_ref, class_ref, v_all, logits_a, logits_b, weights_a, weights_b, kept_sem, class_sem = scratch
+    kept_ref, class_ref, q_parts, k_twice, v_all, logits_a, logits_b, weights_a, weights_b, kept_sem, class_sem = scratch
     logits_slots = (logits_a, logits_b)
     weights_slots = (weights_a, weights_b)
     block_count = qkv_ref.shape[0]
@@ -297,6 +297,13 @@
     kept_copy.start()
     v_all[:, :, :HD] = qkv_ref[:, 2]
     v_all[:, :, HD:] = jnp.ones((block_count, BLOCK, HD), jnp.bfloat16)
+    for block in range(block_count):
+        scaled = qkv_ref[block, 0].astype(jnp.float32) * exponent_scale
+        high = scaled.astype(jnp.bfloat16)
+        q_parts[block, :, :HD] = high
+        q_parts[block, :, HD:] = (scaled - high.astype(jnp.float32)).astype(jnp.bfloat16)
+        k_twice[block, :, :HD] = qkv_ref[block, 1]
+        k_twice[block, :, HD:] = qkv_ref[block, 1]
     class_copy.wait()
 
     def scores(query_rows, key_rows):
@@ -307,7 +314,7 @@
     def weigh(rows, columns, slot):
         logits = logits_slots[slot][:rows, :columns]
         largest = jnp.max(logits, axis=-1, keepdims=True)
-        weights = jnp.exp2((logits - largest) * exponent_scale).astype(jnp.bfloat16)
+        weights = jnp.exp2(logits - largest).astype(jnp.bfloat16)
         weights_slots[slot][:rows, :columns] = weights
 
     def normalized(summed):
@@ -320,8 +327,8 @@
 
         def score(i):
             rows = sizes[i] * BLOCK
-            query_rows = qkv_ref[starts[i] : starts[i] + sizes[i], 0].reshape(rows, HD)
-            key_rows = qkv_ref[:, 1].reshape(block_count * BLOCK, HD)
+            query_rows = q_parts[starts[i] : starts[i] + sizes[i]].reshape(rows, 2 * HD)
+            key_rows = k_twice[...].reshape(block_count * BLOCK, 2 * HD)
             logits_slots[i % 2][:rows, :] = scores(query_rows, key_rows)
 
         def weigh_all(i):
@@ -359,9 +366,9 @@
                 block = group * i + member
                 rows = slice(member * BLOCK, (member + 1) * BLOCK)
                 for place, (one, other) in enumerate(block_pairs(block)):
-                    key_rows = jnp.concatenate([qkv_ref[one, 1], qkv_ref[other, 1]], axis=0)
+                    key_rows = jnp.concatenate([k_twice[one], k_twice[other]], axis=0)
                     columns = slice(place * 2 * BLOCK, (place + 1) * 2 * BLOCK)
-                    logits_slots[slot][rows, columns] = scores(qkv_ref[block, 0], key_rows)
+                    logits_slots[slot][rows, columns] = scores(q_parts[block], key_rows)
 
         def blend(i, slot):
             for member in range(group):
@@ -404,6 +411,8 @@
             pltpu.SMEM(kept.shape[1:], jnp.int32),
             pltpu.SMEM(dense_class.shape, jnp.int32),
             pltpu.VMEM((block_count, BLOCK, 2 * HD), jnp.bfloat16),
+            pltpu.VMEM((block_count, BLOCK, 2 * HD), jnp.bfloat16),
+            pltpu.VMEM((block_count, BLOCK, 2 * HD), jnp.bfloat16),
             pltpu.VMEM((stage_rows, block_count * BLOCK), jnp.float32),
             pltpu.VMEM((stage_rows, block_count * BLOCK), jnp.float32),
             pltpu.VMEM((stage_rows, block_count * BLOCK), jnp.bfloat16),

time: 70.8 us -> 71 us (level)
  no operation moved by 1% of the time
where the time goes in v16:
time: 71 us; the launch traced here: 70.8 us
  blocking collectives  62.7 us (88%)
  Pallas kernels  8.03 us (11%)
    all_to_all x2, blocking collectives, exchange(): return lax.all_to_all(send, axes, split_axis=0, concat_axis=0, tiled=True)  62.7 us
    pallas_call x1, Pallas kernels, heads_by_device(): pl.pallas_call(lambda *refs: attend_kernel(axes, *refs), out_shape=jax.Sh...  5.62 us
    pallas_call x1, Pallas kernels, pack_heads(): pl.pallas_call(pack_kernel, out_shape=jax.ShapeDtypeStruct((HEADS, count,...  1.56 us

profile of v16, /device:TPU:0, one launch (start us, length us, event | category | flops | bytes accessed | tf_op | source)
XLA Modules:
  0.0 70.8 jit_solution(3314923977653634250)
XLA Ops:
  0.0 1.6 %pack_heads.1 = bf16[16,3,128,128]{3,2,1,0:T(8,128)(2,1)S(1)} custom-call(bf16[128,2048]{1,0:T(8,128)(2,1)} %refs_0_.2, bf16[128,2048]{1,0:T(8,128)(2,1)} %refs_1_.2, bf16[128,2048]{1,0:T(8,128)(2,1)} %refs_2_.1), custom_call_target="tpu_custom_call" | custom-call | tf_op jit(solution)/shard_map/pack_heads/pallas_call | solution.py:217
  1.6 0.0 copy-start
  1.6 0.0 copy-start.1
  1.6 43.4 %all_to_all.10.refs_2_ = bf16[16,3,128,128]{3,2,1,0:T(8,128)(2,1)S(1)} all-to-all(bf16[16,3,128,128]{3,2,1,0:T(8,128)(2,1)S(1)} %pack_heads.1), channel_id=1, replica_groups=mesh['clip'=2,'seq'=4,'blk'=4] {'seq','blk'}, dimensions={0} | all-to-all | bytes 3145728 | tf_op jit(solution)/shard_map/all_to_all | solution.py:397
  45.0 0.0 copy-done
  45.0 0.0 copy-done.1
  45.0 5.6 %attend_head.1 = bf16[16,128,128]{2,1,0:T(8,128)(2,1)S(1)} custom-call(s32[16,16,16]{2,1,0:T(8,128)S(1)} %copy-done, s32[16]{0:T(128)S(1)} %copy-done.1, bf16[16,3,128,128]{3,2,1,0:T(8,128)(2,1)S(1)} %all_to_all.10.refs_2_), custom_call_target="tpu_custom_call" | custom-call | tf_op jit(solution)/shard_map/attend_head/pallas_call | solution.py:401
  50.6 19.3 %all_to_all.11.held_ref = bf16[16,128,128]{2,1,0:T(8,128)(2,1)S(1)} all-to-all(bf16[16,128,128]{2,1,0:T(8,128)(2,1)S(1)} %attend_head.1), channel_id=1, replica_groups=mesh['clip'=2,'seq'=4,'blk'=4] {'seq','blk'}, dimensions={0} | all-to-all | bytes 1048576 | tf_op jit(solution)/shard_map/all_to_all | solution.py:397
  69.9 0.8 %unpack_heads.1 = bf16[128,2048]{1,0:T(8,128)(2,1)} custom-call(bf16[16,128,128]{2,1,0:T(8,128)(2,1)S(1)} %all_to_all.11.held_ref), custom_call_target="tpu_custom_call" | custom-call | tf_op jit(solution)/shard_map/unpack_heads/pallas_call | solution.py:253
Async XLA Ops:
  1.6 43.4 %copy-start = (s32[16,16,16]{2,1,0:T(8,128)S(1)}, s32[16,16,16]{2,1,0:T(8,128)}, u32[]{:S(2)}) copy-start(s32[16,16,16]{2,1,0:T(8,128)} %refs_0_.3) | copy-start | bytes 49156
  1.6 43.4 %copy-start.1 = (s32[16]{0:T(128)S(1)}, s32[16]{0:T(128)}, u32[]{:S(2)}) copy-start(s32[16]{0:T(128)} %refs_1_.3) | copy-start | bytes 196

commit v17 on v13

--- a/solution.py
+++ b/solution.py
@@ -304,11 +304,13 @@
             query_rows, key_rows, (((1,), (1,)), ((), ())), preferred_element_type=jnp.float32
         )
 
-    def weigh(rows, columns, slot):
+    def weigh(rows, columns, slot, scale=None):
         logits = logits_slots[slot][:rows, :columns]
         largest = jnp.max(logits, axis=-1, keepdims=True)
-        weights = jnp.exp2((logits - largest) * exponent_scale).astype(jnp.bfloat16)
-        weights_slots[slot][:rows, :columns] = weights
+        below = logits - largest
+        if scale is not None:
+            below = below * scale
+        weights_slots[slot][:rows, :columns] = jnp.exp2(below).astype(jnp.bfloat16)
 
     def normalized(summed):
         return (summed[:, :HD] / summed[:, HD:]).astype(jnp.bfloat16)
@@ -321,8 +323,13 @@
         def score(i):
             rows = sizes[i] * BLOCK
             query_rows = qkv_ref[starts[i] : starts[i] + sizes[i], 0].reshape(rows, HD)
+            scaled = query_rows.astype(jnp.float32) * exponent_scale
+            high = scaled.astype(jnp.bfloat16)
+            low = (scaled - high.astype(jnp.float32)).astype(jnp.bfloat16)
             key_rows = qkv_ref[:, 1].reshape(block_count * BLOCK, HD)
-            logits_slots[i % 2][:rows, :] = scores(query_rows, key_rows)
+            logits_slots[i % 2][:rows, :] = scores(
+                jnp.concatenate([high, low], axis=1), jnp.concatenate([key_rows, key_rows], axis=1)
+            )
 
         def weigh_all(i):
             weigh(sizes[i] * BLOCK, block_count * BLOCK, i % 2)
@@ -376,7 +383,7 @@
                 out_ref[block] = normalized(summed)
 
         def weigh_few(i, slot):
-            weigh(group * BLOCK, block_count // KEEP * LIGHT * BLOCK, slot)
+            weigh(group * BLOCK, block_count // KEEP * LIGHT * BLOCK, slot, exponent_scale)
 
         pipelined(block_count // group, score, weigh_few, blend)
 

time: 70.8 us -> 71.2 us (level)
  no operation moved by 1% of the time
where the time goes in v17:
time: 71.2 us; the launch traced here: 71 us
  blocking collectives  62.7 us (88%)
  Pallas kernels  8.23 us (12%)
    all_to_all x2, blocking collectives, exchange(): return lax.all_to_all(send, axes, split_axis=0, concat_axis=0, tiled=True)  62.7 us
    pallas_call x1, Pallas kernels, heads_by_device(): pl.pallas_call(lambda *refs: attend_kernel(axes, *refs), out_shape=jax.Sh...  5.82 us
    pallas_call x1, Pallas kernels, pack_heads(): pl.pallas_call(pack_kernel, out_shape=jax.ShapeDtypeStruct((HEADS, count,...  1.56 us

profile of v17, /device:TPU:0, one launch (start us, length us, event | category | flops | bytes accessed | tf_op | source)
XLA Modules:
  0.0 71.0 jit_solution(12054673004140951145)
XLA Ops:
  0.0 1.6 %pack_heads.1 = bf16[16,3,128,128]{3,2,1,0:T(8,128)(2,1)S(1)} custom-call(bf16[128,2048]{1,0:T(8,128)(2,1)} %refs_0_.2, bf16[128,2048]{1,0:T(8,128)(2,1)} %refs_1_.2, bf16[128,2048]{1,0:T(8,128)(2,1)} %refs_2_.1), custom_call_target="tpu_custom_call" | custom-call | tf_op jit(solution)/shard_map/pack_heads/pallas_call | solution.py:217
  1.6 0.0 copy-start
  1.6 0.0 copy-start.1
  1.6 43.4 %all_to_all.10.refs_2_ = bf16[16,3,128,128]{3,2,1,0:T(8,128)(2,1)S(1)} all-to-all(bf16[16,3,128,128]{3,2,1,0:T(8,128)(2,1)S(1)} %pack_heads.1), channel_id=1, replica_groups=mesh['clip'=2,'seq'=4,'blk'=4] {'seq','blk'}, dimensions={0} | all-to-all | bytes 3145728 | tf_op jit(solution)/shard_map/all_to_all | solution.py:397
  45.0 0.0 copy-done
  45.0 0.0 copy-done.1
  45.0 5.8 %attend_head.1 = bf16[16,128,128]{2,1,0:T(8,128)(2,1)S(1)} custom-call(s32[16,16,16]{2,1,0:T(8,128)S(1)} %copy-done, s32[16]{0:T(128)S(1)} %copy-done.1, bf16[16,3,128,128]{3,2,1,0:T(8,128)(2,1)S(1)} %all_to_all.10.refs_2_), custom_call_target="tpu_custom_call" | custom-call | tf_op jit(solution)/shard_map/attend_head/pallas_call | solution.py:401
  50.8 19.3 %all_to_all.11.held_ref = bf16[16,128,128]{2,1,0:T(8,128)(2,1)S(1)} all-to-all(bf16[16,128,128]{2,1,0:T(8,128)(2,1)S(1)} %attend_head.1), channel_id=1, replica_groups=mesh['clip'=2,'seq'=4,'blk'=4] {'seq','blk'}, dimensions={0} | all-to-all | bytes 1048576 | tf_op jit(solution)/shard_map/all_to_all | solution.py:397
  70.1 0.8 %unpack_heads.1 = bf16[128,2048]{1,0:T(8,128)(2,1)} custom-call(bf16[16,128,128]{2,1,0:T(8,128)(2,1)S(1)} %all_to_all.11.held_ref), custom_call_target="tpu_custom_call" | custom-call | tf_op jit(solution)/shard_map/unpack_heads/pallas_call | solution.py:253
Async XLA Ops:
  1.6 43.4 %copy-start = (s32[16,16,16]{2,1,0:T(8,128)S(1)}, s32[16,16,16]{2,1,0:T(8,128)}, u32[]{:S(2)}) copy-start(s32[16,16,16]{2,1,0:T(8,128)} %refs_0_.3) | copy-start | bytes 49156
  1.6 43.4 %copy-start.1 = (s32[16]{0:T(128)S(1)}, s32[16]{0:T(128)}, u32[]{:S(2)}) copy-start(s32[16]{0:T(128)} %refs_1_.3) | copy-start | bytes 196

commit v18 on v13

--- a/solution.py
+++ b/solution.py
@@ -311,7 +311,10 @@
         weights_slots[slot][:rows, :columns] = weights
 
     def normalized(summed):
-        return (summed[:, :HD] / summed[:, HD:]).astype(jnp.bfloat16)
+        totals = summed[:, HD:]
+        inverse = pl.reciprocal(totals, approx=True)
+        inverse = inverse * (2.0 - totals * inverse)
+        return (summed[:, :HD] * inverse).astype(jnp.bfloat16)
 
     @pl.when(class_ref[me] == 1)
     def _():

time: 70.8 us -> 70.4 us (level)
  no operation moved by 1% of the time
where the time goes in v18:
time: 70.4 us; the launch traced here: 70.8 us
  blocking collectives  62.7 us (89%)
  Pallas kernels  8.12 us (12%)
    all_to_all x2, blocking collectives, exchange(): return lax.all_to_all(send, axes, split_axis=0, concat_axis=0, tiled=True)  62.7 us
    pallas_call x1, Pallas kernels, heads_by_device(): pl.pallas_call(lambda *refs: attend_kernel(axes, *refs), out_shape=jax.Sh...  5.72 us
    pallas_call x1, Pallas kernels, pack_heads(): pl.pallas_call(pack_kernel, out_shape=jax.ShapeDtypeStruct((HEADS, count,...  1.56 us

profile of v18, /device:TPU:0, one launch (start us, length us, event | category | flops | bytes accessed | tf_op | source)
XLA Modules:
  0.0 70.8 jit_solution(14621313292800000934)
XLA Ops:
  0.0 1.6 %pack_heads.1 = bf16[16,3,128,128]{3,2,1,0:T(8,128)(2,1)S(1)} custom-call(bf16[128,2048]{1,0:T(8,128)(2,1)} %refs_0_.2, bf16[128,2048]{1,0:T(8,128)(2,1)} %refs_1_.2, bf16[128,2048]{1,0:T(8,128)(2,1)} %refs_2_.1), custom_call_target="tpu_custom_call" | custom-call | tf_op jit(solution)/shard_map/pack_heads/pallas_call | solution.py:217
  1.6 0.0 copy-start
  1.6 0.0 copy-start.1
  1.6 43.4 %all_to_all.10.refs_2_ = bf16[16,3,128,128]{3,2,1,0:T(8,128)(2,1)S(1)} all-to-all(bf16[16,3,128,128]{3,2,1,0:T(8,128)(2,1)S(1)} %pack_heads.1), channel_id=1, replica_groups=mesh['clip'=2,'seq'=4,'blk'=4] {'seq','blk'}, dimensions={0} | all-to-all | bytes 3145728 | tf_op jit(solution)/shard_map/all_to_all | solution.py:393
  45.0 0.0 copy-done
  45.0 0.0 copy-done.1
  45.0 5.7 %attend_head.1 = bf16[16,128,128]{2,1,0:T(8,128)(2,1)S(1)} custom-call(s32[16,16,16]{2,1,0:T(8,128)S(1)} %copy-done, s32[16]{0:T(128)S(1)} %copy-done.1, bf16[16,3,128,128]{3,2,1,0:T(8,128)(2,1)S(1)} %all_to_all.10.refs_2_), custom_call_target="tpu_custom_call" | custom-call | tf_op jit(solution)/shard_map/attend_head/pallas_call | solution.py:397
  50.7 19.3 %all_to_all.11.held_ref = bf16[16,128,128]{2,1,0:T(8,128)(2,1)S(1)} all-to-all(bf16[16,128,128]{2,1,0:T(8,128)(2,1)S(1)} %attend_head.1), channel_id=1, replica_groups=mesh['clip'=2,'seq'=4,'blk'=4] {'seq','blk'}, dimensions={0} | all-to-all | bytes 1048576 | tf_op jit(solution)/shard_map/all_to_all | solution.py:393
  70.0 0.8 %unpack_heads.1 = bf16[128,2048]{1,0:T(8,128)(2,1)} custom-call(bf16[16,128,128]{2,1,0:T(8,128)(2,1)S(1)} %all_to_all.11.held_ref), custom_call_target="tpu_custom_call" | custom-call | tf_op jit(solution)/shard_map/unpack_heads/pallas_call | solution.py:253
Async XLA Ops:
  1.6 43.4 %copy-start = (s32[16,16,16]{2,1,0:T(8,128)S(1)}, s32[16,16,16]{2,1,0:T(8,128)}, u32[]{:S(2)}) copy-start(s32[16,16,16]{2,1,0:T(8,128)} %refs_0_.3) | copy-start | bytes 49156
  1.6 43.4 %copy-start.1 = (s32[16]{0:T(128)S(1)}, s32[16]{0:T(128)}, u32[]{:S(2)}) copy-start(s32[16]{0:T(128)} %refs_1_.3) | copy-start | bytes 196

commit v19 on v13

--- a/solution.py
+++ b/solution.py
@@ -315,7 +315,7 @@
 
     @pl.when(class_ref[me] == 1)
     def _():
-        sizes = [2] + [4] * (block_count // 4 - 1) + [2]
+        sizes = [1, 3] + [4] * (block_count // 4 - 2) + [3, 1]
         starts = [sum(sizes[:i]) for i in range(len(sizes))]
 
         def score(i):

time: 70.8 us -> 70.4 us (level)
  no operation moved by 1% of the time
where the time goes in v19:
time: 70.4 us; the launch traced here: 70.8 us
  blocking collectives  62.7 us (89%)
  Pallas kernels  8.11 us (12%)
    all_to_all x2, blocking collectives, exchange(): return lax.all_to_all(send, axes, split_axis=0, concat_axis=0, tiled=True)  62.7 us
    pallas_call x1, Pallas kernels, heads_by_device(): pl.pallas_call(lambda *refs: attend_kernel(axes, *refs), out_shape=jax.Sh...  5.71 us
    pallas_call x1, Pallas kernels, pack_heads(): pl.pallas_call(pack_kernel, out_shape=jax.ShapeDtypeStruct((HEADS, count,...  1.56 us

profile of v19, /device:TPU:0, one launch (start us, length us, event | category | flops | bytes accessed | tf_op | source)
XLA Modules:
  0.0 70.8 jit_solution(1254167831178254200)
XLA Ops:
  0.0 1.6 %pack_heads.1 = bf16[16,3,128,128]{3,2,1,0:T(8,128)(2,1)S(1)} custom-call(bf16[128,2048]{1,0:T(8,128)(2,1)} %refs_0_.2, bf16[128,2048]{1,0:T(8,128)(2,1)} %refs_1_.2, bf16[128,2048]{1,0:T(8,128)(2,1)} %refs_2_.1), custom_call_target="tpu_custom_call" | custom-call | tf_op jit(solution)/shard_map/pack_heads/pallas_call | solution.py:217
  1.6 0.0 copy-start
  1.6 0.0 copy-start.1
  1.6 43.4 %all_to_all.10.refs_2_ = bf16[16,3,128,128]{3,2,1,0:T(8,128)(2,1)S(1)} all-to-all(bf16[16,3,128,128]{3,2,1,0:T(8,128)(2,1)S(1)} %pack_heads.1), channel_id=1, replica_groups=mesh['clip'=2,'seq'=4,'blk'=4] {'seq','blk'}, dimensions={0} | all-to-all | bytes 3145728 | tf_op jit(solution)/shard_map/all_to_all | solution.py:390
  45.0 0.0 copy-done
  45.0 0.0 copy-done.1
  45.0 5.7 %attend_head.1 = bf16[16,128,128]{2,1,0:T(8,128)(2,1)S(1)} custom-call(s32[16,16,16]{2,1,0:T(8,128)S(1)} %copy-done, s32[16]{0:T(128)S(1)} %copy-done.1, bf16[16,3,128,128]{3,2,1,0:T(8,128)(2,1)S(1)} %all_to_all.10.refs_2_), custom_call_target="tpu_custom_call" | custom-call | tf_op jit(solution)/shard_map/attend_head/pallas_call | solution.py:394
  50.7 19.3 %all_to_all.11.held_ref = bf16[16,128,128]{2,1,0:T(8,128)(2,1)S(1)} all-to-all(bf16[16,128,128]{2,1,0:T(8,128)(2,1)S(1)} %attend_head.1), channel_id=1, replica_groups=mesh['clip'=2,'seq'=4,'blk'=4] {'seq','blk'}, dimensions={0} | all-to-all | bytes 1048576 | tf_op jit(solution)/shard_map/all_to_all | solution.py:390
  70.0 0.8 %unpack_heads.1 = bf16[128,2048]{1,0:T(8,128)(2,1)} custom-call(bf16[16,128,128]{2,1,0:T(8,128)(2,1)S(1)} %all_to_all.11.held_ref), custom_call_target="tpu_custom_call" | custom-call | tf_op jit(solution)/shard_map/unpack_heads/pallas_call | solution.py:253
Async XLA Ops:
  1.6 43.4 %copy-start = (s32[16,16,16]{2,1,0:T(8,128)S(1)}, s32[16,16,16]{2,1,0:T(8,128)}, u32[]{:S(2)}) copy-start(s32[16,16,16]{2,1,0:T(8,128)} %refs_0_.3) | copy-start | bytes 49156
  1.6 43.4 %copy-start.1 = (s32[16]{0:T(128)S(1)}, s32[16]{0:T(128)}, u32[]{:S(2)}) copy-start(s32[16]{0:T(128)} %refs_1_.3) | copy-start | bytes 196

commit v20 on v13

--- a/solution.py
+++ b/solution.py
@@ -213,7 +213,7 @@
 def pack_heads(*sources):
     count = len(sources)
     rows = sources[0].shape[0]
-    pieces = 4
+    pieces = 8
     return pl.pallas_call(
         pack_kernel,
         out_shape=jax.ShapeDtypeStruct((HEADS, count, rows, HD), jnp.bfloat16),

time: 70.8 us -> 71.2 us (level)
  no operation moved by 1% of the time
where the time goes in v20:
time: 71.2 us; the launch traced here: 70.9 us
  blocking collectives  62.7 us (88%)
  Pallas kernels  8.22 us (12%)
    all_to_all x2, blocking collectives, exchange(): return lax.all_to_all(send, axes, split_axis=0, concat_axis=0, tiled=True)  62.7 us
    pallas_call x1, Pallas kernels, heads_by_device(): pl.pallas_call(lambda *refs: attend_kernel(axes, *refs), out_shape=jax.Sh...  5.77 us
    pallas_call x1, Pallas kernels, pack_heads(): pl.pallas_call(pack_kernel, out_shape=jax.ShapeDtypeStruct((HEADS, count,...  1.61 us

profile of v20, /device:TPU:0, one launch (start us, length us, event | category | flops | bytes accessed | tf_op | source)
XLA Modules:
  0.0 70.9 jit_solution(9085296655777176767)
XLA Ops:
  0.0 1.6 %pack_heads.1 = bf16[16,3,128,128]{3,2,1,0:T(8,128)(2,1)S(1)} custom-call(bf16[128,2048]{1,0:T(8,128)(2,1)} %refs_0_.2, bf16[128,2048]{1,0:T(8,128)(2,1)} %refs_1_.2, bf16[128,2048]{1,0:T(8,128)(2,1)} %refs_2_.1), custom_call_target="tpu_custom_call" | custom-call | tf_op jit(solution)/shard_map/pack_heads/pallas_call | solution.py:217
  1.6 0.0 copy-start
  1.6 0.0 copy-start.1
  1.6 43.4 %all_to_all.10.refs_2_ = bf16[16,3,128,128]{3,2,1,0:T(8,128)(2,1)S(1)} all-to-all(bf16[16,3,128,128]{3,2,1,0:T(8,128)(2,1)S(1)} %pack_heads.1), channel_id=1, replica_groups=mesh['clip'=2,'seq'=4,'blk'=4] {'seq','blk'}, dimensions={0} | all-to-all | bytes 3145728 | tf_op jit(solution)/shard_map/all_to_all | solution.py:390
  45.0 0.0 copy-done
  45.0 0.0 copy-done.1
  45.0 5.8 %attend_head.1 = bf16[16,128,128]{2,1,0:T(8,128)(2,1)S(1)} custom-call(s32[16,16,16]{2,1,0:T(8,128)S(1)} %copy-done, s32[16]{0:T(128)S(1)} %copy-done.1, bf16[16,3,128,128]{3,2,1,0:T(8,128)(2,1)S(1)} %all_to_all.10.refs_2_), custom_call_target="tpu_custom_call" | custom-call | tf_op jit(solution)/shard_map/attend_head/pallas_call | solution.py:394
  50.8 19.3 %all_to_all.11.held_ref = bf16[16,128,128]{2,1,0:T(8,128)(2,1)S(1)} all-to-all(bf16[16,128,128]{2,1,0:T(8,128)(2,1)S(1)} %attend_head.1), channel_id=1, replica_groups=mesh['clip'=2,'seq'=4,'blk'=4] {'seq','blk'}, dimensions={0} | all-to-all | bytes 1048576 | tf_op jit(solution)/shard_map/all_to_all | solution.py:390
  70.1 0.8 %unpack_heads.1 = bf16[128,2048]{1,0:T(8,128)(2,1)} custom-call(bf16[16,128,128]{2,1,0:T(8,128)(2,1)S(1)} %all_to_all.11.held_ref), custom_call_target="tpu_custom_call" | custom-call | tf_op jit(solution)/shard_map/unpack_heads/pallas_call | solution.py:253
Async XLA Ops:
  1.6 43.4 %copy-start = (s32[16,16,16]{2,1,0:T(8,128)S(1)}, s32[16,16,16]{2,1,0:T(8,128)}, u32[]{:S(2)}) copy-start(s32[16,16,16]{2,1,0:T(8,128)} %refs_0_.3) | copy-start | bytes 49156
  1.6 43.4 %copy-start.1 = (s32[16]{0:T(128)S(1)}, s32[16]{0:T(128)}, u32[]{:S(2)}) copy-start(s32[16]{0:T(128)} %refs_1_.3) | copy-start | bytes 196
